TPU v7x, 256 devices: a whole 4x4x8 slice. The times are simulated.
256 devices in a mesh: island: 16 (over z_hi, y), fsdp: 16 (over x, z_lo, core).
Axes of the slice: x: 4, y: 4, z: 8 (z_hi: 4, z_lo: 2; z = z_hi * 2 + z_lo), core: 2. Of those that a mesh axis runs over, the one named last changes fastest.
Arguments:
- tokens: bfloat16 [131072, 8192], P(('island', 'fsdp')), may hold values from -6 to 6
- input_norm_gain: bfloat16 [8192], replicated, may hold values from 0.099609375 to 1.8984375
- key_value_weight: bfloat16 [8192, 1024], P('fsdp'), may hold values from -0.0625 to 0.0625
- adapter_down_factors: bfloat16 [16, 8192, 128], P('island', 'fsdp'), may hold values from -0.0625 to 0.0625
- adapter_up_factors: bfloat16 [16, 2, 64, 512], P('island'), may hold values from -0.75 to 0.75
Outputs:
- keys_values: bfloat16 [131072, 1024], P(('island', 'fsdp'))
All inputs are finite; a program needn't handle non-finite values.
Results may differ from a plain program's by a relative error of at most 0.0058.
Values may be sent and summed in bfloat16 or wider, within the bound.
No kernel may reach another device: no remote copies, remote signals or barrier semaphores. Data moves between devices by JAX's collectives and lax.ppermute only.
A program may use at most 128 MiB of HBM per device.

v0:
```python
import jax
import jax.numpy as jnp
from jax import lax
from jax.sharding import PartitionSpec as P

ADAPTER_RANK = 64


def per_device(tokens, input_norm_gain, key_value_weight, adapter_down_factors, adapter_up_factors):
    values = tokens.astype(jnp.float32)
    meansq = jnp.mean(values * values, axis=-1, keepdims=True)
    normed = (values * lax.rsqrt(meansq + 1e-05) * input_norm_gain.astype(jnp.float32)).astype(
        jnp.bfloat16
    )
    token_row_count = key_value_weight.shape[0]
    width = key_value_weight.shape[1]
    down_factor_parts = adapter_down_factors[0].reshape(token_row_count, 2, ADAPTER_RANK)
    local_term = jnp.einsum(
        "xni,niq->xnq", down_factor_parts, adapter_up_factors[0], preferred_element_type=jnp.float32
    ).reshape(token_row_count, width)
    update = lax.psum(local_term, "island")
    merged = (key_value_weight.astype(jnp.float32) + 0.25 * update).astype(jnp.bfloat16)
    projected = jnp.dot(
        normed,
        lax.all_gather(merged, "fsdp", axis=0, tiled=True),
        preferred_element_type=jnp.float32,
    )
    return projected.astype(jnp.bfloat16)


def solution(mesh):
    placed = (
        P(("island", "fsdp"), None),
        P(),
        P("fsdp", None),
        P("island", "fsdp", None),
        P("island", None, None, None),
    )
    return jax.shard_map(
        per_device,
        mesh=mesh,
        in_specs=placed,
        out_specs=P(("island", "fsdp"), None),
        check_vma=False,
    )
```

profile of v0, /device:TPU:1, one launch (start us, length us, event | category | flops | bytes accessed | tf_op | source)
XLA Modules:
  0.0 312.1 jit_solution(10284440144637394227)
XLA Ops:
  6.5 0.0 copy-start
  6.5 0.0 copy-start.1
  6.5 0.0 copy-start.2
  6.5 0.0 all-reduce.2.cloned.1.call-start
  6.5 1.1 copy.8
  7.7 0.0 copy-done
  7.7 0.5 fusion.10
  8.2 1.8 copy.9
  10.0 0.0 all-reduce.2.cloned.1.call-update
  10.0 0.0 all-gather.2.cloned.1.call-start
  10.1 173.4 %all-reduce.2.cloned.1.call-done = f32[512,1024]{1,0:T(8,128)} async-done(((f32[512,1024]{1,0:T(8,128)}), f32[512,1024]{1,0:T(8,128)}) %all-reduce.2.cloned.1.call-update) | async-done | bytes 2097168 | tf_op jit(solution)/shard_map/psum | solution.py:21
  183.4 0.0 copy-done.1
  183.4 2.9 add_convert_fusion
  186.4 0.0 all-gather.2.cloned.1.call-update
  186.4 0.0 copy-done.2
  186.4 5.1 %fusion = f32[512]{0:T(512)S(1)} fusion(bf16[512,8192]{1,0:T(8,128)(2,1)} %param.5), kind=kLoop, calls=%fused_computation.2 | loop fusion | flops 12582400 | bytes 8390656 | tf_op jit(solution)/shard_map/reduce_sum | solution.py:11
  191.5 98.1 %all-gather.2.cloned.1.call-done = bf16[8192,1024]{1,0:T(8,128)(2,1)} async-done(((bf16[512,1024]{1,0:T(8,128)(2,1)}), bf16[8192,1024]{1,0:T(8,128)(2,1)}) %all-gather.2.cloned.1.call-update) | async-done | bytes 16777232 | tf_op jit(solution)/shard_map/all_gather | solution.py:25
  289.6 15.7 %fusion.7 = bf16[512,1024]{1,0:T(8,128)(2,1)} fusion(bf16[8192,1024]{1,0:T(8,128)(2,1)} %all-gather.2.cloned.1.call-done, bf16[512,8192]{1,0:T(8,128)(2,1)} %param.5, f32[8192]{0:T(1024)S(1)} %convert_element_type.19, f32[512]{0:T(512)S(1)} %add_rsqrt_fusion), kind=kOutput, calls=%fused_computation.9 | convolution fusion | flops 8607236096 | bytes 26249216 | tf_op jit(solution)/shard_map/dot_general | solution.py:23
  (2 shorter events, 0.0 us)
Async XLA Ops:
  6.5 1.1 copy-start
  6.5 176.9 %copy-start.1 = (bf16[512,1024]{1,0:T(8,128)(2,1)S(1)}, bf16[512,1024]{1,0:T(8,128)(2,1)}, u32[]{:S(2)}) copy-start(bf16[512,1024]{1,0:T(8,128)(2,1)} %param.7) | copy-start | bytes 3145732
  6.5 179.8 %copy-start.2 = (bf16[8192]{0:T(1024)(128)(2,1)S(1)}, bf16[8192]{0:T(1024)(128)(2,1)}, u32[]{:S(2)}) copy-start(bf16[8192]{0:T(1024)(128)(2,1)} %param.6) | copy-start | bytes 49156
  6.5 176.9 %all-reduce.2.cloned.1.call-start = ((), (), s32[]{:S(2)}) async-start(), calls=%async_computation | async-start | bytes 4194304 | tf_op jit(solution)/shard_map/psum | solution.py:21
  10.0 279.6 %all-gather.2.cloned.1.call-start = ((), (), s32[]{:S(2)}) async-start(), calls=%async_computation.1 | async-start | bytes 17825792 | tf_op jit(solution)/shard_map/all_gather | solution.py:25
Sparse Core Ops, SparseCore 0:
  10.1 173.2 all-reduce.1
  186.5 103.0 all-gather.1
where the time goes:
time: 312 us
  waiting for transfers between devices  272 us (87%)
  matrix products  16.2 us (5%)
  between operations  13.4 us (4%)
  other arithmetic  8.04 us (3%)
    psum x1, waiting for transfers between devices, per_device(): update = lax.psum(local_term, 'island')  173 us
    all_gather x1, waiting for transfers between devices, per_device(): lax.all_gather(merged, 'fsdp', axis=0, tiled=True)  98.1 us
    dot_general x1, matrix products, per_device(): jnp.dot(normed, lax.all_gather(merged, 'fsdp', axis=0, tiled=True), prefe...  15.7 us
  transfers between devices with their start and end apart: 2, of which 2 were waited for; matrix products, arithmetic and copies ran while one was open for 2% of the time, Pallas kernels for 0%

commit v1 on v0

v1 whole, which is shorter than its diff:
```python
import jax
import jax.numpy as jnp
from jax import lax
from jax.experimental import pallas as pl
from jax.experimental.pallas import tpu as pltpu
from jax.sharding import Mesh, PartitionSpec as P

AXES = ("zh", "y", "x", "zl", "c")
SIZES = (4, 4, 4, 2, 2)
RANK = 64
HALF = 512
EPS = 1e-05
F32 = jnp.float32
BF16 = jnp.bfloat16


def pairs(move):
    out = []
    for src in range(256):
        core, rest = src % 2, src // 2
        zl, rest = rest % 2, rest // 2
        x, rest = rest % 4, rest // 4
        y, zh = rest % 4, rest // 4
        zh2, y2, x2, zl2, core2 = move(zh, y, x, zl, core)
        out.append((src, (((zh2 % 4 * 4 + y2 % 4) * 4 + x2 % 4) * 2 + zl2) * 2 + core2))
    return out


def send(array, move):
    return lax.ppermute(array, AXES, pairs(move))


def to_core(zh, y, x, zl, c):
    return zh, y, x, zl, 1 - c


def to_zl(zh, y, x, zl, c):
    return zh, y, x, 1 - zl, c


def along_y(k):
    return lambda zh, y, x, zl, c: (zh, y + k, x, zl, c)


def along_zh(k):
    return lambda zh, y, x, zl, c: (zh + k, y, x, zl, c)


def first(k):
    return lambda zh, y, x, zl, c: (zh, y + k, x, zl, c) if c == 0 else (zh, y, x + k, zl, c)


def last(k):
    return lambda zh, y, x, zl, c: (zh, y, x + k, zl, c) if c == 0 else (zh, y + k, x, zl, c)


VMEM = pl.BlockSpec(memory_space=pltpu.VMEM)
SMEM = pl.BlockSpec(memory_space=pltpu.SMEM)


def shape(rows, columns, dtype=BF16):
    return jax.ShapeDtypeStruct((rows, columns), dtype)


def call(body, place, operands, outs, scratch=(), cost=1 << 20):
    return pl.pallas_call(
        body,
        out_shape=outs,
        in_specs=[SMEM] + [VMEM] * len(operands),
        out_specs=jax.tree.map(lambda _: VMEM, outs),
        scratch_shapes=list(scratch),
        cost_estimate=pl.CostEstimate(flops=cost, bytes_accessed=cost, transcendentals=0),
    )(place, *operands)


def prepare(place, own, other, up, *rest):
    outs, packed = rest[:4], rest[4]
    y, c = place[1], place[4]
    swapped = pltpu.roll(other[...].astype(F32), RANK, 1)
    lane = lax.broadcasted_iota(jnp.int32, swapped.shape, 1)
    mine = (lane < RANK) == (c == 0)
    packed[...] = jnp.where(mine, own[...].astype(F32), swapped).astype(BF16)
    factor = up[pl.ds(c, 1)][0]
    for k in range(4):
        block = lax.rem(y + k, 4)
        outs[k][0:64, :] = factor
        for j in range(4):
            start = pl.multiple_of(block * 128 + j * 32, 32)
            outs[k][64:96, j * 128 : (j + 1) * 128] = packed[pl.ds(start, 32), :]


def partial_sums(place, *rest):
    parts, outs, total = rest[:4], rest[4:8], rest[8]
    zh = place[0]
    lane = lax.broadcasted_iota(jnp.int32, (128, 128), 1)
    zero = jnp.zeros((128, 128), BF16)
    lefts, rights = [], []
    for part in parts:
        down = jnp.concatenate([part[64:96, j * 128 : (j + 1) * 128] for j in range(4)], axis=0)
        low = jnp.where(lane < RANK, down, zero)
        high = jnp.where(lane < RANK, zero, down)
        lefts.append(jnp.concatenate([low, high], axis=0))
        factor = part[0:64, :]
        rights.append(jnp.concatenate([factor, factor], axis=0))
    value = None
    for k in (0, 2):
        left = jnp.concatenate(lefts[k : k + 2], axis=1)
        right = jnp.concatenate(rights[k : k + 2], axis=0)
        term = jnp.dot(left, right, preferred_element_type=F32)
        value = term if value is None else value + term
    total[...] = value
    for k in range(4):
        start = pl.multiple_of(lax.rem(zh + k, 4) * 32, 32)
        outs[k][0:32, :] = total[pl.ds(start, 32), :]
        outs[k][32:64, :] = total[pl.ds(start + 128, 32), :]


def merge(place, own, other, a, b, c, d, out):
    core = place[4]
    mine, theirs = own[...].astype(F32), other[...].astype(F32)
    update = 0.25 * ((a[...] + b[...]) + (c[...] + d[...]))
    out[0:32, :] = (jnp.where(core == 0, mine, theirs) + update[0:32]).astype(BF16)
    out[32:64, :] = (jnp.where(core == 0, theirs, mine) + update[32:64]).astype(BF16)


def assemble(place, *rest):
    parts, out = rest[:4], rest[4]
    zh = place[0]
    for k in range(4):
        start = pl.multiple_of(lax.rem(zh + 4 - k, 4) * 32, 32)
        out[pl.ds(start, 32), :] = parts[k][0:32, :]
        out[pl.ds(start + 128, 32), :] = parts[k][32:64, :]


def join(place, *rest):
    parts, out = rest[:4], rest[4]
    for k in range(4):
        out[k * 256 : (k + 1) * 256, :] = parts[k][...]


def norm_body(table, tokens, gain, *outs):
    rows = tokens.shape[0]
    squares = jnp.zeros((rows, 128), F32)
    for g in range(64):
        value = tokens[:, g * 128 : (g + 1) * 128].astype(F32)
        squares = squares + value * value
    mean = jnp.sum(squares, axis=1, keepdims=True) / 8192.0
    scale = jnp.broadcast_to(lax.rsqrt(mean + EPS), (rows, 128))
    for g in range(64):
        at = pl.ds(pl.multiple_of(table[g] * 128, 128), 128)
        value = tokens[:, at].astype(F32) * scale * gain[:, at].astype(F32)
        outs[g // 8][:, (g % 8) * 128 : (g % 8 + 1) * 128] = value.astype(BF16)


def normalise(table, tokens, gain):
    rows = 64
    return pl.pallas_call(
        norm_body,
        grid=(512 // rows,),
        out_shape=[shape(512, 1024)] * 8,
        in_specs=[
            SMEM,
            pl.BlockSpec((rows, 8192), lambda i: (i, 0)),
            pl.BlockSpec((1, 8192), lambda i: (0, 0)),
        ],
        out_specs=[pl.BlockSpec((rows, 1024), lambda i: (i, 0))] * 8,
        cost_estimate=pl.CostEstimate(flops=1 << 24, bytes_accessed=1 << 24, transcendentals=0),
    )(table, tokens, gain.reshape(1, 8192))


def feature_order(y, x, zl, c):
    place = jnp.arange(64, dtype=jnp.int32)
    block, part, step, core = place // 16, place // 8 % 2, place // 2 % 4, place % 2
    far = jnp.where(c == 0, x, y)
    near = jnp.where(c == 0, y, x)
    far = (far + 4 - block) % 4
    near = (near + 4 - step) % 4
    row_x = jnp.where(c == 0, far, near)
    row_y = jnp.where(c == 0, near, far)
    return row_x * 16 + (zl ^ part) * 8 + core * 4 + row_y


def per_device(tokens, gain, weight, down, up):
    zh, y, x, zl, c = (lax.axis_index(a) for a in AXES)
    place = jnp.stack([zh, y, x, zl, c]).astype(jnp.int32)
    down, up = down[0], up[0]

    down_other = send(down, to_core)
    row = y * 128 + zh * 32
    weight_own = lax.dynamic_slice(weight, (row, c * HALF), (32, HALF))
    weight_other = send(lax.dynamic_slice(weight, (row, (1 - c) * HALF), (32, HALF)), to_core)

    parts = call(prepare, place, (down, down_other, up), [shape(96, HALF)] * 4, [pltpu.VMEM((512, 128), BF16)])
    parts = [parts[0]] + [send(parts[k], along_y(k)) for k in (1, 3, 2)]
    sums = call(partial_sums, place, parts, [shape(64, HALF, F32)] * 4, [pltpu.VMEM((256, HALF), F32)])
    sums = [sums[0]] + [send(sums[k], along_zh(k)) for k in (1, 3, 2)]
    merged = call(merge, place, (weight_own, weight_other, *sums), shape(64, HALF))
    near = [merged] + [send(merged, along_zh(k)) for k in (1, 2, 3)]
    chunk = call(assemble, place, near, shape(256, HALF))

    tokens_other = send(tokens, to_core)
    table = feature_order(y, x, zl, c)
    normed = normalise(table, tokens, gain)
    normed_other = normalise(table, tokens_other, gain)

    blocks = {}
    for part, piece in ((0, chunk), (1, send(chunk, to_zl))):
        pieces = [piece] + [send(piece, first(k)) for k in (1, 2, 3)]
        blocks[0, part] = call(join, place, pieces, shape(1024, HALF))
    for part in (0, 1):
        blocks[1, part] = send(blocks[0, part], last(1))
        blocks[3, part] = send(blocks[0, part], last(-1))
    blocks[2, 0] = send(blocks[1, 0], last(1))
    blocks[2, 1] = send(blocks[3, 1], last(-1))

    mine = theirs = None
    for block in (0, 1, 3, 2):
        for part in (0, 1):
            rows = blocks[block, part]
            term = jnp.dot(normed_other[block * 2 + part], rows, preferred_element_type=F32)
            theirs = term if theirs is None else theirs + term
            term = jnp.dot(normed[block * 2 + part], rows, preferred_element_type=F32)
            mine = term if mine is None else mine + term
    back = send(theirs.astype(BF16), to_core)
    mine = mine.astype(BF16)
    left = jnp.where(c == 0, mine, back)
    right = jnp.where(c == 0, back, mine)
    return jnp.concatenate([left, right], axis=1)


def solution(mesh):
    fine = Mesh(mesh.devices.reshape(SIZES), AXES)
    rows = ("x", "zl", "c")
    placed = (
        P(AXES, None),
        P(),
        P(rows, None),
        P(("zh", "y"), rows, None),
        P(("zh", "y"), None, None, None),
    )
    return jax.shard_map(per_device, mesh=fine, in_specs=placed, out_specs=P(AXES, None), check_vma=False)
```

time: 312 us -> 161 us (0.52)
  waiting for transfers between devices: 272 us -> 40.1 us
  starting transfers between devices: 0.04 us -> 46.3 us
  Pallas kernels: 0 us -> 31.9 us
  matrix products: 16.2 us -> 30.2 us
  between operations: 13.4 us -> 0.4 us
  local copies, waits for them, and re-layouts: 2.94 us -> 10.8 us
  other arithmetic: 8.04 us -> 0.68 us
    psum x1 -> x0, waiting for transfers between devices: 173 us -> none  [per_device(): update = lax.psum(local_term, 'island')]
    all_gather x1 -> x0, waiting for transfers between devices: 98.1 us -> none  [per_device(): lax.all_gather(merged, 'fsdp', axis=0, tiled=True)]
    ppermute x0 -> x26, starting transfers between devices: none -> 46.3 us  [send(): return lax.ppermute(array, AXES, pairs(move))]
    ppermute x0 -> x26, waiting for transfers between devices: none -> 40.1 us  [send(): return lax.ppermute(array, AXES, pairs(move))]
    pallas_call x0 -> x8, Pallas kernels: none -> 31.9 us  [the longest x2 19.8 us: normalise(): pl.pallas_call(norm_body, grid=(512 // rows,), out_shape=[shape(512, 1024...]
    dot_general x2 -> x16, matrix products: 16.2 us -> 30.2 us  [the longest x8 17.5 us: per_device(): term = jnp.dot(normed[block * 2 + part], rows, preferred_element_type=F32)]
    unnamed x7 -> x84, local copies, waits for them, and re-layouts: 1.11 us -> 6.9 us
    reduce_sum x1 -> x0, other arithmetic: 5.1 us -> none  [per_device(): meansq = jnp.mean(values * values, axis=-1, keepdims=True)]
  transfers between devices with their start and end apart: 2 -> 26, of which waited for: 2 -> 12; matrix products, arithmetic and copies ran while one was open for 2% -> 20% of each run, Pallas kernels for 0% -> 20%
where the time goes in v1:
time: 161 us; the launch traced here: 160 us
  starting transfers between devices  46.3 us (29%)
  waiting for transfers between devices  40.1 us (25%)
  Pallas kernels  31.9 us (20%)
  matrix products  30.2 us (19%)
  local copies, waits for them, and re-layouts  10.8 us (7%)
    ppermute x26, starting transfers between devices, send(): return lax.ppermute(array, AXES, pairs(move))  46.3 us
    ppermute x26, waiting for transfers between devices, send(): return lax.ppermute(array, AXES, pairs(move))  40.1 us
    pallas_call x2, Pallas kernels, normalise(): pl.pallas_call(norm_body, grid=(512 // rows,), out_shape=[shape(512, 1024...  19.8 us
    dot_general x8, matrix products, per_device(): term = jnp.dot(normed[block * 2 + part], rows, preferred_element_type=F32)  17.5 us
    dot_general x8, matrix products, per_device(): jnp.dot(normed_other[block * 2 + part], rows, preferred_element_type=F32)  12.7 us
    pallas_call x6, Pallas kernels, call(): pl.pallas_call(body, out_shape=outs, in_specs=[SMEM] + [VMEM] * len(opera...  12.1 us
    unnamed x84, local copies, waits for them, and re-layouts  6.9 us
  transfers between devices with their start and end apart: 26, of which 12 were waited for; matrix products, arithmetic and copies ran while one was open for 20% of the time, Pallas kernels for 20%

profile of v1, /device:TPU:1, one launch (start us, length us, event | category | flops | bytes accessed | tf_op | source)
XLA Modules:
  0.0 160.3 jit_solution(9003143655712593708)
XLA Ops:
  0.0 3.2 %collective-permute-start.24 = (bf16[512,8192]{1,0:T(8,128)(2,1)}, bf16[512,8192]{1,0:T(8,128)(2,1)}, u32[]{:S(2)}, u32[]{:S(2)}) collective-permute-start(bf16[512,8192]{1,0:T(8,128)(2,1)} %tokens.1), channel_id=1, source_target_pairs={{0,1},{1,0},{2,3},{3,2},{4,5},{5,4},{6,7},{7,6},{8,9},{9,8},{10,11... | collective-permute-start | bytes 25165832 | tf_op jit(solution)/shard_map/ppermute | solution.py:30
  3.9 5.7 %collective-permute-done.1.other = bf16[512,128]{1,0:T(8,128)(2,1)S(1)} collective-permute-done((bf16[512,128]{1,0:T(8,128)(2,1)}, bf16[512,128]{1,0:T(8,128)(2,1)S(1)}, u32[]{:S(2)}, u32[]{:S(2)}) %collective-permute-start.1) | collective-permute-done | bytes 131104 | tf_op jit(solution)/shard_map/ppermute | solution.py:30
  12.1 2.7 %collective-permute-start.3 = (bf16[96,512]{1,0:T(8,128)(2,1)}, bf16[96,512]{1,0:T(8,128)(2,1)S(1)}, u32[]{:S(2)}, u32[]{:S(2)}) collective-permute-start(bf16[96,512]{1,0:T(8,128)(2,1)} %get-tuple-element.32), channel_id=1, source_target_pairs={{0,48},{1,49},{2,50},{3,51},{4,52},{5,53},{6,54},{7,55},{8,56},{9,... | collective-permute-start | bytes 294920 | tf_op jit(solution)/shard_map/ppermute | solution.py:30
  14.8 3.0 %collective-permute-done.2.rest_1_ = bf16[96,512]{1,0:T(8,128)(2,1)S(1)} collective-permute-done((bf16[96,512]{1,0:T(8,128)(2,1)}, bf16[96,512]{1,0:T(8,128)(2,1)S(1)}, u32[]{:S(2)}, u32[]{:S(2)}) %collective-permute-start.2) | collective-permute-done | bytes 98336 | tf_op jit(solution)/shard_map/ppermute | solution.py:30
  20.6 2.2 %shard_map.57 = (f32[64,512]{1,0:T(8,128)}, f32[64,512]{1,0:T(8,128)}, f32[64,512]{1,0:T(8,128)}, f32[64,512]{1,0:T(8,128)}) custom-call(s32[5]{0:T(128)} %stack.23.place, bf16[96,512]{1,0:T(8,128)(2,1)} %get-tuple-element.30.rest_0_, bf16[96,512]{1,0:T(8,128)(2,1)} %copy-done.22, bf16[96,512]{1,0:T(8,128)(2,1)} %copy-done.23, bf16[96,512]{1,0:T(8,128)(2,1)} %copy-done.24), custom_call_target="tpu_custom_call" | custom-call | flops 1048576 | bytes 1048576 | tf_op jit(solution)/shard_map/pallas_call | solution.py:66
  22.8 2.2 %collective-permute-start.5 = (f32[64,512]{1,0:T(8,128)}, f32[64,512]{1,0:T(8,128)S(1)}, u32[]{:S(2)}, u32[]{:S(2)}) collective-permute-start(f32[64,512]{1,0:T(8,128)} %get-tuple-element.35), channel_id=1, source_target_pairs={{0,64},{1,65},{2,66},{3,67},{4,68},{5,69},{6,70},{7,71},{8,72},{9,... | collective-permute-start | bytes 393224 | tf_op jit(solution)/shard_map/ppermute | solution.py:30
  25.0 3.1 %collective-permute-start.6 = (f32[64,512]{1,0:T(8,128)}, f32[64,512]{1,0:T(8,128)S(1)}, u32[]{:S(2)}, u32[]{:S(2)}) collective-permute-start(f32[64,512]{1,0:T(8,128)} %get-tuple-element.36), channel_id=1, source_target_pairs={{0,192},{1,193},{2,194},{3,195},{4,196},{5,197},{6,198},{7,199},{8... | collective-permute-start | bytes 393224 | tf_op jit(solution)/shard_map/ppermute | solution.py:30
  28.0 4.4 %collective-permute-start.7 = (f32[64,512]{1,0:T(8,128)}, f32[64,512]{1,0:T(8,128)S(1)}, u32[]{:S(2)}, u32[]{:S(2)}) collective-permute-start(f32[64,512]{1,0:T(8,128)} %get-tuple-element.37), channel_id=1, source_target_pairs={{0,128},{1,129},{2,130},{3,131},{4,132},{5,133},{6,134},{7,135},{8... | collective-permute-start | bytes 393224 | tf_op jit(solution)/shard_map/ppermute | solution.py:30
  33.9 2.0 %collective-permute-start = (bf16[32,512]{1,0:T(8,128)(2,1)S(1)}, bf16[32,512]{1,0:T(8,128)(2,1)S(1)}, u32[]{:S(2)}, u32[]{:S(2)}) collective-permute-start(bf16[32,512]{1,0:T(8,128)(2,1)S(1)} %get-tuple-element.55), channel_id=1, source_target_pairs={{0,1},{1,0},{2,3},{3,2},{4,5},{5,4},{6,7},{7,6},{8,9},{9,8},{10,11... | collective-permute-start | bytes 98312 | tf_op jit(solution)/shard_map/ppermute | solution.py:30
  37.7 2.9 %collective-permute-done.7.d = f32[64,512]{1,0:T(8,128)S(1)} collective-permute-done((f32[64,512]{1,0:T(8,128)}, f32[64,512]{1,0:T(8,128)S(1)}, u32[]{:S(2)}, u32[]{:S(2)}) %collective-permute-start.7) | collective-permute-done | bytes 131104 | tf_op jit(solution)/shard_map/ppermute | solution.py:30
  43.1 3.6 %collective-permute-start.9 = (bf16[64,512]{1,0:T(8,128)(2,1)}, bf16[64,512]{1,0:T(8,128)(2,1)S(1)}, u32[]{:S(2)}, u32[]{:S(2)}) collective-permute-start(bf16[64,512]{1,0:T(8,128)(2,1)} %shard_map.58.rest_0_), channel_id=1, source_target_pairs={{0,128},{1,129},{2,130},{3,131},{4,132},{5,133},{6,134},{7,135},{8... | collective-permute-start | bytes 196616 | tf_op jit(solution)/shard_map/ppermute | solution.py:30
  46.7 2.8 %collective-permute-start.10 = (bf16[64,512]{1,0:T(8,128)(2,1)}, bf16[64,512]{1,0:T(8,128)(2,1)S(1)}, u32[]{:S(2)}, u32[]{:S(2)}) collective-permute-start(bf16[64,512]{1,0:T(8,128)(2,1)} %shard_map.58.rest_0_), channel_id=1, source_target_pairs={{0,192},{1,193},{2,194},{3,195},{4,196},{5,197},{6,198},{7,199},{8... | collective-permute-start | bytes 196616 | tf_op jit(solution)/shard_map/ppermute | solution.py:30
  56.0 2.4 %collective-permute-start.12 = (bf16[256,512]{1,0:T(8,128)(2,1)}, bf16[256,512]{1,0:T(8,128)(2,1)S(1)}, u32[]{:S(2)}, u32[]{:S(2)}) collective-permute-start(bf16[256,512]{1,0:T(8,128)(2,1)} %shard_map.59.rest_0_), channel_id=1, source_target_pairs={{0,32},{1,9},{2,34},{3,11},{4,36},{5,13},{6,38},{7,15},{8,40},{9,1... | collective-permute-start | bytes 786440 | tf_op jit(solution)/shard_map/ppermute | solution.py:30
  59.6 6.6 %collective-permute-start.14 = (bf16[256,512]{1,0:T(8,128)(2,1)}, bf16[256,512]{1,0:T(8,128)(2,1)S(1)}, u32[]{:S(2)}, u32[]{:S(2)}) collective-permute-start(bf16[256,512]{1,0:T(8,128)(2,1)} %shard_map.59.rest_0_), channel_id=1, source_target_pairs={{0,2},{1,3},{2,0},{3,1},{4,6},{5,7},{6,4},{7,5},{8,10},{9,11},{10,... | collective-permute-start | bytes 786440 | tf_op jit(solution)/shard_map/ppermute | solution.py:30
  67.7 2.3 %shard_map.60 = bf16[1024,512]{1,0:T(8,128)(2,1)} custom-call(s32[5]{0:T(128)} %stack.23.place, bf16[256,512]{1,0:T(8,128)(2,1)} %shard_map.59.rest_0_, bf16[256,512]{1,0:T(8,128)(2,1)} %copy-done.13, bf16[256,512]{1,0:T(8,128)(2,1)} %copy-done.14, bf16[256,512]{1,0:T(8,128)(2,1)} %copy-done.16), custom_call_target="tpu_custom_call" | custom-call | flops 1048576 | bytes 1048576 | tf_op jit(solution)/shard_map/pallas_call | solution.py:66
  70.6 2.3 %collective-permute-done.14.rest_0_ = bf16[256,512]{1,0:T(8,128)(2,1)S(1)} collective-permute-done((bf16[256,512]{1,0:T(8,128)(2,1)}, bf16[256,512]{1,0:T(8,128)(2,1)S(1)}, u32[]{:S(2)}, u32[]{:S(2)}) %collective-permute-start.14) | collective-permute-done | bytes 262176 | tf_op jit(solution)/shard_map/ppermute | solution.py:30
  74.1 10.7 %collective-permute-done.15.rest_1_ = bf16[256,512]{1,0:T(8,128)(2,1)S(1)} collective-permute-done((bf16[256,512]{1,0:T(8,128)(2,1)S(1)}, bf16[256,512]{1,0:T(8,128)(2,1)S(1)}, u32[]{:S(2)}, u32[]{:S(2)}) %collective-permute-start.15) | collective-permute-done | bytes 262176 | tf_op jit(solution)/shard_map/ppermute | solution.py:30
  84.8 8.5 %collective-permute-done.17.rest_3_ = bf16[256,512]{1,0:T(8,128)(2,1)S(1)} collective-permute-done((bf16[256,512]{1,0:T(8,128)(2,1)S(1)}, bf16[256,512]{1,0:T(8,128)(2,1)S(1)}, u32[]{:S(2)}, u32[]{:S(2)}) %collective-permute-start.17) | collective-permute-done | bytes 262176 | tf_op jit(solution)/shard_map/ppermute | solution.py:30
  94.0 2.2 %shard_map.61 = bf16[1024,512]{1,0:T(8,128)(2,1)} custom-call(s32[5]{0:T(128)} %stack.23.place, bf16[256,512]{1,0:T(8,128)(2,1)} %copy-done.11, bf16[256,512]{1,0:T(8,128)(2,1)} %copy-done.12, bf16[256,512]{1,0:T(8,128)(2,1)} %copy-done.15, bf16[256,512]{1,0:T(8,128)(2,1)} %copy-done.17), custom_call_target="tpu_custom_call" | custom-call | flops 1048576 | bytes 1048576 | tf_op jit(solution)/shard_map/pallas_call | solution.py:66
  97.4 10.0 %shard_map.55 = (bf16[512,1024]{1,0:T(8,128)(2,1)}, bf16[512,1024]{1,0:T(8,128)(2,1)}, bf16[512,1024]{1,0:T(8,128)(2,1)}, bf16[512,1024]{1,0:T(8,128)(2,1)}, bf1...) custom-call(s32[64]{0:T(128)} %fusion.14.table, ...), custom_call_target="tpu_custom_call" | custom-call | flops 16777216 | bytes 16777216 | tf_op jit(solution)/shard_map/pallas_call | solution.py:157
  109.0 3.0 %fusion.27 = f32[512,512]{0,1:T(8,128)} fusion(bf16[512,1024]{1,0:T(8,128)(2,1)} %get-tuple-element.29, bf16[1024,512]{1,0:T(8,128)(2,1)S(1)} %copy-done.1), kind=kOutput, calls=%fused_computation.59 | convolution fusion | flops 536870912 | bytes 3145728 | tf_op jit(solution)/shard_map/dot_general | solution.py:222
  112.6 3.0 %fusion.28 = f32[512,512]{0,1:T(8,128)} fusion(bf16[512,1024]{1,0:T(8,128)(2,1)S(1)} %copy-done.37, bf16[1024,512]{1,0:T(8,128)(2,1)} %collective-permute-done.18), kind=kOutput, calls=%fused_computation.60 | convolution fusion | flops 536870912 | bytes 3145728 | tf_op jit(solution)/shard_map/dot_general | solution.py:222
  115.6 3.1 %fusion.30 = f32[512,512]{0,1:T(8,128)} fusion(bf16[512,1024]{1,0:T(8,128)(2,1)S(1)} %copy-done.35, bf16[1024,512]{1,0:T(8,128)(2,1)} %collective-permute-done.20), kind=kOutput, calls=%fused_computation.62 | convolution fusion | flops 536870912 | bytes 3145728 | tf_op jit(solution)/shard_map/dot_general | solution.py:222
  118.7 2.0 %collective-permute-start.23 = (bf16[1024,512]{1,0:T(8,128)(2,1)}, bf16[1024,512]{1,0:T(8,128)(2,1)}, u32[]{:S(2)}, u32[]{:S(2)}) collective-permute-start(bf16[1024,512]{1,0:T(8,128)(2,1)} %collective-permute-done.21), channel_id=1, source_target_pairs={{0,12},{1,49},{2,14},{3,51},{4,0},{5,53},{6,2},{7,55},{8,4},{9,57}... | collective-permute-start | bytes 3145736 | tf_op jit(solution)/shard_map/ppermute | solution.py:30
  120.7 3.0 %fusion.31 = f32[512,512]{0,1:T(8,128)} fusion(bf16[512,1024]{1,0:T(8,128)(2,1)S(1)} %copy-done.34, bf16[1024,512]{1,0:T(8,128)(2,1)} %collective-permute-done.21), kind=kOutput, calls=%fused_computation.63 | convolution fusion | flops 536870912 | bytes 3145728 | tf_op jit(solution)/shard_map/dot_general | solution.py:222
  126.4 9.8 %shard_map.62 = (bf16[512,1024]{1,0:T(8,128)(2,1)}, bf16[512,1024]{1,0:T(8,128)(2,1)}, bf16[512,1024]{1,0:T(8,128)(2,1)}, bf16[512,1024]{1,0:T(8,128)(2,1)}, bf1...) custom-call(s32[64]{0:T(128)} %fusion.14.table, ...), custom_call_target="tpu_custom_call" | custom-call | flops 16777216 | bytes 16777216 | tf_op jit(solution)/shard_map/pallas_call | solution.py:157
  136.3 2.1 %fusion.33 = f32[512,512]{0,1:T(8,128)S(1)} fusion(bf16[512,1024]{1,0:T(8,128)(2,1)} %get-tuple-element.45, bf16[1024,512]{1,0:T(8,128)(2,1)S(1)} %copy-done.1), kind=kOutput, calls=%fused_computation.65 | convolution fusion | flops 536870912 | bytes 3145728 | tf_op jit(solution)/shard_map/dot_general | solution.py:220
  138.4 2.1 %fusion.37 = f32[512,512]{0,1:T(8,128)S(1)} fusion(bf16[512,1024]{1,0:T(8,128)(2,1)S(1)} %copy-done.41, bf16[1024,512]{1,0:T(8,128)(2,1)} %collective-permute-done.21), kind=kOutput, calls=%fused_computation.69 | convolution fusion | flops 536870912 | bytes 3145728 | tf_op jit(solution)/shard_map/dot_general | solution.py:220
  140.5 2.1 %fusion.36 = f32[512,512]{0,1:T(8,128)S(1)} fusion(bf16[512,1024]{1,0:T(8,128)(2,1)S(1)} %copy-done.40, bf16[1024,512]{1,0:T(8,128)(2,1)} %collective-permute-done.20), kind=kOutput, calls=%fused_computation.68 | convolution fusion | flops 536870912 | bytes 3145728 | tf_op jit(solution)/shard_map/dot_general | solution.py:220
  143.8 2.0 %fusion.34 = f32[512,512]{0,1:T(8,128)S(1)} fusion(bf16[512,1024]{1,0:T(8,128)(2,1)S(1)} %copy-done.38, bf16[1024,512]{1,0:T(8,128)(2,1)} %collective-permute-done.18), kind=kOutput, calls=%fused_computation.66 | convolution fusion | flops 536870912 | bytes 3145728 | tf_op jit(solution)/shard_map/dot_general | solution.py:220
  145.9 2.1 %fusion.38 = f32[512,512]{0,1:T(8,128)S(1)} fusion(bf16[512,1024]{1,0:T(8,128)(2,1)S(1)} %copy-done.36, bf16[1024,512]{1,0:T(8,128)(2,1)} %collective-permute-done.23), kind=kOutput, calls=%fused_computation.70 | convolution fusion | flops 536870912 | bytes 3145728 | tf_op jit(solution)/shard_map/dot_general | solution.py:220
  150.0 4.8 %collective-permute-start.25 = (bf16[512,512]{0,1:T(8,128)(2,1)S(1)}, bf16[512,512]{0,1:T(8,128)(2,1)S(1)}, u32[]{:S(2)}, u32[]{:S(2)}) collective-permute-start(bf16[512,512]{0,1:T(8,128)(2,1)S(1)} %fusion.11), channel_id=1, source_target_pairs={{0,1},{1,0},{2,3},{3,2},{4,5},{5,4},{6,7},{7,6},{8,9},{9,8},{10,11... | collective-permute-start | bytes 1572872 | tf_op jit(solution)/shard_map/ppermute | solution.py:30
  (134 shorter events, 38.0 us)
Async XLA Ops:
  0.0 126.4 %collective-permute-start.24 = (bf16[512,8192]{1,0:T(8,128)(2,1)}, bf16[512,8192]{1,0:T(8,128)(2,1)}, u32[]{:S(2)}, u32[]{:S(2)}) collective-permute-start(bf16[512,8192]{1,0:T(8,128)(2,1)} %tokens.1), channel_id=1, source_target_pairs={{0,1},{1,0},{2,3},{3,2},{4,5},{5,4},{6,7},{7,6},{8,9},{9,8},{10,11... | collective-permute-start | bytes 25165832 | tf_op jit(solution)/shard_map/ppermute | solution.py:30
  3.2 6.3 %collective-permute-start.1 = (bf16[512,128]{1,0:T(8,128)(2,1)}, bf16[512,128]{1,0:T(8,128)(2,1)S(1)}, u32[]{:S(2)}, u32[]{:S(2)}) collective-permute-start(bf16[512,128]{1,0:T(8,128)(2,1)} %bitcast.39), channel_id=1, source_target_pairs={{0,1},{1,0},{2,3},{3,2},{4,5},{5,4},{6,7},{7,6},{8,9},{9,8},{10,11... | collective-permute-start | bytes 393224 | tf_op jit(solution)/shard_map/ppermute | solution.py:30
  12.1 5.7 %collective-permute-start.2 = (bf16[96,512]{1,0:T(8,128)(2,1)}, bf16[96,512]{1,0:T(8,128)(2,1)S(1)}, u32[]{:S(2)}, u32[]{:S(2)}) collective-permute-start(bf16[96,512]{1,0:T(8,128)(2,1)} %get-tuple-element.31), channel_id=1, source_target_pairs={{0,16},{1,17},{2,18},{3,19},{4,20},{5,21},{6,22},{7,23},{8,24},{9,... | collective-permute-start | bytes 294920 | tf_op jit(solution)/shard_map/ppermute | solution.py:30
  12.1 7.0 %collective-permute-start.3 = (bf16[96,512]{1,0:T(8,128)(2,1)}, bf16[96,512]{1,0:T(8,128)(2,1)S(1)}, u32[]{:S(2)}, u32[]{:S(2)}) collective-permute-start(bf16[96,512]{1,0:T(8,128)(2,1)} %get-tuple-element.32), channel_id=1, source_target_pairs={{0,48},{1,49},{2,50},{3,51},{4,52},{5,53},{6,54},{7,55},{8,56},{9,... | collective-permute-start | bytes 294920 | tf_op jit(solution)/shard_map/ppermute | solution.py:30
  14.8 5.2 %collective-permute-start.4 = (bf16[96,512]{1,0:T(8,128)(2,1)}, bf16[96,512]{1,0:T(8,128)(2,1)S(1)}, u32[]{:S(2)}, u32[]{:S(2)}) collective-permute-start(bf16[96,512]{1,0:T(8,128)(2,1)} %get-tuple-element.33), channel_id=1, source_target_pairs={{0,32},{1,33},{2,34},{3,35},{4,36},{5,37},{6,38},{7,39},{8,40},{9,... | collective-permute-start | bytes 294920 | tf_op jit(solution)/shard_map/ppermute | solution.py:30
  22.8 14.0 %collective-permute-start.5 = (f32[64,512]{1,0:T(8,128)}, f32[64,512]{1,0:T(8,128)S(1)}, u32[]{:S(2)}, u32[]{:S(2)}) collective-permute-start(f32[64,512]{1,0:T(8,128)} %get-tuple-element.35), channel_id=1, source_target_pairs={{0,64},{1,65},{2,66},{3,67},{4,68},{5,69},{6,70},{7,71},{8,72},{9,... | collective-permute-start | bytes 393224 | tf_op jit(solution)/shard_map/ppermute | solution.py:30
  25.0 12.7 %collective-permute-start.6 = (f32[64,512]{1,0:T(8,128)}, f32[64,512]{1,0:T(8,128)S(1)}, u32[]{:S(2)}, u32[]{:S(2)}) collective-permute-start(f32[64,512]{1,0:T(8,128)} %get-tuple-element.36), channel_id=1, source_target_pairs={{0,192},{1,193},{2,194},{3,195},{4,196},{5,197},{6,198},{7,199},{8... | collective-permute-start | bytes 393224 | tf_op jit(solution)/shard_map/ppermute | solution.py:30
  28.0 12.6 %collective-permute-start.7 = (f32[64,512]{1,0:T(8,128)}, f32[64,512]{1,0:T(8,128)S(1)}, u32[]{:S(2)}, u32[]{:S(2)}) collective-permute-start(f32[64,512]{1,0:T(8,128)} %get-tuple-element.37), channel_id=1, source_target_pairs={{0,128},{1,129},{2,130},{3,131},{4,132},{5,133},{6,134},{7,135},{8... | collective-permute-start | bytes 393224 | tf_op jit(solution)/shard_map/ppermute | solution.py:30
  33.9 2.9 %collective-permute-start = (bf16[32,512]{1,0:T(8,128)(2,1)S(1)}, bf16[32,512]{1,0:T(8,128)(2,1)S(1)}, u32[]{:S(2)}, u32[]{:S(2)}) collective-permute-start(bf16[32,512]{1,0:T(8,128)(2,1)S(1)} %get-tuple-element.55), channel_id=1, source_target_pairs={{0,1},{1,0},{2,3},{3,2},{4,5},{5,4},{6,7},{7,6},{8,9},{9,8},{10,11... | collective-permute-start | bytes 98312 | tf_op jit(solution)/shard_map/ppermute | solution.py:30
  43.1 6.4 %collective-permute-start.8 = (bf16[64,512]{1,0:T(8,128)(2,1)}, bf16[64,512]{1,0:T(8,128)(2,1)S(1)}, u32[]{:S(2)}, u32[]{:S(2)}) collective-permute-start(bf16[64,512]{1,0:T(8,128)(2,1)} %shard_map.58.rest_0_), channel_id=1, source_target_pairs={{0,64},{1,65},{2,66},{3,67},{4,68},{5,69},{6,70},{7,71},{8,72},{9,... | collective-permute-start | bytes 196616 | tf_op jit(solution)/shard_map/ppermute | solution.py:30
  43.1 7.5 %collective-permute-start.9 = (bf16[64,512]{1,0:T(8,128)(2,1)}, bf16[64,512]{1,0:T(8,128)(2,1)S(1)}, u32[]{:S(2)}, u32[]{:S(2)}) collective-permute-start(bf16[64,512]{1,0:T(8,128)(2,1)} %shard_map.58.rest_0_), channel_id=1, source_target_pairs={{0,128},{1,129},{2,130},{3,131},{4,132},{5,133},{6,134},{7,135},{8... | collective-permute-start | bytes 196616 | tf_op jit(solution)/shard_map/ppermute | solution.py:30
  46.7 5.7 %collective-permute-start.10 = (bf16[64,512]{1,0:T(8,128)(2,1)}, bf16[64,512]{1,0:T(8,128)(2,1)S(1)}, u32[]{:S(2)}, u32[]{:S(2)}) collective-permute-start(bf16[64,512]{1,0:T(8,128)(2,1)} %shard_map.58.rest_0_), channel_id=1, source_target_pairs={{0,192},{1,193},{2,194},{3,195},{4,196},{5,197},{6,198},{7,199},{8... | collective-permute-start | bytes 196616 | tf_op jit(solution)/shard_map/ppermute | solution.py:30
  54.8 41.4 %copy-start.29 = (bf16[8192]{0:T(1024)(128)(2,1)S(1)}, bf16[8192]{0:T(1024)(128)(2,1)}, u32[]{:S(2)}) copy-start(bf16[8192]{0:T(1024)(128)(2,1)} %param.6) | copy-start | bytes 49156
  54.8 11.5 %collective-permute-start.11 = (bf16[256,512]{1,0:T(8,128)(2,1)}, bf16[256,512]{1,0:T(8,128)(2,1)S(1)}, u32[]{:S(2)}, u32[]{:S(2)}) collective-permute-start(bf16[256,512]{1,0:T(8,128)(2,1)} %shard_map.59.rest_0_), channel_id=1, source_target_pairs={{0,16},{1,5},{2,18},{3,7},{4,20},{5,9},{6,22},{7,11},{8,24},{9,13}... | collective-permute-start | bytes 786440 | tf_op jit(solution)/shard_map/ppermute | solution.py:30
  56.0 10.3 %collective-permute-start.12 = (bf16[256,512]{1,0:T(8,128)(2,1)}, bf16[256,512]{1,0:T(8,128)(2,1)S(1)}, u32[]{:S(2)}, u32[]{:S(2)}) collective-permute-start(bf16[256,512]{1,0:T(8,128)(2,1)} %shard_map.59.rest_0_), channel_id=1, source_target_pairs={{0,32},{1,9},{2,34},{3,11},{4,36},{5,13},{6,38},{7,15},{8,40},{9,1... | collective-permute-start | bytes 786440 | tf_op jit(solution)/shard_map/ppermute | solution.py:30
  58.4 7.8 %collective-permute-start.13 = (bf16[256,512]{1,0:T(8,128)(2,1)}, bf16[256,512]{1,0:T(8,128)(2,1)S(1)}, u32[]{:S(2)}, u32[]{:S(2)}) collective-permute-start(bf16[256,512]{1,0:T(8,128)(2,1)} %shard_map.59.rest_0_), channel_id=1, source_target_pairs={{0,48},{1,13},{2,50},{3,15},{4,52},{5,1},{6,54},{7,3},{8,56},{9,5}... | collective-permute-start | bytes 786440 | tf_op jit(solution)/shard_map/ppermute | solution.py:30
  59.6 13.3 %collective-permute-start.14 = (bf16[256,512]{1,0:T(8,128)(2,1)}, bf16[256,512]{1,0:T(8,128)(2,1)S(1)}, u32[]{:S(2)}, u32[]{:S(2)}) collective-permute-start(bf16[256,512]{1,0:T(8,128)(2,1)} %shard_map.59.rest_0_), channel_id=1, source_target_pairs={{0,2},{1,3},{2,0},{3,1},{4,6},{5,7},{6,4},{7,5},{8,10},{9,11},{10,... | collective-permute-start | bytes 786440 | tf_op jit(solution)/shard_map/ppermute | solution.py:30
  70.0 41.9 %collective-permute-start.18 = (bf16[1024,512]{1,0:T(8,128)(2,1)}, bf16[1024,512]{1,0:T(8,128)(2,1)}, u32[]{:S(2)}, u32[]{:S(2)}) collective-permute-start(bf16[1024,512]{1,0:T(8,128)(2,1)} %shard_map.60), channel_id=1, source_target_pairs={{0,4},{1,17},{2,6},{3,19},{4,8},{5,21},{6,10},{7,23},{8,12},{9,25}... | collective-permute-start | bytes 3145736 | tf_op jit(solution)/shard_map/ppermute | solution.py:30
  72.9 20.3 %copy-start.11 = (bf16[256,512]{1,0:T(8,128)(2,1)}, bf16[256,512]{1,0:T(8,128)(2,1)S(1)}, u32[]{:S(2)}) copy-start(bf16[256,512]{1,0:T(8,128)(2,1)S(1)} %collective-permute-done.14.rest_0_) | copy-start | bytes 786436
  72.9 11.8 %collective-permute-start.15 = (bf16[256,512]{1,0:T(8,128)(2,1)S(1)}, bf16[256,512]{1,0:T(8,128)(2,1)S(1)}, u32[]{:S(2)}, u32[]{:S(2)}) collective-permute-start(bf16[256,512]{1,0:T(8,128)(2,1)S(1)} %collective-permute-done.14.rest_0_), channel_id=1, source_target_pairs={{0,16},{1,5},{2,18},{3,7},{4,20},{5,9},{6,22},{7,11},{8,24},{9,13}... | collective-permute-start | bytes 786440 | tf_op jit(solution)/shard_map/ppermute | solution.py:30
  72.9 42.7 %collective-permute-start.20 = (bf16[1024,512]{1,0:T(8,128)(2,1)}, bf16[1024,512]{1,0:T(8,128)(2,1)}, u32[]{:S(2)}, u32[]{:S(2)}) collective-permute-start(bf16[1024,512]{1,0:T(8,128)(2,1)} %shard_map.60), channel_id=1, source_target_pairs={{0,12},{1,49},{2,14},{3,51},{4,0},{5,53},{6,2},{7,55},{8,4},{9,57}... | collective-permute-start | bytes 3145736 | tf_op jit(solution)/shard_map/ppermute | solution.py:30
  73.0 11.7 %collective-permute-start.16 = (bf16[256,512]{1,0:T(8,128)(2,1)S(1)}, bf16[256,512]{1,0:T(8,128)(2,1)S(1)}, u32[]{:S(2)}, u32[]{:S(2)}) collective-permute-start(bf16[256,512]{1,0:T(8,128)(2,1)S(1)} %collective-permute-done.14.rest_0_), channel_id=1, source_target_pairs={{0,32},{1,9},{2,34},{3,11},{4,36},{5,13},{6,38},{7,15},{8,40},{9,1... | collective-permute-start | bytes 786440 | tf_op jit(solution)/shard_map/ppermute | solution.py:30
  84.7 8.5 %copy-start.12 = (bf16[256,512]{1,0:T(8,128)(2,1)}, bf16[256,512]{1,0:T(8,128)(2,1)S(1)}, u32[]{:S(2)}) copy-start(bf16[256,512]{1,0:T(8,128)(2,1)S(1)} %collective-permute-done.15.rest_1_) | copy-start | bytes 786436
  84.7 8.5 %collective-permute-start.17 = (bf16[256,512]{1,0:T(8,128)(2,1)S(1)}, bf16[256,512]{1,0:T(8,128)(2,1)S(1)}, u32[]{:S(2)}, u32[]{:S(2)}) collective-permute-start(bf16[256,512]{1,0:T(8,128)(2,1)S(1)} %collective-permute-done.14.rest_0_), channel_id=1, source_target_pairs={{0,48},{1,13},{2,50},{3,15},{4,52},{5,1},{6,54},{7,3},{8,56},{9,5}... | collective-permute-start | bytes 786440 | tf_op jit(solution)/shard_map/ppermute | solution.py:30
  84.7 8.5 %copy-start.15 = (bf16[256,512]{1,0:T(8,128)(2,1)}, bf16[256,512]{1,0:T(8,128)(2,1)S(1)}, u32[]{:S(2)}) copy-start(bf16[256,512]{1,0:T(8,128)(2,1)S(1)} %collective-permute-done.16.rest_2_) | copy-start | bytes 786436
  96.2 22.5 %collective-permute-start.21 = (bf16[1024,512]{1,0:T(8,128)(2,1)}, bf16[1024,512]{1,0:T(8,128)(2,1)}, u32[]{:S(2)}, u32[]{:S(2)}) collective-permute-start(bf16[1024,512]{1,0:T(8,128)(2,1)} %shard_map.61), channel_id=1, source_target_pairs={{0,12},{1,49},{2,14},{3,51},{4,0},{5,53},{6,2},{7,55},{8,4},{9,57}... | collective-permute-start | bytes 3145736 | tf_op jit(solution)/shard_map/ppermute | solution.py:30
  97.4 10.0 %copy-start = (bf16[1024,512]{1,0:T(8,128)(2,1)S(1)}, bf16[1024,512]{1,0:T(8,128)(2,1)}, u32[]{:S(2)}) copy-start(bf16[1024,512]{1,0:T(8,128)(2,1)} %shard_map.61) | copy-start | bytes 3145732
  97.4 11.6 %copy-start.1 = (bf16[1024,512]{1,0:T(8,128)(2,1)S(1)}, bf16[1024,512]{1,0:T(8,128)(2,1)}, u32[]{:S(2)}) copy-start(bf16[1024,512]{1,0:T(8,128)(2,1)} %shard_map.60) | copy-start | bytes 3145732
  107.4 16.3 %collective-permute-start.19 = (bf16[1024,512]{1,0:T(8,128)(2,1)S(1)}, bf16[1024,512]{1,0:T(8,128)(2,1)S(1)}, u32[]{:S(2)}, u32[]{:S(2)}) collective-permute-start(bf16[1024,512]{1,0:T(8,128)(2,1)S(1)} %copy-done), channel_id=1, source_target_pairs={{0,4},{1,17},{2,6},{3,19},{4,8},{5,21},{6,10},{7,23},{8,12},{9,25}... | collective-permute-start | bytes 3145736 | tf_op jit(solution)/shard_map/ppermute | solution.py:30
  111.9 36.9 %collective-permute-start.22 = (bf16[1024,512]{1,0:T(8,128)(2,1)}, bf16[1024,512]{1,0:T(8,128)(2,1)S(1)}, u32[]{:S(2)}, u32[]{:S(2)}) collective-permute-start(bf16[1024,512]{1,0:T(8,128)(2,1)} %collective-permute-done.18), channel_id=1, source_target_pairs={{0,4},{1,17},{2,6},{3,19},{4,8},{5,21},{6,10},{7,23},{8,12},{9,25}... | collective-permute-start | bytes 3145736 | tf_op jit(solution)/shard_map/ppermute | solution.py:30
  118.7 27.1 %collective-permute-start.23 = (bf16[1024,512]{1,0:T(8,128)(2,1)}, bf16[1024,512]{1,0:T(8,128)(2,1)}, u32[]{:S(2)}, u32[]{:S(2)}) collective-permute-start(bf16[1024,512]{1,0:T(8,128)(2,1)} %collective-permute-done.21), channel_id=1, source_target_pairs={{0,12},{1,49},{2,14},{3,51},{4,0},{5,53},{6,2},{7,55},{8,4},{9,57}... | collective-permute-start | bytes 3145736 | tf_op jit(solution)/shard_map/ppermute | solution.py:30
  150.0 8.1 %collective-permute-start.25 = (bf16[512,512]{0,1:T(8,128)(2,1)S(1)}, bf16[512,512]{0,1:T(8,128)(2,1)S(1)}, u32[]{:S(2)}, u32[]{:S(2)}) collective-permute-start(bf16[512,512]{0,1:T(8,128)(2,1)S(1)} %fusion.11), channel_id=1, source_target_pairs={{0,1},{1,0},{2,3},{3,2},{4,5},{5,4},{6,7},{7,6},{8,9},{9,8},{10,11... | collective-permute-start | bytes 1572872 | tf_op jit(solution)/shard_map/ppermute | solution.py:30
  (36 other events, 100.5 us)

commit v2 on v0

v2 whole, which is shorter than its diff:
```python
import functools

import jax
import jax.numpy as jnp
from jax import lax
from jax.experimental import pallas as pl
from jax.experimental.pallas import tpu as pltpu
from jax.sharding import Mesh, PartitionSpec as P

AXES = ("zh", "y", "x", "zl", "c")
SIZES = (4, 4, 4, 2, 2)
RANK = 64
HALF = 512
EPS = 1e-05
FEATURES = 8192
F32 = jnp.float32
BF16 = jnp.bfloat16


def pairs(move):
    out = []
    for src in range(256):
        core, rest = src % 2, src // 2
        zl, rest = rest % 2, rest // 2
        x, rest = rest % 4, rest // 4
        y, zh = rest % 4, rest // 4
        zh2, y2, x2, zl2, core2 = move(zh, y, x, zl, core)
        out.append((src, (((zh2 % 4 * 4 + y2 % 4) * 4 + x2 % 4) * 2 + zl2) * 2 + core2))
    return out


def send(array, move):
    return lax.ppermute(array, AXES, pairs(move))


def to_core(zh, y, x, zl, c):
    return zh, y, x, zl, 1 - c


def beside(zh, y, x, zl, c):
    if c == 0:
        return zh, y, x, 1 - zl, c
    return (zh - 1, y, x, 1, c) if zl == 0 else (zh + 1, y, x, 0, c)


def along_zh(k):
    return lambda zh, y, x, zl, c: (zh + k, y, x, zl, c)


def along_y(k):
    return lambda zh, y, x, zl, c: (zh, y + k, x, zl, c)


def first(k):
    return lambda zh, y, x, zl, c: (zh, y + k, x, zl, c) if c == 0 else (zh, y, x + k, zl, c)


def last(k):
    return lambda zh, y, x, zl, c: (zh, y, x + k, zl, c) if c == 0 else (zh, y + k, x, zl, c)


def after(array, *others):
    return lax.optimization_barrier((array, *others))[0]


VMEM = pl.BlockSpec(memory_space=pltpu.VMEM)


def call(body, operands, outs, scratch=(), cost=1024, flops=1024, free=()):
    operands = [
        pltpu.with_memory_space_constraint(a, pltpu.HBM if i in free else pltpu.VMEM) for i, a in enumerate(operands)
    ]
    return pl.pallas_call(
        body,
        out_shape=outs,
        in_specs=[VMEM] * len(operands),
        out_specs=jax.tree.map(lambda _: VMEM, outs),
        scratch_shapes=list(scratch),
        compiler_params=pltpu.CompilerParams(vmem_limit_bytes=16 << 20),
        cost_estimate=pl.CostEstimate(flops=flops, bytes_accessed=cost, transcendentals=0),
    )(*operands)


def prepare(own, other, up, *rest):
    outs, packed = rest[:4], rest[4]
    zh, c = lax.axis_index("zh"), lax.axis_index("c")
    mine, theirs = own[...].astype(F32), other[...].astype(F32)
    turned = jnp.where(c == 0, theirs, mine)
    turned = pltpu.roll(turned, RANK, 1)
    lane = lax.broadcasted_iota(jnp.int32, mine.shape, 1)
    low = jnp.where(c == 0, mine, turned)
    high = jnp.where(c == 0, turned, theirs)
    packed[...] = jnp.where(lane < RANK, low, high).astype(BF16)
    factor = up[pl.ds(c, 1)][0]
    for k in range(4):
        start = lax.rem(zh + k, 4) * 32
        outs[k][0:64, :] = factor
        for y in range(4):
            rows = pl.ds(pl.multiple_of(start + y * 128, 32), 32)
            outs[k][64:96, y * 128 : (y + 1) * 128] = packed[rows, :]


def partial_sums(*rest):
    parts, outs, total = rest[:4], rest[4:8], rest[8]
    y = lax.axis_index("y")
    lane = lax.broadcasted_iota(jnp.int32, (128, 128), 1)
    zero = jnp.zeros((128, 128), BF16)
    lefts, rights = [], []
    for part in parts:
        down = jnp.concatenate([part[64:96, j * 128 : (j + 1) * 128] for j in range(4)], axis=0)
        low = jnp.where(lane < RANK, down, zero)
        high = jnp.where(lane < RANK, zero, down)
        lefts.append(jnp.concatenate([low, high], axis=0))
        rights += [part[0:64, :]] * 2
    left = jnp.concatenate(lefts, axis=1)
    right = jnp.concatenate(rights, axis=0)
    total[...] = jnp.dot(left, right, preferred_element_type=F32)
    for k in range(4):
        start = pl.multiple_of(lax.rem(y + k, 4) * 32, 32)
        outs[k][0:32, :] = total[pl.ds(start, 32), :]
        outs[k][32:64, :] = total[pl.ds(start + 128, 32), :]


def merge(own, other, gain, a, b, c, d, out):
    update = 0.25 * ((a[...] + b[...]) + (c[...] + d[...]))
    out[0:32, :] = ((own[...].astype(F32) + update[0:32]) * gain[0:32]).astype(BF16)
    out[32:64, :] = ((other[...].astype(F32) + update[32:64]) * gain[32:64]).astype(BF16)


def assemble(*refs):
    parts, out = refs[:4], refs[4]
    zh = lax.axis_index("zh")
    for k in range(4):
        start = pl.multiple_of(lax.rem(zh + 4 - k, 4) * 32, 32)
        out[pl.ds(start, 32), :] = parts[k][0:32, :]
        out[pl.ds(start + 128, 32), :] = parts[k][32:64, :]


def join(*refs):
    parts, whole, mine, theirs = refs[:4], refs[4], refs[5], refs[6]
    for k in range(4):
        at, below = slice(k * 128, (k + 1) * 128), slice(512 + k * 128, 512 + (k + 1) * 128)
        whole[at, :] = mine[at, :] = parts[k][0:128, :]
        whole[below, :] = theirs[at, :] = parts[k][128:256, :]


def upper(rows, out):
    out[...] = rows[0:512, :]


def strip(place):
    y, x, zl, c = (lax.axis_index(a) for a in AXES[1:])
    block, part, core, step = place // 16, place // 8 % 2, place // 4 % 2, place % 4
    far = jnp.where(c == 0, x, y)
    near = jnp.where(c == 0, y, x)
    far = lax.rem(far + 4 - block, 4)
    near = lax.rem(near + 4 - step, 4)
    row_x = jnp.where(c == 0, far, near)
    row_y = jnp.where(c == 0, near, far)
    zl = zl if part == 0 else 1 - zl
    core = c if core == 0 else 1 - c
    return row_x * 16 + zl * 8 + core * 4 + row_y


TALL = 64
SHARE = 256


def stage_body(tokens, out, scale):
    at = pl.ds(pl.multiple_of(pl.program_id(0) * TALL, TALL), TALL)
    square = jnp.zeros((TALL, 128), F32)
    for place in range(64):
        column = pl.ds(pl.multiple_of(strip(place) * 128, 128), 128)
        piece = tokens[:, column]
        out[at, place * 128 : (place + 1) * 128] = piece
        value = piece.astype(F32)
        square = square + value * value
    mean = jnp.sum(square, axis=1, keepdims=True) / FEATURES
    scale[at, :] = jnp.broadcast_to(lax.rsqrt(mean + EPS), (TALL, 128))


def stage(tokens, share):
    steps = SHARE // TALL
    return pl.pallas_call(
        stage_body,
        grid=(steps,),
        out_shape=[pltpu.VMEM((SHARE, FEATURES), BF16), pltpu.VMEM((SHARE, 128), F32)],
        in_specs=[pl.BlockSpec((TALL, FEATURES), lambda i: (i + share * steps, 0))],
        out_specs=[VMEM] * 2,
        compiler_params=pltpu.CompilerParams(vmem_limit_bytes=16 << 20),
        cost_estimate=pl.CostEstimate(flops=1024, bytes_accessed=1024, transcendentals=0),
    )(pltpu.with_memory_space_constraint(tokens, pltpu.HBM))


def product_body(opening, closing, ats, *refs):
    shares = 2 if closing else 4
    tokens, rows, refs = refs[:shares], refs[shares : shares + len(ats)], refs[shares + len(ats) :]
    if not opening:
        sums, refs = refs[0], refs[1:]
    if closing:
        scales, refs = refs[:2], refs[2:]
    for who in range(shares):
        tall = slice(who * SHARE, (who + 1) * SHARE)
        past = slice((who + closing * 2 - 2) * SHARE, (who + closing * 2 - 1) * SHARE) if closing else tall
        total = None if opening else sums[past, :]
        for at, some in zip(ats, rows):
            term = jnp.dot(tokens[who][:, at : at + some.shape[0]], some[...], preferred_element_type=F32)
            total = term if total is None else total + term
        if closing:
            refs[0][tall, :] = (total * scales[who][:, 0:1]).astype(BF16)
        else:
            refs[0][tall, :] = total


def product(tokens, rows, state, ats, scales=(), closing=0):
    opening = state is None
    out = pltpu.VMEM((512, HALF), BF16) if closing else pltpu.VMEM((1024, HALF), F32)
    body = functools.partial(product_body, opening, closing, ats)
    operands = (*tokens, *rows, *(() if opening else (state,)), *scales)
    return call(body, operands, out)


def combine(own, other, out):
    c = lax.axis_index("c")

    @pl.when(c == 0)
    def _():
        out[:, 0:HALF] = own[...]
        out[:, HALF:] = other[...]

    @pl.when(c == 1)
    def _():
        out[:, 0:HALF] = other[...]
        out[:, HALF:] = own[...]


def per_device(tokens, gain, weight, down, up):
    zh, y, x, zl, c = (lax.axis_index(a) for a in AXES)
    down, up = down[0], up[0]

    down_other = send(down, to_core)
    parts = call(
        prepare,
        (down, down_other, up),
        [pltpu.VMEM((96, HALF), BF16)] * 4,
        [pltpu.VMEM((512, 128), BF16)],
        free=(0, 2),
    )
    parts = [parts[0]] + [send(parts[k], along_zh(k)) for k in (2, 1, 3)]

    row = y * 128 + zh * 32
    weight_own = lax.dynamic_slice(weight, (row, c * HALF), (32, HALF))
    weight_other = lax.dynamic_slice(weight, (row, (1 - c) * HALF), (32, HALF))
    weight_other = send(after(weight_other, parts[1]), to_core)
    tokens_other = send(after(tokens, down_other), to_core)
    start = (x * 2 + zl) * 1024 + row
    gains = [lax.dynamic_slice(gain, (start + who * HALF,), (32,)) for who in (c, 1 - c)]
    gains = jnp.broadcast_to(jnp.concatenate(gains).astype(F32)[:, None], (64, HALF))

    staged = [stage(after(tokens, parts[0]), 0), stage(tokens, 1), stage(tokens_other, 0), stage(tokens_other, 1)]
    every, scales = zip(*staged)

    parts = [after(parts[0], every[0]), *parts[1:]]
    sums = call(partial_sums, parts, [pltpu.VMEM((64, HALF), F32)] * 4, [pltpu.VMEM((256, HALF), F32)])
    sums = [sums[0]] + [send(sums[k], along_y(k)) for k in (1, 3, 2)]
    sums = [after(sums[0], every[1]), *sums[1:]]
    merged = call(merge, (weight_own, weight_other, gains, *sums), pltpu.VMEM((64, HALF), BF16))
    merged = [merged] + [send(merged, along_zh(k)) for k in (2, 1, 3)]
    merged = [after(merged[0], every[2]), merged[2], merged[1], merged[3]]
    chunk = call(assemble, merged, pltpu.VMEM((256, HALF), BF16))

    whole, slab = pltpu.VMEM((1024, HALF), BF16), pltpu.VMEM((512, HALF), BF16)
    near = [send(chunk, first(k)) for k in (1, 2, 3)]
    here0, up0, low0 = call(join, [after(chunk, every[3]), *near], [whole, slab, slab])

    here1 = send(here0, beside)
    left_low0, right_low0 = send(low0, last(-1)), send(low0, last(1))
    left_up0, right_up0 = send(up0, last(-1)), send(up0, last(1))
    state = product(every, (here0,), None, (0,))
    left_low0 = after(left_low0, state)
    left_low1 = send(left_low0, beside)
    right_low0 = after(right_low0, left_low0)
    right_low1 = send(right_low0, beside)
    here1 = after(here1, right_low0)
    up1 = call(upper, (here1,), slab)
    right_up1 = send(up1, last(1))
    left_up0 = after(left_up0, up1)
    left_up1 = send(after(up1, left_up0), last(-1))
    state = product(every, (here1,), after(state, left_up0), (1024,))
    right_up0 = after(right_up0, state)
    far_up0 = send(right_up0, last(1))
    left_low1 = after(left_low1, right_up0)
    far_low0 = send(after(left_low0, left_low1), last(-1))
    state = product(every, (left_up0, left_low0), after(state, left_low1), (6144, 6656))
    state = product(every, (right_up0, right_low0), state, (2048, 2560))
    right_up1 = after(right_up1, state)
    far_up1 = send(right_up1, last(1))
    left_up1 = after(left_up1, right_up1)
    far_low1 = send(after(left_low1, left_up1), last(-1))
    right_low1 = after(right_low1, left_up1)
    state = product(every, (right_up1, right_low1), after(state, right_low1), (3072, 3584))
    state = product(every, (left_up1, left_low1), state, (7168, 7680))
    far_up0 = after(far_up0, state)
    far_low0 = after(far_low0, far_up0)
    state = product(every, (far_up0, far_low0), state, (4096, 4608))
    far_up1 = after(far_up1, state)
    ending, ats = (far_up1, far_low1), (5120, 5632)
    theirs = product(every[2:], ending, state, ats, scales[2:], 2)
    back = send(theirs, to_core)
    mine = product(every[:2], ending, state, ats, scales[:2], 1)
    return call(combine, (mine, back), shape(512, 2 * HALF))


def shape(rows, columns, dtype=BF16):
    return jax.ShapeDtypeStruct((rows, columns), dtype)


def solution(mesh):
    fine = Mesh(mesh.devices.reshape(SIZES), AXES)
    rows = ("x", "zl", "c")
    placed = (
        P(AXES, None),
        P(),
        P(rows, None),
        P(("zh", "y"), rows, None),
        P(("zh", "y"), None, None, None),
    )
    return jax.shard_map(per_device, mesh=fine, in_specs=placed, out_specs=P(AXES, None), check_vma=False)
```

time: 312 us -> 101 us (0.32)
  waiting for transfers between devices: 272 us -> 20.8 us
  starting transfers between devices: 0.04 us -> 48.9 us
  Pallas kernels: 0 us -> 28.7 us
  matrix products: 16.2 us -> 0 us
  between operations: 13.4 us -> 0.23 us
  other arithmetic: 8.04 us -> 0.07 us
    psum x1 -> x0, waiting for transfers between devices: 173 us -> none  [per_device(): update = lax.psum(local_term, 'island')]
    all_gather x1 -> x0, waiting for transfers between devices: 98.1 us -> none  [per_device(): lax.all_gather(merged, 'fsdp', axis=0, tiled=True)]
    ppermute x0 -> x29, starting transfers between devices: none -> 48.9 us  [send(): return lax.ppermute(array, AXES, pairs(move))]
    pallas_call x0 -> x20, Pallas kernels: none -> 28.7 us  [the longest x4 15.8 us: stage(): pl.pallas_call(stage_body, grid=(steps,), out_shape=[pltpu.VMEM((SHARE, F...]
    ppermute x0 -> x29, waiting for transfers between devices: none -> 20.8 us  [send(): return lax.ppermute(array, AXES, pairs(move))]
    dot_general x2 -> x0, matrix products: 16.2 us -> none  [the longest x1 15.7 us: per_device(): jnp.dot(normed, lax.all_gather(merged, 'fsdp', axis=0, tiled=True), prefe...]
    reduce_sum x1 -> x0, other arithmetic: 5.1 us -> none  [per_device(): meansq = jnp.mean(values * values, axis=-1, keepdims=True)]
  transfers between devices with their start and end apart: 2 -> 29, of which waited for: 2 -> 12; matrix products, arithmetic and copies ran while one was open for 2% -> 2% of each run, Pallas kernels for 0% -> 27%
where the time goes in v2:
time: 101 us; the launch traced here: 100 us
  starting transfers between devices  48.9 us (48%)
  Pallas kernels  28.7 us (28%)
  waiting for transfers between devices  20.8 us (21%)
  local copies, waits for them, and re-layouts  1.68 us (2%)
    ppermute x29, starting transfers between devices, send(): return lax.ppermute(array, AXES, pairs(move))  48.9 us
    ppermute x29, waiting for transfers between devices, send(): return lax.ppermute(array, AXES, pairs(move))  20.8 us
    pallas_call x4, Pallas kernels, stage(): pl.pallas_call(stage_body, grid=(steps,), out_shape=[pltpu.VMEM((SHARE, F...  15.8 us
    pallas_call x16, Pallas kernels, call(): pl.pallas_call(body, out_shape=outs, in_specs=[VMEM] * len(operands), out...  12.9 us
  transfers between devices with their start and end apart: 29, of which 12 were waited for; matrix products, arithmetic and copies ran while one was open for 2% of the time, Pallas kernels for 27%

profile of v2, /device:TPU:1, one launch (start us, length us, event | category | flops | bytes accessed | tf_op | source)
XLA Modules:
  0.0 100.4 jit_solution(4099729805452337968)
XLA Ops:
  0.0 3.2 %collective-permute-start = (bf16[512,128]{1,0:T(8,128)(2,1)}, bf16[512,128]{1,0:T(8,128)(2,1)S(1)}, u32[]{:S(2)}, u32[]{:S(2)}) collective-permute-start(bf16[512,128]{1,0:T(8,128)(2,1)} %bitcast.2), channel_id=1, source_target_pairs={{0,1},{1,0},{2,3},{3,2},{4,5},{5,4},{6,7},{7,6},{8,9},{9,8},{10,11... | collective-permute-start | bytes 393224 | tf_op jit(solution)/shard_map/ppermute | solution.py:33
  5.9 5.3 %collective-permute-start.1 = (bf16[96,512]{1,0:T(8,128)(2,1)S(1)}, bf16[96,512]{1,0:T(8,128)(2,1)S(1)}, u32[]{:S(2)}, u32[]{:S(2)}) collective-permute-start(bf16[96,512]{1,0:T(8,128)(2,1)S(1)} %get-tuple-element.53), channel_id=1, source_target_pairs={{0,128},{1,129},{2,130},{3,131},{4,132},{5,133},{6,134},{7,135},{8... | collective-permute-start | bytes 294920 | tf_op jit(solution)/shard_map/ppermute | solution.py:33
  12.4 2.4 %collective-permute-start.4 = (bf16[96,512]{1,0:T(8,128)(2,1)S(1)}, bf16[96,512]{1,0:T(8,128)(2,1)S(1)}, u32[]{:S(2)}, u32[]{:S(2)}) collective-permute-start(bf16[96,512]{1,0:T(8,128)(2,1)S(1)} %get-tuple-element.57), channel_id=1, source_target_pairs={{0,192},{1,193},{2,194},{3,195},{4,196},{5,197},{6,198},{7,199},{8... | collective-permute-start | bytes 294920 | tf_op jit(solution)/shard_map/ppermute | solution.py:33
  15.5 4.0 %shard_map.56 = (bf16[256,8192]{1,0:T(8,128)(2,1)S(1)}, f32[256,128]{1,0:T(8,128)S(1)}) custom-call(bf16[512,8192]{1,0:T(8,128)(2,1)} %tokens.2), custom_call_target="tpu_custom_call" | custom-call | flops 1024 | bytes 1024 | tf_op jit(solution)/shard_map/pallas_call | solution.py:184
  19.5 1.8 %collective-permute-done.4.rest_3_ = bf16[96,512]{1,0:T(8,128)(2,1)S(1)} collective-permute-done((bf16[96,512]{1,0:T(8,128)(2,1)S(1)}, bf16[96,512]{1,0:T(8,128)(2,1)S(1)}, u32[]{:S(2)}, u32[]{:S(2)}) %collective-permute-start.4) | collective-permute-done | bytes 98336 | tf_op jit(solution)/shard_map/ppermute | solution.py:33
  21.7 1.4 %collective-permute-start.5 = (f32[64,512]{1,0:T(8,128)S(1)}, f32[64,512]{1,0:T(8,128)S(1)}, u32[]{:S(2)}, u32[]{:S(2)}) collective-permute-start(f32[64,512]{1,0:T(8,128)S(1)} %get-tuple-element.60), channel_id=1, source_target_pairs={{0,16},{1,17},{2,18},{3,19},{4,20},{5,21},{6,22},{7,23},{8,24},{9,... | collective-permute-start | bytes 393224 | tf_op jit(solution)/shard_map/ppermute | solution.py:33
  23.0 1.5 %collective-permute-start.6 = (f32[64,512]{1,0:T(8,128)S(1)}, f32[64,512]{1,0:T(8,128)S(1)}, u32[]{:S(2)}, u32[]{:S(2)}) collective-permute-start(f32[64,512]{1,0:T(8,128)S(1)} %get-tuple-element.61), channel_id=1, source_target_pairs={{0,48},{1,49},{2,50},{3,51},{4,52},{5,53},{6,54},{7,55},{8,56},{9,... | collective-permute-start | bytes 393224 | tf_op jit(solution)/shard_map/ppermute | solution.py:33
  24.6 1.6 %collective-permute-start.7 = (f32[64,512]{1,0:T(8,128)S(1)}, f32[64,512]{1,0:T(8,128)S(1)}, u32[]{:S(2)}, u32[]{:S(2)}) collective-permute-start(f32[64,512]{1,0:T(8,128)S(1)} %get-tuple-element.62), channel_id=1, source_target_pairs={{0,32},{1,33},{2,34},{3,35},{4,36},{5,37},{6,38},{7,39},{8,40},{9,... | collective-permute-start | bytes 393224 | tf_op jit(solution)/shard_map/ppermute | solution.py:33
  27.0 1.4 %collective-permute-start.2 = (bf16[32,512]{1,0:T(8,128)(2,1)S(1)}, bf16[32,512]{1,0:T(8,128)(2,1)S(1)}, u32[]{:S(2)}, u32[]{:S(2)}) collective-permute-start(bf16[32,512]{1,0:T(8,128)(2,1)S(1)} %get-tuple-element.54), channel_id=1, source_target_pairs={{0,1},{1,0},{2,3},{3,2},{4,5},{5,4},{6,7},{7,6},{8,9},{9,8},{10,11... | collective-permute-start | bytes 98312 | tf_op jit(solution)/shard_map/ppermute | solution.py:33
  28.4 4.0 %shard_map.57 = (bf16[256,8192]{1,0:T(8,128)(2,1)S(1)}, f32[256,128]{1,0:T(8,128)S(1)}) custom-call(bf16[512,8192]{1,0:T(8,128)(2,1)} %tokens.2), custom_call_target="tpu_custom_call" | custom-call | flops 1024 | bytes 1024 | tf_op jit(solution)/shard_map/pallas_call | solution.py:184
  32.6 4.0 %collective-permute-start.10 = (bf16[64,512]{1,0:T(8,128)(2,1)S(1)}, bf16[64,512]{1,0:T(8,128)(2,1)S(1)}, u32[]{:S(2)}, u32[]{:S(2)}) collective-permute-start(bf16[64,512]{1,0:T(8,128)(2,1)S(1)} %shard_map.59.refs_0_), channel_id=1, source_target_pairs={{0,128},{1,129},{2,130},{3,131},{4,132},{5,133},{6,134},{7,135},{8... | collective-permute-start | bytes 196616 | tf_op jit(solution)/shard_map/ppermute | solution.py:33
  37.1 1.8 %collective-permute-start.9 = (bf16[64,512]{1,0:T(8,128)(2,1)S(1)}, bf16[64,512]{1,0:T(8,128)(2,1)S(1)}, u32[]{:S(2)}, u32[]{:S(2)}) collective-permute-start(bf16[64,512]{1,0:T(8,128)(2,1)S(1)} %shard_map.59.refs_0_), channel_id=1, source_target_pairs={{0,64},{1,65},{2,66},{3,67},{4,68},{5,69},{6,70},{7,71},{8,72},{9,... | collective-permute-start | bytes 196616 | tf_op jit(solution)/shard_map/ppermute | solution.py:33
  39.0 4.0 %shard_map.60 = (bf16[256,8192]{1,0:T(8,128)(2,1)S(1)}, f32[256,128]{1,0:T(8,128)S(1)}) custom-call(bf16[512,8192]{1,0:T(8,128)(2,1)} %collective-permute-done.8.tokens), custom_call_target="tpu_custom_call" | custom-call | flops 1024 | bytes 1024 | tf_op jit(solution)/shard_map/pallas_call | solution.py:184
  42.9 1.7 %collective-permute-done.11.refs_3_ = bf16[64,512]{1,0:T(8,128)(2,1)S(1)} collective-permute-done((bf16[64,512]{1,0:T(8,128)(2,1)S(1)}, bf16[64,512]{1,0:T(8,128)(2,1)S(1)}, u32[]{:S(2)}, u32[]{:S(2)}) %collective-permute-start.11) | collective-permute-done | bytes 65568 | tf_op jit(solution)/shard_map/ppermute | solution.py:33
  44.6 1.3 %collective-permute-start.12 = (bf16[256,512]{1,0:T(8,128)(2,1)S(1)}, bf16[256,512]{1,0:T(8,128)(2,1)S(1)}, u32[]{:S(2)}, u32[]{:S(2)}) collective-permute-start(bf16[256,512]{1,0:T(8,128)(2,1)S(1)} %shard_map.61.refs_0_), channel_id=1, source_target_pairs={{0,16},{1,5},{2,18},{3,7},{4,20},{5,9},{6,22},{7,11},{8,24},{9,13}... | collective-permute-start | bytes 786440 | tf_op jit(solution)/shard_map/ppermute | solution.py:33
  45.9 2.4 %collective-permute-start.13 = (bf16[256,512]{1,0:T(8,128)(2,1)S(1)}, bf16[256,512]{1,0:T(8,128)(2,1)S(1)}, u32[]{:S(2)}, u32[]{:S(2)}) collective-permute-start(bf16[256,512]{1,0:T(8,128)(2,1)S(1)} %shard_map.61.refs_0_), channel_id=1, source_target_pairs={{0,32},{1,9},{2,34},{3,11},{4,36},{5,13},{6,38},{7,15},{8,40},{9,1... | collective-permute-start | bytes 786440 | tf_op jit(solution)/shard_map/ppermute | solution.py:33
  49.5 4.0 %shard_map.62 = (bf16[256,8192]{1,0:T(8,128)(2,1)S(1)}, f32[256,128]{1,0:T(8,128)S(1)}) custom-call(bf16[512,8192]{1,0:T(8,128)(2,1)} %collective-permute-done.8.tokens), custom_call_target="tpu_custom_call" | custom-call | flops 1024 | bytes 1024 | tf_op jit(solution)/shard_map/pallas_call | solution.py:184
  53.5 1.4 %collective-permute-done.13.refs_2_ = bf16[256,512]{1,0:T(8,128)(2,1)S(1)} collective-permute-done((bf16[256,512]{1,0:T(8,128)(2,1)S(1)}, bf16[256,512]{1,0:T(8,128)(2,1)S(1)}, u32[]{:S(2)}, u32[]{:S(2)}) %collective-permute-start.13) | collective-permute-done | bytes 262176 | tf_op jit(solution)/shard_map/ppermute | solution.py:33
  55.1 1.3 %collective-permute-start.15 = (bf16[1024,512]{1,0:T(8,128)(2,1)S(1)}, bf16[1024,512]{1,0:T(8,128)(2,1)S(1)}, u32[]{:S(2)}, u32[]{:S(2)}) collective-permute-start(bf16[1024,512]{1,0:T(8,128)(2,1)S(1)} %get-tuple-element.68.refs_4_), channel_id=1, source_target_pairs={{0,2},{1,195},{2,0},{3,65},{4,6},{5,199},{6,4},{7,69},{8,10},{9,20... | collective-permute-start | bytes 3145736 | tf_op jit(solution)/shard_map/ppermute | solution.py:33
  56.4 1.5 %collective-permute-start.16 = (bf16[512,512]{1,0:T(8,128)(2,1)S(1)}, bf16[512,512]{1,0:T(8,128)(2,1)S(1)}, u32[]{:S(2)}, u32[]{:S(2)}) collective-permute-start(bf16[512,512]{1,0:T(8,128)(2,1)S(1)} %get-tuple-element.69), channel_id=1, source_target_pairs={{0,4},{1,17},{2,6},{3,19},{4,8},{5,21},{6,10},{7,23},{8,12},{9,25}... | collective-permute-start | bytes 1572872 | tf_op jit(solution)/shard_map/ppermute | solution.py:33
  60.6 4.1 %collective-permute-done.17.refs_5_ = bf16[512,512]{1,0:T(8,128)(2,1)S(1)} collective-permute-done((bf16[512,512]{1,0:T(8,128)(2,1)S(1)}, bf16[512,512]{1,0:T(8,128)(2,1)S(1)}, u32[]{:S(2)}, u32[]{:S(2)}) %collective-permute-start.17) | collective-permute-done | bytes 524320 | tf_op jit(solution)/shard_map/ppermute | solution.py:33
  64.7 1.5 %collective-permute-start.21 = (bf16[512,512]{1,0:T(8,128)(2,1)S(1)}, bf16[512,512]{1,0:T(8,128)(2,1)S(1)}, u32[]{:S(2)}, u32[]{:S(2)}) collective-permute-start(bf16[512,512]{1,0:T(8,128)(2,1)S(1)} %collective-permute-done.17.refs_5_), channel_id=1, source_target_pairs={{0,2},{1,195},{2,0},{3,65},{4,6},{5,199},{6,4},{7,69},{8,10},{9,20... | collective-permute-start | bytes 1572872 | tf_op jit(solution)/shard_map/ppermute | solution.py:33
  66.2 4.1 %collective-permute-done.15.rows.refs_4_ = bf16[1024,512]{1,0:T(8,128)(2,1)S(1)} collective-permute-done((bf16[1024,512]{1,0:T(8,128)(2,1)S(1)}, bf16[1024,512]{1,0:T(8,128)(2,1)S(1)}, u32[]{:S(2)}, u32[]{:S(2)}) %collective-permute-start.15) | collective-permute-done | bytes 1048608 | tf_op jit(solution)/shard_map/ppermute | solution.py:33
  70.8 2.3 %collective-permute-start.24 = (bf16[512,512]{1,0:T(8,128)(2,1)S(1)}, bf16[512,512]{1,0:T(8,128)(2,1)S(1)}, u32[]{:S(2)}, u32[]{:S(2)}) collective-permute-start(bf16[512,512]{1,0:T(8,128)(2,1)S(1)} %shard_map.65), channel_id=1, source_target_pairs={{0,12},{1,49},{2,14},{3,51},{4,0},{5,53},{6,2},{7,55},{8,4},{9,57}... | collective-permute-start | bytes 1572872 | tf_op jit(solution)/shard_map/ppermute | solution.py:33
  74.3 1.2 %shard_map.66.refs_6_ = f32[1024,512]{1,0:T(8,128)S(1)} custom-call(bf16[256,8192]{1,0:T(8,128)(2,1)S(1)} %get-tuple-element.51.refs_0_, bf16[256,8192]{1,0:T(8,128)(2,1)S(1)} %get-tuple-element.52.refs_1_, bf16[256,8192]{1,0:T(8,128)(2,1)S(1)} %get-tuple-element.64.refs_2_.refs_0_, bf16[256,8192]{1,0:T(8,128)(2,1)S(1)} %get-tuple-element.66.refs_3_.refs_1_, ...), custom_call_target="tpu_custom_call" | custom-call | flops 1024 | bytes 1024 | tf_op jit(solution)/shard_map/pallas_call | solution.py:73
  77.7 1.2 %shard_map.68.refs_6_ = f32[1024,512]{1,0:T(8,128)S(1)} custom-call(bf16[256,8192]{1,0:T(8,128)(2,1)S(1)} %get-tuple-element.51.refs_0_, bf16[256,8192]{1,0:T(8,128)(2,1)S(1)} %get-tuple-element.52.refs_1_, bf16[256,8192]{1,0:T(8,128)(2,1)S(1)} %get-tuple-element.64.refs_2_.refs_0_, bf16[256,8192]{1,0:T(8,128)(2,1)S(1)} %get-tuple-element.66.refs_3_.refs_1_, ...), custom_call_target="tpu_custom_call" | custom-call | flops 1024 | bytes 1024 | tf_op jit(solution)/shard_map/pallas_call | solution.py:73
  78.9 2.4 %collective-permute-start.26 = (bf16[512,512]{1,0:T(8,128)(2,1)S(1)}, bf16[512,512]{1,0:T(8,128)(2,1)S(1)}, u32[]{:S(2)}, u32[]{:S(2)}) collective-permute-start(bf16[512,512]{1,0:T(8,128)(2,1)S(1)} %collective-permute-done.17.refs_5_), channel_id=1, source_target_pairs={{0,12},{1,49},{2,14},{3,51},{4,0},{5,53},{6,2},{7,55},{8,4},{9,57}... | collective-permute-start | bytes 1572872 | tf_op jit(solution)/shard_map/ppermute | solution.py:33
  81.3 2.7 %collective-permute-start.27 = (bf16[512,512]{1,0:T(8,128)(2,1)S(1)}, bf16[512,512]{1,0:T(8,128)(2,1)S(1)}, u32[]{:S(2)}, u32[]{:S(2)}) collective-permute-start(bf16[512,512]{1,0:T(8,128)(2,1)S(1)} %collective-permute-done.21.refs_5_), channel_id=1, source_target_pairs={{0,12},{1,49},{2,14},{3,51},{4,0},{5,53},{6,2},{7,55},{8,4},{9,57}... | collective-permute-start | bytes 1572872 | tf_op jit(solution)/shard_map/ppermute | solution.py:33
  84.0 1.2 %shard_map.69.refs_6_ = f32[1024,512]{1,0:T(8,128)S(1)} custom-call(bf16[256,8192]{1,0:T(8,128)(2,1)S(1)} %get-tuple-element.51.refs_0_, bf16[256,8192]{1,0:T(8,128)(2,1)S(1)} %get-tuple-element.52.refs_1_, bf16[256,8192]{1,0:T(8,128)(2,1)S(1)} %get-tuple-element.64.refs_2_.refs_0_, bf16[256,8192]{1,0:T(8,128)(2,1)S(1)} %get-tuple-element.66.refs_3_.refs_1_, ...), custom_call_target="tpu_custom_call" | custom-call | flops 1024 | bytes 1024 | tf_op jit(solution)/shard_map/pallas_call | solution.py:73
  85.2 1.2 %shard_map.70.refs_6_ = f32[1024,512]{1,0:T(8,128)S(1)} custom-call(bf16[256,8192]{1,0:T(8,128)(2,1)S(1)} %get-tuple-element.51.refs_0_, bf16[256,8192]{1,0:T(8,128)(2,1)S(1)} %get-tuple-element.52.refs_1_, bf16[256,8192]{1,0:T(8,128)(2,1)S(1)} %get-tuple-element.64.refs_2_.refs_0_, bf16[256,8192]{1,0:T(8,128)(2,1)S(1)} %get-tuple-element.66.refs_3_.refs_1_, ...), custom_call_target="tpu_custom_call" | custom-call | flops 1024 | bytes 1024 | tf_op jit(solution)/shard_map/pallas_call | solution.py:73
  88.6 3.8 %collective-permute-done.22.refs_2_ = bf16[512,512]{1,0:T(8,128)(2,1)S(1)} collective-permute-done((bf16[512,512]{1,0:T(8,128)(2,1)S(1)}, bf16[512,512]{1,0:T(8,128)(2,1)S(1)}, u32[]{:S(2)}, u32[]{:S(2)}) %collective-permute-start.22) | collective-permute-done | bytes 524320 | tf_op jit(solution)/shard_map/ppermute | solution.py:33
  93.7 4.0 %collective-permute-start.28 = (bf16[512,512]{1,0:T(8,128)(2,1)S(1)}, bf16[512,512]{1,0:T(8,128)(2,1)S(1)}, u32[]{:S(2)}, u32[]{:S(2)}) collective-permute-start(bf16[512,512]{1,0:T(8,128)(2,1)S(1)} %shard_map.73), channel_id=1, source_target_pairs={{0,1},{1,0},{2,3},{3,2},{4,5},{5,4},{6,7},{7,6},{8,9},{9,8},{10,11... | collective-permute-start | bytes 1572872 | tf_op jit(solution)/shard_map/ppermute | solution.py:33
  (50 shorter events, 20.5 us)
Async XLA Ops:
  0.0 4.4 %collective-permute-start = (bf16[512,128]{1,0:T(8,128)(2,1)}, bf16[512,128]{1,0:T(8,128)(2,1)S(1)}, u32[]{:S(2)}, u32[]{:S(2)}) collective-permute-start(bf16[512,128]{1,0:T(8,128)(2,1)} %bitcast.2), channel_id=1, source_target_pairs={{0,1},{1,0},{2,3},{3,2},{4,5},{5,4},{6,7},{7,6},{8,9},{9,8},{10,11... | collective-permute-start | bytes 393224 | tf_op jit(solution)/shard_map/ppermute | solution.py:33
  4.4 34.5 %collective-permute-start.8 = (bf16[512,8192]{1,0:T(8,128)(2,1)}, bf16[512,8192]{1,0:T(8,128)(2,1)}, u32[]{:S(2)}, u32[]{:S(2)}) collective-permute-start(bf16[512,8192]{1,0:T(8,128)(2,1)} %tokens.2), channel_id=1, source_target_pairs={{0,1},{1,0},{2,3},{3,2},{4,5},{5,4},{6,7},{7,6},{8,9},{9,8},{10,11... | collective-permute-start | bytes 25165832 | tf_op jit(solution)/shard_map/ppermute | solution.py:33
  5.9 13.6 %collective-permute-start.1 = (bf16[96,512]{1,0:T(8,128)(2,1)S(1)}, bf16[96,512]{1,0:T(8,128)(2,1)S(1)}, u32[]{:S(2)}, u32[]{:S(2)}) collective-permute-start(bf16[96,512]{1,0:T(8,128)(2,1)S(1)} %get-tuple-element.53), channel_id=1, source_target_pairs={{0,128},{1,129},{2,130},{3,131},{4,132},{5,133},{6,134},{7,135},{8... | collective-permute-start | bytes 294920 | tf_op jit(solution)/shard_map/ppermute | solution.py:33
  11.2 8.3 %collective-permute-start.3 = (bf16[96,512]{1,0:T(8,128)(2,1)S(1)}, bf16[96,512]{1,0:T(8,128)(2,1)S(1)}, u32[]{:S(2)}, u32[]{:S(2)}) collective-permute-start(bf16[96,512]{1,0:T(8,128)(2,1)S(1)} %get-tuple-element.56), channel_id=1, source_target_pairs={{0,64},{1,65},{2,66},{3,67},{4,68},{5,69},{6,70},{7,71},{8,72},{9,... | collective-permute-start | bytes 294920 | tf_op jit(solution)/shard_map/ppermute | solution.py:33
  12.4 8.9 %collective-permute-start.4 = (bf16[96,512]{1,0:T(8,128)(2,1)S(1)}, bf16[96,512]{1,0:T(8,128)(2,1)S(1)}, u32[]{:S(2)}, u32[]{:S(2)}) collective-permute-start(bf16[96,512]{1,0:T(8,128)(2,1)S(1)} %get-tuple-element.57), channel_id=1, source_target_pairs={{0,192},{1,193},{2,194},{3,195},{4,196},{5,197},{6,198},{7,199},{8... | collective-permute-start | bytes 294920 | tf_op jit(solution)/shard_map/ppermute | solution.py:33
  21.7 10.8 %collective-permute-start.5 = (f32[64,512]{1,0:T(8,128)S(1)}, f32[64,512]{1,0:T(8,128)S(1)}, u32[]{:S(2)}, u32[]{:S(2)}) collective-permute-start(f32[64,512]{1,0:T(8,128)S(1)} %get-tuple-element.60), channel_id=1, source_target_pairs={{0,16},{1,17},{2,18},{3,19},{4,20},{5,21},{6,22},{7,23},{8,24},{9,... | collective-permute-start | bytes 393224 | tf_op jit(solution)/shard_map/ppermute | solution.py:33
  23.0 9.4 %collective-permute-start.6 = (f32[64,512]{1,0:T(8,128)S(1)}, f32[64,512]{1,0:T(8,128)S(1)}, u32[]{:S(2)}, u32[]{:S(2)}) collective-permute-start(f32[64,512]{1,0:T(8,128)S(1)} %get-tuple-element.61), channel_id=1, source_target_pairs={{0,48},{1,49},{2,50},{3,51},{4,52},{5,53},{6,54},{7,55},{8,56},{9,... | collective-permute-start | bytes 393224 | tf_op jit(solution)/shard_map/ppermute | solution.py:33
  24.6 7.9 %collective-permute-start.7 = (f32[64,512]{1,0:T(8,128)S(1)}, f32[64,512]{1,0:T(8,128)S(1)}, u32[]{:S(2)}, u32[]{:S(2)}) collective-permute-start(f32[64,512]{1,0:T(8,128)S(1)} %get-tuple-element.62), channel_id=1, source_target_pairs={{0,32},{1,33},{2,34},{3,35},{4,36},{5,37},{6,38},{7,39},{8,40},{9,... | collective-permute-start | bytes 393224 | tf_op jit(solution)/shard_map/ppermute | solution.py:33
  27.0 5.5 %collective-permute-start.2 = (bf16[32,512]{1,0:T(8,128)(2,1)S(1)}, bf16[32,512]{1,0:T(8,128)(2,1)S(1)}, u32[]{:S(2)}, u32[]{:S(2)}) collective-permute-start(bf16[32,512]{1,0:T(8,128)(2,1)S(1)} %get-tuple-element.54), channel_id=1, source_target_pairs={{0,1},{1,0},{2,3},{3,2},{4,5},{5,4},{6,7},{7,6},{8,9},{9,8},{10,11... | collective-permute-start | bytes 98312 | tf_op jit(solution)/shard_map/ppermute | solution.py:33
  32.6 10.4 %collective-permute-start.10 = (bf16[64,512]{1,0:T(8,128)(2,1)S(1)}, bf16[64,512]{1,0:T(8,128)(2,1)S(1)}, u32[]{:S(2)}, u32[]{:S(2)}) collective-permute-start(bf16[64,512]{1,0:T(8,128)(2,1)S(1)} %shard_map.59.refs_0_), channel_id=1, source_target_pairs={{0,128},{1,129},{2,130},{3,131},{4,132},{5,133},{6,134},{7,135},{8... | collective-permute-start | bytes 196616 | tf_op jit(solution)/shard_map/ppermute | solution.py:33
  36.6 8.0 %collective-permute-start.11 = (bf16[64,512]{1,0:T(8,128)(2,1)S(1)}, bf16[64,512]{1,0:T(8,128)(2,1)S(1)}, u32[]{:S(2)}, u32[]{:S(2)}) collective-permute-start(bf16[64,512]{1,0:T(8,128)(2,1)S(1)} %shard_map.59.refs_0_), channel_id=1, source_target_pairs={{0,192},{1,193},{2,194},{3,195},{4,196},{5,197},{6,198},{7,199},{8... | collective-permute-start | bytes 196616 | tf_op jit(solution)/shard_map/ppermute | solution.py:33
  37.1 7.5 %collective-permute-start.9 = (bf16[64,512]{1,0:T(8,128)(2,1)S(1)}, bf16[64,512]{1,0:T(8,128)(2,1)S(1)}, u32[]{:S(2)}, u32[]{:S(2)}) collective-permute-start(bf16[64,512]{1,0:T(8,128)(2,1)S(1)} %shard_map.59.refs_0_), channel_id=1, source_target_pairs={{0,64},{1,65},{2,66},{3,67},{4,68},{5,69},{6,70},{7,71},{8,72},{9,... | collective-permute-start | bytes 196616 | tf_op jit(solution)/shard_map/ppermute | solution.py:33
  44.6 8.9 %collective-permute-start.12 = (bf16[256,512]{1,0:T(8,128)(2,1)S(1)}, bf16[256,512]{1,0:T(8,128)(2,1)S(1)}, u32[]{:S(2)}, u32[]{:S(2)}) collective-permute-start(bf16[256,512]{1,0:T(8,128)(2,1)S(1)} %shard_map.61.refs_0_), channel_id=1, source_target_pairs={{0,16},{1,5},{2,18},{3,7},{4,20},{5,9},{6,22},{7,11},{8,24},{9,13}... | collective-permute-start | bytes 786440 | tf_op jit(solution)/shard_map/ppermute | solution.py:33
  45.9 9.0 %collective-permute-start.13 = (bf16[256,512]{1,0:T(8,128)(2,1)S(1)}, bf16[256,512]{1,0:T(8,128)(2,1)S(1)}, u32[]{:S(2)}, u32[]{:S(2)}) collective-permute-start(bf16[256,512]{1,0:T(8,128)(2,1)S(1)} %shard_map.61.refs_0_), channel_id=1, source_target_pairs={{0,32},{1,9},{2,34},{3,11},{4,36},{5,13},{6,38},{7,15},{8,40},{9,1... | collective-permute-start | bytes 786440 | tf_op jit(solution)/shard_map/ppermute | solution.py:33
  48.4 6.6 %collective-permute-start.14 = (bf16[256,512]{1,0:T(8,128)(2,1)S(1)}, bf16[256,512]{1,0:T(8,128)(2,1)S(1)}, u32[]{:S(2)}, u32[]{:S(2)}) collective-permute-start(bf16[256,512]{1,0:T(8,128)(2,1)S(1)} %shard_map.61.refs_0_), channel_id=1, source_target_pairs={{0,48},{1,13},{2,50},{3,15},{4,52},{5,1},{6,54},{7,3},{8,56},{9,5}... | collective-permute-start | bytes 786440 | tf_op jit(solution)/shard_map/ppermute | solution.py:33
  55.1 15.2 %collective-permute-start.15 = (bf16[1024,512]{1,0:T(8,128)(2,1)S(1)}, bf16[1024,512]{1,0:T(8,128)(2,1)S(1)}, u32[]{:S(2)}, u32[]{:S(2)}) collective-permute-start(bf16[1024,512]{1,0:T(8,128)(2,1)S(1)} %get-tuple-element.68.refs_4_), channel_id=1, source_target_pairs={{0,2},{1,195},{2,0},{3,65},{4,6},{5,199},{6,4},{7,69},{8,10},{9,20... | collective-permute-start | bytes 3145736 | tf_op jit(solution)/shard_map/ppermute | solution.py:33
  56.4 8.3 %collective-permute-start.17 = (bf16[512,512]{1,0:T(8,128)(2,1)S(1)}, bf16[512,512]{1,0:T(8,128)(2,1)S(1)}, u32[]{:S(2)}, u32[]{:S(2)}) collective-permute-start(bf16[512,512]{1,0:T(8,128)(2,1)S(1)} %get-tuple-element.69), channel_id=1, source_target_pairs={{0,12},{1,49},{2,14},{3,51},{4,0},{5,53},{6,2},{7,55},{8,4},{9,57}... | collective-permute-start | bytes 1572872 | tf_op jit(solution)/shard_map/ppermute | solution.py:33
  56.4 9.8 %collective-permute-start.16 = (bf16[512,512]{1,0:T(8,128)(2,1)S(1)}, bf16[512,512]{1,0:T(8,128)(2,1)S(1)}, u32[]{:S(2)}, u32[]{:S(2)}) collective-permute-start(bf16[512,512]{1,0:T(8,128)(2,1)S(1)} %get-tuple-element.69), channel_id=1, source_target_pairs={{0,4},{1,17},{2,6},{3,19},{4,8},{5,21},{6,10},{7,23},{8,12},{9,25}... | collective-permute-start | bytes 1572872 | tf_op jit(solution)/shard_map/ppermute | solution.py:33
  57.8 13.0 %collective-permute-start.20 = (bf16[512,512]{1,0:T(8,128)(2,1)S(1)}, bf16[512,512]{1,0:T(8,128)(2,1)S(1)}, u32[]{:S(2)}, u32[]{:S(2)}) collective-permute-start(bf16[512,512]{1,0:T(8,128)(2,1)S(1)} %get-tuple-element.73), channel_id=1, source_target_pairs={{0,12},{1,49},{2,14},{3,51},{4,0},{5,53},{6,2},{7,55},{8,4},{9,57}... | collective-permute-start | bytes 1572872 | tf_op jit(solution)/shard_map/ppermute | solution.py:33
  60.3 15.3 %collective-permute-start.19 = (bf16[512,512]{1,0:T(8,128)(2,1)S(1)}, bf16[512,512]{1,0:T(8,128)(2,1)S(1)}, u32[]{:S(2)}, u32[]{:S(2)}) collective-permute-start(bf16[512,512]{1,0:T(8,128)(2,1)S(1)} %get-tuple-element.73), channel_id=1, source_target_pairs={{0,4},{1,17},{2,6},{3,19},{4,8},{5,21},{6,10},{7,23},{8,12},{9,25}... | collective-permute-start | bytes 1572872 | tf_op jit(solution)/shard_map/ppermute | solution.py:33
  64.7 11.2 %collective-permute-start.21 = (bf16[512,512]{1,0:T(8,128)(2,1)S(1)}, bf16[512,512]{1,0:T(8,128)(2,1)S(1)}, u32[]{:S(2)}, u32[]{:S(2)}) collective-permute-start(bf16[512,512]{1,0:T(8,128)(2,1)S(1)} %collective-permute-done.17.refs_5_), channel_id=1, source_target_pairs={{0,2},{1,195},{2,0},{3,65},{4,6},{5,199},{6,4},{7,69},{8,10},{9,20... | collective-permute-start | bytes 1572872 | tf_op jit(solution)/shard_map/ppermute | solution.py:33
  70.4 10.9 %collective-permute-start.18 = (bf16[512,512]{1,0:T(8,128)(2,1)S(1)}, bf16[512,512]{1,0:T(8,128)(2,1)S(1)}, u32[]{:S(2)}, u32[]{:S(2)}) collective-permute-start(bf16[512,512]{1,0:T(8,128)(2,1)S(1)} %shard_map.65), channel_id=1, source_target_pairs={{0,4},{1,17},{2,6},{3,19},{4,8},{5,21},{6,10},{7,23},{8,12},{9,25}... | collective-permute-start | bytes 1572872 | tf_op jit(solution)/shard_map/ppermute | solution.py:33
  70.8 10.4 %collective-permute-start.24 = (bf16[512,512]{1,0:T(8,128)(2,1)S(1)}, bf16[512,512]{1,0:T(8,128)(2,1)S(1)}, u32[]{:S(2)}, u32[]{:S(2)}) collective-permute-start(bf16[512,512]{1,0:T(8,128)(2,1)S(1)} %shard_map.65), channel_id=1, source_target_pairs={{0,12},{1,49},{2,14},{3,51},{4,0},{5,53},{6,2},{7,55},{8,4},{9,57}... | collective-permute-start | bytes 1572872 | tf_op jit(solution)/shard_map/ppermute | solution.py:33
  73.1 10.8 %collective-permute-start.25 = (bf16[512,512]{1,0:T(8,128)(2,1)S(1)}, bf16[512,512]{1,0:T(8,128)(2,1)S(1)}, u32[]{:S(2)}, u32[]{:S(2)}) collective-permute-start(bf16[512,512]{1,0:T(8,128)(2,1)S(1)} %collective-permute-done.16.refs_5_), channel_id=1, source_target_pairs={{0,2},{1,195},{2,0},{3,65},{4,6},{5,199},{6,4},{7,69},{8,10},{9,20... | collective-permute-start | bytes 1572872 | tf_op jit(solution)/shard_map/ppermute | solution.py:33
  77.2 9.6 %collective-permute-start.23 = (bf16[512,512]{1,0:T(8,128)(2,1)S(1)}, bf16[512,512]{1,0:T(8,128)(2,1)S(1)}, u32[]{:S(2)}, u32[]{:S(2)}) collective-permute-start(bf16[512,512]{1,0:T(8,128)(2,1)S(1)} %collective-permute-done.19.refs_4_), channel_id=1, source_target_pairs={{0,4},{1,17},{2,6},{3,19},{4,8},{5,21},{6,10},{7,23},{8,12},{9,25}... | collective-permute-start | bytes 1572872 | tf_op jit(solution)/shard_map/ppermute | solution.py:33
  78.9 8.5 %collective-permute-start.26 = (bf16[512,512]{1,0:T(8,128)(2,1)S(1)}, bf16[512,512]{1,0:T(8,128)(2,1)S(1)}, u32[]{:S(2)}, u32[]{:S(2)}) collective-permute-start(bf16[512,512]{1,0:T(8,128)(2,1)S(1)} %collective-permute-done.17.refs_5_), channel_id=1, source_target_pairs={{0,12},{1,49},{2,14},{3,51},{4,0},{5,53},{6,2},{7,55},{8,4},{9,57}... | collective-permute-start | bytes 1572872 | tf_op jit(solution)/shard_map/ppermute | solution.py:33
  81.3 11.1 %collective-permute-start.22 = (bf16[512,512]{1,0:T(8,128)(2,1)S(1)}, bf16[512,512]{1,0:T(8,128)(2,1)S(1)}, u32[]{:S(2)}, u32[]{:S(2)}) collective-permute-start(bf16[512,512]{1,0:T(8,128)(2,1)S(1)} %collective-permute-done.18.refs_4_), channel_id=1, source_target_pairs={{0,4},{1,17},{2,6},{3,19},{4,8},{5,21},{6,10},{7,23},{8,12},{9,25}... | collective-permute-start | bytes 1572872 | tf_op jit(solution)/shard_map/ppermute | solution.py:33
  81.3 11.7 %collective-permute-start.27 = (bf16[512,512]{1,0:T(8,128)(2,1)S(1)}, bf16[512,512]{1,0:T(8,128)(2,1)S(1)}, u32[]{:S(2)}, u32[]{:S(2)}) collective-permute-start(bf16[512,512]{1,0:T(8,128)(2,1)S(1)} %collective-permute-done.21.refs_5_), channel_id=1, source_target_pairs={{0,12},{1,49},{2,14},{3,51},{4,0},{5,53},{6,2},{7,55},{8,4},{9,57}... | collective-permute-start | bytes 1572872 | tf_op jit(solution)/shard_map/ppermute | solution.py:33
  93.7 5.6 %collective-permute-start.28 = (bf16[512,512]{1,0:T(8,128)(2,1)S(1)}, bf16[512,512]{1,0:T(8,128)(2,1)S(1)}, u32[]{:S(2)}, u32[]{:S(2)}) collective-permute-start(bf16[512,512]{1,0:T(8,128)(2,1)S(1)} %shard_map.73), channel_id=1, source_target_pairs={{0,1},{1,0},{2,3},{3,2},{4,5},{5,4},{6,7},{7,6},{8,9},{9,8},{10,11... | collective-permute-start | bytes 1572872 | tf_op jit(solution)/shard_map/ppermute | solution.py:33

commit v3 on v2

--- a/solution.py
+++ b/solution.py
@@ -64,16 +64,18 @@
 
 
 VMEM = pl.BlockSpec(memory_space=pltpu.VMEM)
-
-
-def call(body, operands, outs, scratch=(), cost=1024, flops=1024, free=()):
+HBM = pl.BlockSpec(memory_space=pltpu.HBM)
+
+
+def call(body, operands, outs, scratch=(), cost=1024, flops=1024, free=(), far=()):
     operands = [
-        pltpu.with_memory_space_constraint(a, pltpu.HBM if i in free else pltpu.VMEM) for i, a in enumerate(operands)
+        pltpu.with_memory_space_constraint(a, pltpu.HBM if i in free + far else pltpu.VMEM)
+        for i, a in enumerate(operands)
     ]
     return pl.pallas_call(
         body,
         out_shape=outs,
-        in_specs=[VMEM] * len(operands),
+        in_specs=[HBM if i in far else VMEM for i in range(len(operands))],
         out_specs=jax.tree.map(lambda _: VMEM, outs),
         scratch_shapes=list(scratch),
         compiler_params=pltpu.CompilerParams(vmem_limit_bytes=16 << 20),
@@ -81,9 +83,15 @@
     )(*operands)
 
 
-def prepare(own, other, up, *rest):
-    outs, packed = rest[:4], rest[4]
-    zh, c = lax.axis_index("zh"), lax.axis_index("c")
+def prepare(own, other, up, weight, *rest):
+    outs, kept, given, packed, arrived = rest[:4], rest[4], rest[5], rest[6], rest[7]
+    y, zh, c = lax.axis_index("y"), lax.axis_index("zh"), lax.axis_index("c")
+    rows = pl.ds(pl.multiple_of(y * 128 + zh * 32, 32), 32)
+    copies = []
+    for out, half in ((kept, c), (given, 1 - c)):
+        columns = pl.ds(pl.multiple_of(half * HALF, HALF), HALF)
+        copies.append(pltpu.make_async_copy(weight.at[rows, columns], out, arrived.at[len(copies)]))
+        copies[-1].start()
     mine, theirs = own[...].astype(F32), other[...].astype(F32)
     turned = jnp.where(c == 0, theirs, mine)
     turned = pltpu.roll(turned, RANK, 1)
@@ -98,6 +106,8 @@
         for y in range(4):
             rows = pl.ds(pl.multiple_of(start + y * 128, 32), 32)
             outs[k][64:96, y * 128 : (y + 1) * 128] = packed[rows, :]
+    for copy in copies:
+        copy.wait()
 
 
 def partial_sums(*rest):
@@ -241,17 +251,16 @@
     down_other = send(down, to_core)
     parts = call(
         prepare,
-        (down, down_other, up),
-        [pltpu.VMEM((96, HALF), BF16)] * 4,
-        [pltpu.VMEM((512, 128), BF16)],
+        (down, down_other, up, weight),
+        [pltpu.VMEM((96, HALF), BF16)] * 4 + [pltpu.VMEM((32, HALF), BF16)] * 2,
+        [pltpu.VMEM((512, 128), BF16), pltpu.SemaphoreType.DMA((2,))],
         free=(0, 2),
+        far=(3,),
     )
+    weight_own, weight_other = parts[4], send(parts[5], to_core)
     parts = [parts[0]] + [send(parts[k], along_zh(k)) for k in (2, 1, 3)]
-
+    gain = after(gain, parts[0])
     row = y * 128 + zh * 32
-    weight_own = lax.dynamic_slice(weight, (row, c * HALF), (32, HALF))
-    weight_other = lax.dynamic_slice(weight, (row, (1 - c) * HALF), (32, HALF))
-    weight_other = send(after(weight_other, parts[1]), to_core)
     tokens_other = send(after(tokens, down_other), to_core)
     start = (x * 2 + zl) * 1024 + row
     gains = [lax.dynamic_slice(gain, (start + who * HALF,), (32,)) for who in (c, 1 - c)]
@@ -260,7 +269,7 @@
     staged = [stage(after(tokens, parts[0]), 0), stage(tokens, 1), stage(tokens_other, 0), stage(tokens_other, 1)]
     every, scales = zip(*staged)
 
-    parts = [after(parts[0], every[0]), *parts[1:]]
+    parts = [after(parts[0], every[0], gains, weight_other), *parts[1:]]
     sums = call(partial_sums, parts, [pltpu.VMEM((64, HALF), F32)] * 4, [pltpu.VMEM((256, HALF), F32)])
     sums = [sums[0]] + [send(sums[k], along_y(k)) for k in (1, 3, 2)]
     sums = [after(sums[0], every[1]), *sums[1:]]
@@ -280,30 +289,30 @@
     left_low0 = after(left_low0, state)
     left_low1 = send(left_low0, beside)
     right_low0 = after(right_low0, left_low0)
-    right_low1 = send(right_low0, beside)
+    far_low0 = send(after(left_low0, right_low0), last(-1))
     here1 = after(here1, right_low0)
     up1 = call(upper, (here1,), slab)
     right_up1 = send(up1, last(1))
     left_up0 = after(left_up0, up1)
     left_up1 = send(after(up1, left_up0), last(-1))
-    state = product(every, (here1,), after(state, left_up0), (1024,))
-    right_up0 = after(right_up0, state)
+    right_up0 = after(right_up0, left_up0)
     far_up0 = send(right_up0, last(1))
     left_low1 = after(left_low1, right_up0)
-    far_low0 = send(after(left_low0, left_low1), last(-1))
-    state = product(every, (left_up0, left_low0), after(state, left_low1), (6144, 6656))
+    far_low1 = send(left_low1, last(-1))
+    far_low0 = after(far_low0, left_low1)
+    right_low1 = send(after(right_low0, far_low0), beside)
+    right_up1 = after(right_up1, far_low0)
+    far_up1 = send(right_up1, last(1))
+    state = product(every, (here1,), after(state, right_up1), (1024,))
+    state = product(every, (left_up0, left_low0), state, (6144, 6656))
     state = product(every, (right_up0, right_low0), state, (2048, 2560))
-    right_up1 = after(right_up1, state)
-    far_up1 = send(right_up1, last(1))
-    left_up1 = after(left_up1, right_up1)
-    far_low1 = send(after(left_low1, left_up1), last(-1))
-    right_low1 = after(right_low1, left_up1)
-    state = product(every, (right_up1, right_low1), after(state, right_low1), (3072, 3584))
+    left_up1 = after(left_up1, state)
     state = product(every, (left_up1, left_low1), state, (7168, 7680))
     far_up0 = after(far_up0, state)
-    far_low0 = after(far_low0, far_up0)
     state = product(every, (far_up0, far_low0), state, (4096, 4608))
-    far_up1 = after(far_up1, state)
+    right_low1 = after(right_low1, state)
+    state = product(every, (right_up1, right_low1), state, (3072, 3584))
+    far_low1 = after(far_low1, state)
     ending, ats = (far_up1, far_low1), (5120, 5632)
     theirs = product(every[2:], ending, state, ats, scales[2:], 2)
     back = send(theirs, to_core)

time: 101 us -> 98.2 us (0.972)
  starting transfers between devices: 48.9 us -> 44.6 us
  waiting for transfers between devices: 20.8 us -> 22.6 us
    ppermute x29, starting transfers between devices: 48.9 us -> 44.6 us  [send(): return lax.ppermute(array, AXES, pairs(move))]
    ppermute x29, waiting for transfers between devices: 20.8 us -> 22.6 us  [send(): return lax.ppermute(array, AXES, pairs(move))]
  transfers between devices with their start and end apart: 29 -> 29, of which waited for: 12 -> 16; matrix products, arithmetic and copies ran while one was open for 2% -> 1% of each run, Pallas kernels for 27% -> 28%
where the time goes in v3:
time: 98.2 us; the launch traced here: 97.8 us
  starting transfers between devices  44.6 us (45%)
  Pallas kernels  29.4 us (30%)
  waiting for transfers between devices  22.6 us (23%)
    ppermute x29, starting transfers between devices, send(): return lax.ppermute(array, AXES, pairs(move))  44.6 us
    ppermute x29, waiting for transfers between devices, send(): return lax.ppermute(array, AXES, pairs(move))  22.6 us
    pallas_call x4, Pallas kernels, stage(): pl.pallas_call(stage_body, grid=(steps,), out_shape=[pltpu.VMEM((SHARE, F...  15.8 us
    pallas_call x16, Pallas kernels, call(): pl.pallas_call(body, out_shape=outs, in_specs=[HBM if i in far else VMEM...  13.6 us
  transfers between devices with their start and end apart: 29, of which 16 were waited for; matrix products, arithmetic and copies ran while one was open for 1% of the time, Pallas kernels for 28%

profile of v3, /device:TPU:1, one launch (start us, length us, event | category | flops | bytes accessed | tf_op | source)
XLA Modules:
  0.0 97.8 jit_solution(9551366364343064099)
XLA Ops:
  0.0 3.2 %collective-permute-start = (bf16[512,128]{1,0:T(8,128)(2,1)}, bf16[512,128]{1,0:T(8,128)(2,1)S(1)}, u32[]{:S(2)}, u32[]{:S(2)}) collective-permute-start(bf16[512,128]{1,0:T(8,128)(2,1)} %bitcast.2), channel_id=1, source_target_pairs={{0,1},{1,0},{2,3},{3,2},{4,5},{5,4},{6,7},{7,6},{8,9},{9,8},{10,11... | collective-permute-start | bytes 393224 | tf_op jit(solution)/shard_map/ppermute | solution.py:33
  4.8 1.8 %shard_map.55 = (bf16[96,512]{1,0:T(8,128)(2,1)S(1)}, bf16[96,512]{1,0:T(8,128)(2,1)S(1)}, bf16[96,512]{1,0:T(8,128)(2,1)S(1)}, bf16[96,512]{1,0:T(8,128)(2,1)S(...) custom-call(bf16[512,128]{1,0:T(8,128)(2,1)} %bitcast.3, bf16[512,128]{1,0:T(8,128)(2,1)S(1)} %collective-permute-done.other, ...), custom_call_target="tpu_custom_call" | custom-call | flops 1024 | bytes 1024 | tf_op jit(solution)/shard_map/pallas_call | solution.py:75
  6.9 5.2 %collective-permute-start.2 = (bf16[96,512]{1,0:T(8,128)(2,1)S(1)}, bf16[96,512]{1,0:T(8,128)(2,1)S(1)}, u32[]{:S(2)}, u32[]{:S(2)}) collective-permute-start(bf16[96,512]{1,0:T(8,128)(2,1)S(1)} %get-tuple-element.57), channel_id=1, source_target_pairs={{0,128},{1,129},{2,130},{3,131},{4,132},{5,133},{6,134},{7,135},{8... | collective-permute-start | bytes 294920 | tf_op jit(solution)/shard_map/ppermute | solution.py:33
  13.2 2.4 %collective-permute-start.4 = (bf16[96,512]{1,0:T(8,128)(2,1)S(1)}, bf16[96,512]{1,0:T(8,128)(2,1)S(1)}, u32[]{:S(2)}, u32[]{:S(2)}) collective-permute-start(bf16[96,512]{1,0:T(8,128)(2,1)S(1)} %get-tuple-element.59), channel_id=1, source_target_pairs={{0,192},{1,193},{2,194},{3,195},{4,196},{5,197},{6,198},{7,199},{8... | collective-permute-start | bytes 294920 | tf_op jit(solution)/shard_map/ppermute | solution.py:33
  16.5 4.0 %shard_map.56 = (bf16[256,8192]{1,0:T(8,128)(2,1)S(1)}, f32[256,128]{1,0:T(8,128)S(1)}) custom-call(bf16[512,8192]{1,0:T(8,128)(2,1)} %tokens.2), custom_call_target="tpu_custom_call" | custom-call | flops 1024 | bytes 1024 | tf_op jit(solution)/shard_map/pallas_call | solution.py:194
  20.6 1.5 %collective-permute-done.4.rest_3_ = bf16[96,512]{1,0:T(8,128)(2,1)S(1)} collective-permute-done((bf16[96,512]{1,0:T(8,128)(2,1)S(1)}, bf16[96,512]{1,0:T(8,128)(2,1)S(1)}, u32[]{:S(2)}, u32[]{:S(2)}) %collective-permute-start.4) | collective-permute-done | bytes 98336 | tf_op jit(solution)/shard_map/ppermute | solution.py:33
  22.5 1.4 %collective-permute-start.5 = (f32[64,512]{1,0:T(8,128)S(1)}, f32[64,512]{1,0:T(8,128)S(1)}, u32[]{:S(2)}, u32[]{:S(2)}) collective-permute-start(f32[64,512]{1,0:T(8,128)S(1)} %get-tuple-element.62), channel_id=1, source_target_pairs={{0,16},{1,17},{2,18},{3,19},{4,20},{5,21},{6,22},{7,23},{8,24},{9,... | collective-permute-start | bytes 393224 | tf_op jit(solution)/shard_map/ppermute | solution.py:33
  23.8 1.5 %collective-permute-start.6 = (f32[64,512]{1,0:T(8,128)S(1)}, f32[64,512]{1,0:T(8,128)S(1)}, u32[]{:S(2)}, u32[]{:S(2)}) collective-permute-start(f32[64,512]{1,0:T(8,128)S(1)} %get-tuple-element.63), channel_id=1, source_target_pairs={{0,48},{1,49},{2,50},{3,51},{4,52},{5,53},{6,54},{7,55},{8,56},{9,... | collective-permute-start | bytes 393224 | tf_op jit(solution)/shard_map/ppermute | solution.py:33
  25.4 1.6 %collective-permute-start.7 = (f32[64,512]{1,0:T(8,128)S(1)}, f32[64,512]{1,0:T(8,128)S(1)}, u32[]{:S(2)}, u32[]{:S(2)}) collective-permute-start(f32[64,512]{1,0:T(8,128)S(1)} %get-tuple-element.64), channel_id=1, source_target_pairs={{0,32},{1,33},{2,34},{3,35},{4,36},{5,37},{6,38},{7,39},{8,40},{9,... | collective-permute-start | bytes 393224 | tf_op jit(solution)/shard_map/ppermute | solution.py:33
  26.9 4.0 %shard_map.57 = (bf16[256,8192]{1,0:T(8,128)(2,1)S(1)}, f32[256,128]{1,0:T(8,128)S(1)}) custom-call(bf16[512,8192]{1,0:T(8,128)(2,1)} %tokens.2), custom_call_target="tpu_custom_call" | custom-call | flops 1024 | bytes 1024 | tf_op jit(solution)/shard_map/pallas_call | solution.py:194
  30.9 1.5 %collective-permute-done.7.d = f32[64,512]{1,0:T(8,128)S(1)} collective-permute-done((f32[64,512]{1,0:T(8,128)S(1)}, f32[64,512]{1,0:T(8,128)S(1)}, u32[]{:S(2)}, u32[]{:S(2)}) %collective-permute-start.7) | collective-permute-done | bytes 131104 | tf_op jit(solution)/shard_map/ppermute | solution.py:33
  32.4 2.5 %collective-permute-start.10 = (bf16[64,512]{1,0:T(8,128)(2,1)S(1)}, bf16[64,512]{1,0:T(8,128)(2,1)S(1)}, u32[]{:S(2)}, u32[]{:S(2)}) collective-permute-start(bf16[64,512]{1,0:T(8,128)(2,1)S(1)} %shard_map.59.refs_0_), channel_id=1, source_target_pairs={{0,128},{1,129},{2,130},{3,131},{4,132},{5,133},{6,134},{7,135},{8... | collective-permute-start | bytes 196616 | tf_op jit(solution)/shard_map/ppermute | solution.py:33
  35.8 2.0 %collective-permute-start.9 = (bf16[64,512]{1,0:T(8,128)(2,1)S(1)}, bf16[64,512]{1,0:T(8,128)(2,1)S(1)}, u32[]{:S(2)}, u32[]{:S(2)}) collective-permute-start(bf16[64,512]{1,0:T(8,128)(2,1)S(1)} %shard_map.59.refs_0_), channel_id=1, source_target_pairs={{0,64},{1,65},{2,66},{3,67},{4,68},{5,69},{6,70},{7,71},{8,72},{9,... | collective-permute-start | bytes 196616 | tf_op jit(solution)/shard_map/ppermute | solution.py:33
  37.8 4.0 %shard_map.60 = (bf16[256,8192]{1,0:T(8,128)(2,1)S(1)}, f32[256,128]{1,0:T(8,128)S(1)}) custom-call(bf16[512,8192]{1,0:T(8,128)(2,1)} %collective-permute-done.8.tokens), custom_call_target="tpu_custom_call" | custom-call | flops 1024 | bytes 1024 | tf_op jit(solution)/shard_map/pallas_call | solution.py:194
  42.9 1.3 %collective-permute-start.12 = (bf16[256,512]{1,0:T(8,128)(2,1)S(1)}, bf16[256,512]{1,0:T(8,128)(2,1)S(1)}, u32[]{:S(2)}, u32[]{:S(2)}) collective-permute-start(bf16[256,512]{1,0:T(8,128)(2,1)S(1)} %shard_map.61.refs_0_), channel_id=1, source_target_pairs={{0,16},{1,5},{2,18},{3,7},{4,20},{5,9},{6,22},{7,11},{8,24},{9,13}... | collective-permute-start | bytes 786440 | tf_op jit(solution)/shard_map/ppermute | solution.py:33
  44.2 2.4 %collective-permute-start.13 = (bf16[256,512]{1,0:T(8,128)(2,1)S(1)}, bf16[256,512]{1,0:T(8,128)(2,1)S(1)}, u32[]{:S(2)}, u32[]{:S(2)}) collective-permute-start(bf16[256,512]{1,0:T(8,128)(2,1)S(1)} %shard_map.61.refs_0_), channel_id=1, source_target_pairs={{0,32},{1,9},{2,34},{3,11},{4,36},{5,13},{6,38},{7,15},{8,40},{9,1... | collective-permute-start | bytes 786440 | tf_op jit(solution)/shard_map/ppermute | solution.py:33
  47.8 4.0 %shard_map.62 = (bf16[256,8192]{1,0:T(8,128)(2,1)S(1)}, f32[256,128]{1,0:T(8,128)S(1)}) custom-call(bf16[512,8192]{1,0:T(8,128)(2,1)} %collective-permute-done.8.tokens), custom_call_target="tpu_custom_call" | custom-call | flops 1024 | bytes 1024 | tf_op jit(solution)/shard_map/pallas_call | solution.py:194
  51.8 1.7 %collective-permute-done.13.refs_2_ = bf16[256,512]{1,0:T(8,128)(2,1)S(1)} collective-permute-done((bf16[256,512]{1,0:T(8,128)(2,1)S(1)}, bf16[256,512]{1,0:T(8,128)(2,1)S(1)}, u32[]{:S(2)}, u32[]{:S(2)}) %collective-permute-start.13) | collective-permute-done | bytes 262176 | tf_op jit(solution)/shard_map/ppermute | solution.py:33
  53.6 1.6 %collective-permute-start.15 = (bf16[1024,512]{1,0:T(8,128)(2,1)S(1)}, bf16[1024,512]{1,0:T(8,128)(2,1)S(1)}, u32[]{:S(2)}, u32[]{:S(2)}) collective-permute-start(bf16[1024,512]{1,0:T(8,128)(2,1)S(1)} %get-tuple-element.70.refs_4_), channel_id=1, source_target_pairs={{0,2},{1,195},{2,0},{3,65},{4,6},{5,199},{6,4},{7,69},{8,10},{9,20... | collective-permute-start | bytes 3145736 | tf_op jit(solution)/shard_map/ppermute | solution.py:33
  55.2 1.4 %collective-permute-start.17 = (bf16[512,512]{1,0:T(8,128)(2,1)S(1)}, bf16[512,512]{1,0:T(8,128)(2,1)S(1)}, u32[]{:S(2)}, u32[]{:S(2)}) collective-permute-start(bf16[512,512]{1,0:T(8,128)(2,1)S(1)} %get-tuple-element.71), channel_id=1, source_target_pairs={{0,12},{1,49},{2,14},{3,51},{4,0},{5,53},{6,2},{7,55},{8,4},{9,57}... | collective-permute-start | bytes 1572872 | tf_op jit(solution)/shard_map/ppermute | solution.py:33
  56.7 2.6 %collective-permute-start.22 = (bf16[512,512]{1,0:T(8,128)(2,1)S(1)}, bf16[512,512]{1,0:T(8,128)(2,1)S(1)}, u32[]{:S(2)}, u32[]{:S(2)}) collective-permute-start(bf16[512,512]{1,0:T(8,128)(2,1)S(1)} %get-tuple-element.76), channel_id=1, source_target_pairs={{0,12},{1,49},{2,14},{3,51},{4,0},{5,53},{6,2},{7,55},{8,4},{9,57}... | collective-permute-start | bytes 1572872 | tf_op jit(solution)/shard_map/ppermute | solution.py:33
  60.6 3.0 %collective-permute-done.17.refs_5_ = bf16[512,512]{1,0:T(8,128)(2,1)S(1)} collective-permute-done((bf16[512,512]{1,0:T(8,128)(2,1)S(1)}, bf16[512,512]{1,0:T(8,128)(2,1)S(1)}, u32[]{:S(2)}, u32[]{:S(2)}) %collective-permute-start.17) | collective-permute-done | bytes 524320 | tf_op jit(solution)/shard_map/ppermute | solution.py:33
  64.7 1.4 %collective-permute-done.16.refs_5_ = bf16[512,512]{1,0:T(8,128)(2,1)S(1)} collective-permute-done((bf16[512,512]{1,0:T(8,128)(2,1)S(1)}, bf16[512,512]{1,0:T(8,128)(2,1)S(1)}, u32[]{:S(2)}, u32[]{:S(2)}) %collective-permute-start.16) | collective-permute-done | bytes 524320 | tf_op jit(solution)/shard_map/ppermute | solution.py:33
  66.7 2.2 %collective-permute-done.15.rows.refs_4_ = bf16[1024,512]{1,0:T(8,128)(2,1)S(1)} collective-permute-done((bf16[1024,512]{1,0:T(8,128)(2,1)S(1)}, bf16[1024,512]{1,0:T(8,128)(2,1)S(1)}, u32[]{:S(2)}, u32[]{:S(2)}) %collective-permute-start.15) | collective-permute-done | bytes 1048608 | tf_op jit(solution)/shard_map/ppermute | solution.py:33
  69.2 2.6 %collective-permute-done.21.refs_4_ = bf16[512,512]{1,0:T(8,128)(2,1)S(1)} collective-permute-done((bf16[512,512]{1,0:T(8,128)(2,1)S(1)}, bf16[512,512]{1,0:T(8,128)(2,1)S(1)}, u32[]{:S(2)}, u32[]{:S(2)}) %collective-permute-start.21) | collective-permute-done | bytes 524320 | tf_op jit(solution)/shard_map/ppermute | solution.py:33
  71.7 1.5 %collective-permute-start.26 = (bf16[512,512]{1,0:T(8,128)(2,1)S(1)}, bf16[512,512]{1,0:T(8,128)(2,1)S(1)}, u32[]{:S(2)}, u32[]{:S(2)}) collective-permute-start(bf16[512,512]{1,0:T(8,128)(2,1)S(1)} %collective-permute-done.21.refs_4_), channel_id=1, source_target_pairs={{0,4},{1,17},{2,6},{3,19},{4,8},{5,21},{6,10},{7,23},{8,12},{9,25}... | collective-permute-start | bytes 1572872 | tf_op jit(solution)/shard_map/ppermute | solution.py:33
  73.2 1.3 %collective-permute-done.20.refs_5_ = bf16[512,512]{1,0:T(8,128)(2,1)S(1)} collective-permute-done((bf16[512,512]{1,0:T(8,128)(2,1)S(1)}, bf16[512,512]{1,0:T(8,128)(2,1)S(1)}, u32[]{:S(2)}, u32[]{:S(2)}) %collective-permute-start.20) | collective-permute-done | bytes 524320 | tf_op jit(solution)/shard_map/ppermute | solution.py:33
  76.0 2.2 %collective-permute-start.24 = (bf16[512,512]{1,0:T(8,128)(2,1)S(1)}, bf16[512,512]{1,0:T(8,128)(2,1)S(1)}, u32[]{:S(2)}, u32[]{:S(2)}) collective-permute-start(bf16[512,512]{1,0:T(8,128)(2,1)S(1)} %collective-permute-done.20.refs_5_), channel_id=1, source_target_pairs={{0,12},{1,49},{2,14},{3,51},{4,0},{5,53},{6,2},{7,55},{8,4},{9,57}... | collective-permute-start | bytes 1572872 | tf_op jit(solution)/shard_map/ppermute | solution.py:33
  79.8 1.2 %shard_map.67.refs_6_ = f32[1024,512]{1,0:T(8,128)S(1)} custom-call(bf16[256,8192]{1,0:T(8,128)(2,1)S(1)} %get-tuple-element.51.refs_0_, bf16[256,8192]{1,0:T(8,128)(2,1)S(1)} %get-tuple-element.52.refs_1_, bf16[256,8192]{1,0:T(8,128)(2,1)S(1)} %get-tuple-element.66.refs_2_.refs_0_, bf16[256,8192]{1,0:T(8,128)(2,1)S(1)} %get-tuple-element.68.refs_3_.refs_1_, ...), custom_call_target="tpu_custom_call" | custom-call | flops 1024 | bytes 1024 | tf_op jit(solution)/shard_map/pallas_call | solution.py:75
  85.4 1.2 %shard_map.71.refs_4_ = f32[1024,512]{1,0:T(8,128)S(1)} custom-call(bf16[256,8192]{1,0:T(8,128)(2,1)S(1)} %get-tuple-element.51.refs_0_, bf16[256,8192]{1,0:T(8,128)(2,1)S(1)} %get-tuple-element.52.refs_1_, bf16[256,8192]{1,0:T(8,128)(2,1)S(1)} %get-tuple-element.66.refs_2_.refs_0_, bf16[256,8192]{1,0:T(8,128)(2,1)S(1)} %get-tuple-element.68.refs_3_.refs_1_, ...), custom_call_target="tpu_custom_call" | custom-call | flops 1024 | bytes 1024 | tf_op jit(solution)/shard_map/pallas_call | solution.py:75
  86.7 3.1 %collective-permute-done.23.refs_2_ = bf16[512,512]{1,0:T(8,128)(2,1)S(1)} collective-permute-done((bf16[512,512]{1,0:T(8,128)(2,1)S(1)}, bf16[512,512]{1,0:T(8,128)(2,1)S(1)}, u32[]{:S(2)}, u32[]{:S(2)}) %collective-permute-start.23) | collective-permute-done | bytes 524320 | tf_op jit(solution)/shard_map/ppermute | solution.py:33
  90.5 4.7 %collective-permute-start.28 = (bf16[512,512]{1,0:T(8,128)(2,1)S(1)}, bf16[512,512]{1,0:T(8,128)(2,1)S(1)}, u32[]{:S(2)}, u32[]{:S(2)}) collective-permute-start(bf16[512,512]{1,0:T(8,128)(2,1)S(1)} %shard_map.73), channel_id=1, source_target_pairs={{0,1},{1,0},{2,3},{3,2},{4,5},{5,4},{6,7},{7,6},{8,9},{9,8},{10,11... | collective-permute-start | bytes 1572872 | tf_op jit(solution)/shard_map/ppermute | solution.py:33
  (49 shorter events, 21.9 us)
Async XLA Ops:
  0.0 4.4 %collective-permute-start = (bf16[512,128]{1,0:T(8,128)(2,1)}, bf16[512,128]{1,0:T(8,128)(2,1)S(1)}, u32[]{:S(2)}, u32[]{:S(2)}) collective-permute-start(bf16[512,128]{1,0:T(8,128)(2,1)} %bitcast.2), channel_id=1, source_target_pairs={{0,1},{1,0},{2,3},{3,2},{4,5},{5,4},{6,7},{7,6},{8,9},{9,8},{10,11... | collective-permute-start | bytes 393224 | tf_op jit(solution)/shard_map/ppermute | solution.py:33
  4.4 33.4 %collective-permute-start.8 = (bf16[512,8192]{1,0:T(8,128)(2,1)}, bf16[512,8192]{1,0:T(8,128)(2,1)}, u32[]{:S(2)}, u32[]{:S(2)}) collective-permute-start(bf16[512,8192]{1,0:T(8,128)(2,1)} %tokens.2), channel_id=1, source_target_pairs={{0,1},{1,0},{2,3},{3,2},{4,5},{5,4},{6,7},{7,6},{8,9},{9,8},{10,11... | collective-permute-start | bytes 25165832 | tf_op jit(solution)/shard_map/ppermute | solution.py:33
  6.6 13.9 %collective-permute-start.1 = (bf16[32,512]{1,0:T(8,128)(2,1)S(1)}, bf16[32,512]{1,0:T(8,128)(2,1)S(1)}, u32[]{:S(2)}, u32[]{:S(2)}) collective-permute-start(bf16[32,512]{1,0:T(8,128)(2,1)S(1)} %get-tuple-element.54), channel_id=1, source_target_pairs={{0,1},{1,0},{2,3},{3,2},{4,5},{5,4},{6,7},{7,6},{8,9},{9,8},{10,11... | collective-permute-start | bytes 98312 | tf_op jit(solution)/shard_map/ppermute | solution.py:33
  6.9 13.7 %collective-permute-start.2 = (bf16[96,512]{1,0:T(8,128)(2,1)S(1)}, bf16[96,512]{1,0:T(8,128)(2,1)S(1)}, u32[]{:S(2)}, u32[]{:S(2)}) collective-permute-start(bf16[96,512]{1,0:T(8,128)(2,1)S(1)} %get-tuple-element.57), channel_id=1, source_target_pairs={{0,128},{1,129},{2,130},{3,131},{4,132},{5,133},{6,134},{7,135},{8... | collective-permute-start | bytes 294920 | tf_op jit(solution)/shard_map/ppermute | solution.py:33
  12.0 8.5 %collective-permute-start.3 = (bf16[96,512]{1,0:T(8,128)(2,1)S(1)}, bf16[96,512]{1,0:T(8,128)(2,1)S(1)}, u32[]{:S(2)}, u32[]{:S(2)}) collective-permute-start(bf16[96,512]{1,0:T(8,128)(2,1)S(1)} %get-tuple-element.58), channel_id=1, source_target_pairs={{0,64},{1,65},{2,66},{3,67},{4,68},{5,69},{6,70},{7,71},{8,72},{9,... | collective-permute-start | bytes 294920 | tf_op jit(solution)/shard_map/ppermute | solution.py:33
  13.2 8.9 %collective-permute-start.4 = (bf16[96,512]{1,0:T(8,128)(2,1)S(1)}, bf16[96,512]{1,0:T(8,128)(2,1)S(1)}, u32[]{:S(2)}, u32[]{:S(2)}) collective-permute-start(bf16[96,512]{1,0:T(8,128)(2,1)S(1)} %get-tuple-element.59), channel_id=1, source_target_pairs={{0,192},{1,193},{2,194},{3,195},{4,196},{5,197},{6,198},{7,199},{8... | collective-permute-start | bytes 294920 | tf_op jit(solution)/shard_map/ppermute | solution.py:33
  22.5 8.4 %collective-permute-start.5 = (f32[64,512]{1,0:T(8,128)S(1)}, f32[64,512]{1,0:T(8,128)S(1)}, u32[]{:S(2)}, u32[]{:S(2)}) collective-permute-start(f32[64,512]{1,0:T(8,128)S(1)} %get-tuple-element.62), channel_id=1, source_target_pairs={{0,16},{1,17},{2,18},{3,19},{4,20},{5,21},{6,22},{7,23},{8,24},{9,... | collective-permute-start | bytes 393224 | tf_op jit(solution)/shard_map/ppermute | solution.py:33
  23.8 7.1 %collective-permute-start.6 = (f32[64,512]{1,0:T(8,128)S(1)}, f32[64,512]{1,0:T(8,128)S(1)}, u32[]{:S(2)}, u32[]{:S(2)}) collective-permute-start(f32[64,512]{1,0:T(8,128)S(1)} %get-tuple-element.63), channel_id=1, source_target_pairs={{0,48},{1,49},{2,50},{3,51},{4,52},{5,53},{6,54},{7,55},{8,56},{9,... | collective-permute-start | bytes 393224 | tf_op jit(solution)/shard_map/ppermute | solution.py:33
  25.4 7.0 %collective-permute-start.7 = (f32[64,512]{1,0:T(8,128)S(1)}, f32[64,512]{1,0:T(8,128)S(1)}, u32[]{:S(2)}, u32[]{:S(2)}) collective-permute-start(f32[64,512]{1,0:T(8,128)S(1)} %get-tuple-element.64), channel_id=1, source_target_pairs={{0,32},{1,33},{2,34},{3,35},{4,36},{5,37},{6,38},{7,39},{8,40},{9,... | collective-permute-start | bytes 393224 | tf_op jit(solution)/shard_map/ppermute | solution.py:33
  32.4 9.4 %collective-permute-start.10 = (bf16[64,512]{1,0:T(8,128)(2,1)S(1)}, bf16[64,512]{1,0:T(8,128)(2,1)S(1)}, u32[]{:S(2)}, u32[]{:S(2)}) collective-permute-start(bf16[64,512]{1,0:T(8,128)(2,1)S(1)} %shard_map.59.refs_0_), channel_id=1, source_target_pairs={{0,128},{1,129},{2,130},{3,131},{4,132},{5,133},{6,134},{7,135},{8... | collective-permute-start | bytes 196616 | tf_op jit(solution)/shard_map/ppermute | solution.py:33
  34.9 8.0 %collective-permute-start.11 = (bf16[64,512]{1,0:T(8,128)(2,1)S(1)}, bf16[64,512]{1,0:T(8,128)(2,1)S(1)}, u32[]{:S(2)}, u32[]{:S(2)}) collective-permute-start(bf16[64,512]{1,0:T(8,128)(2,1)S(1)} %shard_map.59.refs_0_), channel_id=1, source_target_pairs={{0,192},{1,193},{2,194},{3,195},{4,196},{5,197},{6,198},{7,199},{8... | collective-permute-start | bytes 196616 | tf_op jit(solution)/shard_map/ppermute | solution.py:33
  35.8 7.0 %collective-permute-start.9 = (bf16[64,512]{1,0:T(8,128)(2,1)S(1)}, bf16[64,512]{1,0:T(8,128)(2,1)S(1)}, u32[]{:S(2)}, u32[]{:S(2)}) collective-permute-start(bf16[64,512]{1,0:T(8,128)(2,1)S(1)} %shard_map.59.refs_0_), channel_id=1, source_target_pairs={{0,64},{1,65},{2,66},{3,67},{4,68},{5,69},{6,70},{7,71},{8,72},{9,... | collective-permute-start | bytes 196616 | tf_op jit(solution)/shard_map/ppermute | solution.py:33
  42.9 8.9 %collective-permute-start.12 = (bf16[256,512]{1,0:T(8,128)(2,1)S(1)}, bf16[256,512]{1,0:T(8,128)(2,1)S(1)}, u32[]{:S(2)}, u32[]{:S(2)}) collective-permute-start(bf16[256,512]{1,0:T(8,128)(2,1)S(1)} %shard_map.61.refs_0_), channel_id=1, source_target_pairs={{0,16},{1,5},{2,18},{3,7},{4,20},{5,9},{6,22},{7,11},{8,24},{9,13}... | collective-permute-start | bytes 786440 | tf_op jit(solution)/shard_map/ppermute | solution.py:33
  44.2 9.3 %collective-permute-start.13 = (bf16[256,512]{1,0:T(8,128)(2,1)S(1)}, bf16[256,512]{1,0:T(8,128)(2,1)S(1)}, u32[]{:S(2)}, u32[]{:S(2)}) collective-permute-start(bf16[256,512]{1,0:T(8,128)(2,1)S(1)} %shard_map.61.refs_0_), channel_id=1, source_target_pairs={{0,32},{1,9},{2,34},{3,11},{4,36},{5,13},{6,38},{7,15},{8,40},{9,1... | collective-permute-start | bytes 786440 | tf_op jit(solution)/shard_map/ppermute | solution.py:33
  46.6 6.9 %collective-permute-start.14 = (bf16[256,512]{1,0:T(8,128)(2,1)S(1)}, bf16[256,512]{1,0:T(8,128)(2,1)S(1)}, u32[]{:S(2)}, u32[]{:S(2)}) collective-permute-start(bf16[256,512]{1,0:T(8,128)(2,1)S(1)} %shard_map.61.refs_0_), channel_id=1, source_target_pairs={{0,48},{1,13},{2,50},{3,15},{4,52},{5,1},{6,54},{7,3},{8,56},{9,5}... | collective-permute-start | bytes 786440 | tf_op jit(solution)/shard_map/ppermute | solution.py:33
  53.6 15.2 %collective-permute-start.15 = (bf16[1024,512]{1,0:T(8,128)(2,1)S(1)}, bf16[1024,512]{1,0:T(8,128)(2,1)S(1)}, u32[]{:S(2)}, u32[]{:S(2)}) collective-permute-start(bf16[1024,512]{1,0:T(8,128)(2,1)S(1)} %get-tuple-element.70.refs_4_), channel_id=1, source_target_pairs={{0,2},{1,195},{2,0},{3,65},{4,6},{5,199},{6,4},{7,69},{8,10},{9,20... | collective-permute-start | bytes 3145736 | tf_op jit(solution)/shard_map/ppermute | solution.py:33
  55.2 8.3 %collective-permute-start.17 = (bf16[512,512]{1,0:T(8,128)(2,1)S(1)}, bf16[512,512]{1,0:T(8,128)(2,1)S(1)}, u32[]{:S(2)}, u32[]{:S(2)}) collective-permute-start(bf16[512,512]{1,0:T(8,128)(2,1)S(1)} %get-tuple-element.71), channel_id=1, source_target_pairs={{0,12},{1,49},{2,14},{3,51},{4,0},{5,53},{6,2},{7,55},{8,4},{9,57}... | collective-permute-start | bytes 1572872 | tf_op jit(solution)/shard_map/ppermute | solution.py:33
  56.6 9.5 %collective-permute-start.16 = (bf16[512,512]{1,0:T(8,128)(2,1)S(1)}, bf16[512,512]{1,0:T(8,128)(2,1)S(1)}, u32[]{:S(2)}, u32[]{:S(2)}) collective-permute-start(bf16[512,512]{1,0:T(8,128)(2,1)S(1)} %get-tuple-element.71), channel_id=1, source_target_pairs={{0,4},{1,17},{2,6},{3,19},{4,8},{5,21},{6,10},{7,23},{8,12},{9,25}... | collective-permute-start | bytes 1572872 | tf_op jit(solution)/shard_map/ppermute | solution.py:33
  56.7 12.5 %collective-permute-start.22 = (bf16[512,512]{1,0:T(8,128)(2,1)S(1)}, bf16[512,512]{1,0:T(8,128)(2,1)S(1)}, u32[]{:S(2)}, u32[]{:S(2)}) collective-permute-start(bf16[512,512]{1,0:T(8,128)(2,1)S(1)} %get-tuple-element.76), channel_id=1, source_target_pairs={{0,12},{1,49},{2,14},{3,51},{4,0},{5,53},{6,2},{7,55},{8,4},{9,57}... | collective-permute-start | bytes 1572872 | tf_op jit(solution)/shard_map/ppermute | solution.py:33
  60.5 11.2 %collective-permute-start.21 = (bf16[512,512]{1,0:T(8,128)(2,1)S(1)}, bf16[512,512]{1,0:T(8,128)(2,1)S(1)}, u32[]{:S(2)}, u32[]{:S(2)}) collective-permute-start(bf16[512,512]{1,0:T(8,128)(2,1)S(1)} %get-tuple-element.76), channel_id=1, source_target_pairs={{0,4},{1,17},{2,6},{3,19},{4,8},{5,21},{6,10},{7,23},{8,12},{9,25}... | collective-permute-start | bytes 1572872 | tf_op jit(solution)/shard_map/ppermute | solution.py:33
  63.6 10.9 %collective-permute-start.20 = (bf16[512,512]{1,0:T(8,128)(2,1)S(1)}, bf16[512,512]{1,0:T(8,128)(2,1)S(1)}, u32[]{:S(2)}, u32[]{:S(2)}) collective-permute-start(bf16[512,512]{1,0:T(8,128)(2,1)S(1)} %collective-permute-done.17.refs_5_), channel_id=1, source_target_pairs={{0,2},{1,195},{2,0},{3,65},{4,6},{5,199},{6,4},{7,69},{8,10},{9,20... | collective-permute-start | bytes 1572872 | tf_op jit(solution)/shard_map/ppermute | solution.py:33
  66.1 8.7 %collective-permute-start.19 = (bf16[512,512]{1,0:T(8,128)(2,1)S(1)}, bf16[512,512]{1,0:T(8,128)(2,1)S(1)}, u32[]{:S(2)}, u32[]{:S(2)}) collective-permute-start(bf16[512,512]{1,0:T(8,128)(2,1)S(1)} %collective-permute-done.17.refs_5_), channel_id=1, source_target_pairs={{0,12},{1,49},{2,14},{3,51},{4,0},{5,53},{6,2},{7,55},{8,4},{9,57}... | collective-permute-start | bytes 1572872 | tf_op jit(solution)/shard_map/ppermute | solution.py:33
  68.9 9.6 %collective-permute-start.18 = (bf16[512,512]{1,0:T(8,128)(2,1)S(1)}, bf16[512,512]{1,0:T(8,128)(2,1)S(1)}, u32[]{:S(2)}, u32[]{:S(2)}) collective-permute-start(bf16[512,512]{1,0:T(8,128)(2,1)S(1)} %shard_map.65), channel_id=1, source_target_pairs={{0,4},{1,17},{2,6},{3,19},{4,8},{5,21},{6,10},{7,23},{8,12},{9,25}... | collective-permute-start | bytes 1572872 | tf_op jit(solution)/shard_map/ppermute | solution.py:33
  71.7 10.6 %collective-permute-start.27 = (bf16[512,512]{1,0:T(8,128)(2,1)S(1)}, bf16[512,512]{1,0:T(8,128)(2,1)S(1)}, u32[]{:S(2)}, u32[]{:S(2)}) collective-permute-start(bf16[512,512]{1,0:T(8,128)(2,1)S(1)} %shard_map.65), channel_id=1, source_target_pairs={{0,12},{1,49},{2,14},{3,51},{4,0},{5,53},{6,2},{7,55},{8,4},{9,57}... | collective-permute-start | bytes 1572872 | tf_op jit(solution)/shard_map/ppermute | solution.py:33
  71.7 12.4 %collective-permute-start.26 = (bf16[512,512]{1,0:T(8,128)(2,1)S(1)}, bf16[512,512]{1,0:T(8,128)(2,1)S(1)}, u32[]{:S(2)}, u32[]{:S(2)}) collective-permute-start(bf16[512,512]{1,0:T(8,128)(2,1)S(1)} %collective-permute-done.21.refs_4_), channel_id=1, source_target_pairs={{0,4},{1,17},{2,6},{3,19},{4,8},{5,21},{6,10},{7,23},{8,12},{9,25}... | collective-permute-start | bytes 1572872 | tf_op jit(solution)/shard_map/ppermute | solution.py:33
  74.8 10.6 %collective-permute-start.25 = (bf16[512,512]{1,0:T(8,128)(2,1)S(1)}, bf16[512,512]{1,0:T(8,128)(2,1)S(1)}, u32[]{:S(2)}, u32[]{:S(2)}) collective-permute-start(bf16[512,512]{1,0:T(8,128)(2,1)S(1)} %collective-permute-done.16.refs_5_), channel_id=1, source_target_pairs={{0,2},{1,195},{2,0},{3,65},{4,6},{5,199},{6,4},{7,69},{8,10},{9,20... | collective-permute-start | bytes 1572872 | tf_op jit(solution)/shard_map/ppermute | solution.py:33
  76.0 10.7 %collective-permute-start.24 = (bf16[512,512]{1,0:T(8,128)(2,1)S(1)}, bf16[512,512]{1,0:T(8,128)(2,1)S(1)}, u32[]{:S(2)}, u32[]{:S(2)}) collective-permute-start(bf16[512,512]{1,0:T(8,128)(2,1)S(1)} %collective-permute-done.20.refs_5_), channel_id=1, source_target_pairs={{0,12},{1,49},{2,14},{3,51},{4,0},{5,53},{6,2},{7,55},{8,4},{9,57}... | collective-permute-start | bytes 1572872 | tf_op jit(solution)/shard_map/ppermute | solution.py:33
  78.5 11.2 %collective-permute-start.23 = (bf16[512,512]{1,0:T(8,128)(2,1)S(1)}, bf16[512,512]{1,0:T(8,128)(2,1)S(1)}, u32[]{:S(2)}, u32[]{:S(2)}) collective-permute-start(bf16[512,512]{1,0:T(8,128)(2,1)S(1)} %collective-permute-done.18.refs_4_), channel_id=1, source_target_pairs={{0,4},{1,17},{2,6},{3,19},{4,8},{5,21},{6,10},{7,23},{8,12},{9,25}... | collective-permute-start | bytes 1572872 | tf_op jit(solution)/shard_map/ppermute | solution.py:33
  90.5 6.3 %collective-permute-start.28 = (bf16[512,512]{1,0:T(8,128)(2,1)S(1)}, bf16[512,512]{1,0:T(8,128)(2,1)S(1)}, u32[]{:S(2)}, u32[]{:S(2)}) collective-permute-start(bf16[512,512]{1,0:T(8,128)(2,1)S(1)} %shard_map.73), channel_id=1, source_target_pairs={{0,1},{1,0},{2,3},{3,2},{4,5},{5,4},{6,7},{7,6},{8,9},{9,8},{10,11... | collective-permute-start | bytes 1572872 | tf_op jit(solution)/shard_map/ppermute | solution.py:33

commit v4 on v2

--- a/solution.py
+++ b/solution.py
@@ -188,7 +188,7 @@
         in_specs=[pl.BlockSpec((TALL, FEATURES), lambda i: (i + share * steps, 0))],
         out_specs=[VMEM] * 2,
         compiler_params=pltpu.CompilerParams(vmem_limit_bytes=16 << 20),
-        cost_estimate=pl.CostEstimate(flops=1024, bytes_accessed=1024, transcendentals=0),
+        cost_estimate=pl.CostEstimate(flops=1 << 24, bytes_accessed=8 << 20, transcendentals=0),
     )(pltpu.with_memory_space_constraint(tokens, pltpu.HBM))
 
 
@@ -247,7 +247,7 @@
         free=(0, 2),
     )
     parts = [parts[0]] + [send(parts[k], along_zh(k)) for k in (2, 1, 3)]
-
+    gain = after(gain, parts[0])
     row = y * 128 + zh * 32
     weight_own = lax.dynamic_slice(weight, (row, c * HALF), (32, HALF))
     weight_other = lax.dynamic_slice(weight, (row, (1 - c) * HALF), (32, HALF))
@@ -260,7 +260,7 @@
     staged = [stage(after(tokens, parts[0]), 0), stage(tokens, 1), stage(tokens_other, 0), stage(tokens_other, 1)]
     every, scales = zip(*staged)
 
-    parts = [after(parts[0], every[0]), *parts[1:]]
+    parts = [after(parts[0], every[0], gains), *parts[1:]]
     sums = call(partial_sums, parts, [pltpu.VMEM((64, HALF), F32)] * 4, [pltpu.VMEM((256, HALF), F32)])
     sums = [sums[0]] + [send(sums[k], along_y(k)) for k in (1, 3, 2)]
     sums = [after(sums[0], every[1]), *sums[1:]]
@@ -280,30 +280,30 @@
     left_low0 = after(left_low0, state)
     left_low1 = send(left_low0, beside)
     right_low0 = after(right_low0, left_low0)
-    right_low1 = send(right_low0, beside)
+    far_low0 = send(after(left_low0, right_low0), last(-1))
     here1 = after(here1, right_low0)
     up1 = call(upper, (here1,), slab)
     right_up1 = send(up1, last(1))
     left_up0 = after(left_up0, up1)
     left_up1 = send(after(up1, left_up0), last(-1))
-    state = product(every, (here1,), after(state, left_up0), (1024,))
-    right_up0 = after(right_up0, state)
+    right_up0 = after(right_up0, left_up0)
     far_up0 = send(right_up0, last(1))
     left_low1 = after(left_low1, right_up0)
-    far_low0 = send(after(left_low0, left_low1), last(-1))
-    state = product(every, (left_up0, left_low0), after(state, left_low1), (6144, 6656))
+    far_low1 = send(left_low1, last(-1))
+    far_low0 = after(far_low0, left_low1)
+    right_low1 = send(after(right_low0, far_low0), beside)
+    right_up1 = after(right_up1, far_low0)
+    far_up1 = send(right_up1, last(1))
+    state = product(every, (here1,), after(state, right_up1), (1024,))
+    state = product(every, (left_up0, left_low0), state, (6144, 6656))
     state = product(every, (right_up0, right_low0), state, (2048, 2560))
-    right_up1 = after(right_up1, state)
-    far_up1 = send(right_up1, last(1))
-    left_up1 = after(left_up1, right_up1)
-    far_low1 = send(after(left_low1, left_up1), last(-1))
-    right_low1 = after(right_low1, left_up1)
-    state = product(every, (right_up1, right_low1), after(state, right_low1), (3072, 3584))
+    left_up1 = after(left_up1, state)
     state = product(every, (left_up1, left_low1), state, (7168, 7680))
     far_up0 = after(far_up0, state)
-    far_low0 = after(far_low0, far_up0)
     state = product(every, (far_up0, far_low0), state, (4096, 4608))
-    far_up1 = after(far_up1, state)
+    right_low1 = after(right_low1, state)
+    state = product(every, (right_up1, right_low1), state, (3072, 3584))
+    far_low1 = after(far_low1, state)
     ending, ats = (far_up1, far_low1), (5120, 5632)
     theirs = product(every[2:], ending, state, ats, scales[2:], 2)
     back = send(theirs, to_core)

time: 101 us -> 97.6 us (0.966)
  starting transfers between devices: 48.9 us -> 45.2 us
    ppermute x29, starting transfers between devices: 48.9 us -> 45.2 us  [send(): return lax.ppermute(array, AXES, pairs(move))]
  transfers between devices with their start and end apart: 29 -> 29, of which waited for: 12 -> 13; matrix products, arithmetic and copies ran while one was open for 2% -> 2% of each run, Pallas kernels for 27% -> 28%
where the time goes in v4:
time: 97.6 us; the launch traced here: 97.1 us
  starting transfers between devices  45.2 us (46%)
  Pallas kernels  28.7 us (29%)
  waiting for transfers between devices  21.2 us (22%)
  local copies, waits for them, and re-layouts  1.69 us (2%)
    ppermute x29, starting transfers between devices, send(): return lax.ppermute(array, AXES, pairs(move))  45.2 us
    ppermute x29, waiting for transfers between devices, send(): return lax.ppermute(array, AXES, pairs(move))  21.2 us
    pallas_call x4, Pallas kernels, stage(): pl.pallas_call(stage_body, grid=(steps,), out_shape=[pltpu.VMEM((SHARE, F...  15.8 us
    pallas_call x16, Pallas kernels, call(): pl.pallas_call(body, out_shape=outs, in_specs=[VMEM] * len(operands), out...  12.9 us
  transfers between devices with their start and end apart: 29, of which 13 were waited for; matrix products, arithmetic and copies ran while one was open for 2% of the time, Pallas kernels for 28%

profile of v4, /device:TPU:1, one launch (start us, length us, event | category | flops | bytes accessed | tf_op | source)
XLA Modules:
  0.0 97.1 jit_solution(1287104411595281575)
XLA Ops:
  0.0 3.2 %collective-permute-start = (bf16[512,128]{1,0:T(8,128)(2,1)}, bf16[512,128]{1,0:T(8,128)(2,1)S(1)}, u32[]{:S(2)}, u32[]{:S(2)}) collective-permute-start(bf16[512,128]{1,0:T(8,128)(2,1)} %bitcast.2), channel_id=1, source_target_pairs={{0,1},{1,0},{2,3},{3,2},{4,5},{5,4},{6,7},{7,6},{8,9},{9,8},{10,11... | collective-permute-start | bytes 393224 | tf_op jit(solution)/shard_map/ppermute | solution.py:33
  5.9 5.3 %collective-permute-start.1 = (bf16[96,512]{1,0:T(8,128)(2,1)S(1)}, bf16[96,512]{1,0:T(8,128)(2,1)S(1)}, u32[]{:S(2)}, u32[]{:S(2)}) collective-permute-start(bf16[96,512]{1,0:T(8,128)(2,1)S(1)} %get-tuple-element.52), channel_id=1, source_target_pairs={{0,128},{1,129},{2,130},{3,131},{4,132},{5,133},{6,134},{7,135},{8... | collective-permute-start | bytes 294920 | tf_op jit(solution)/shard_map/ppermute | solution.py:33
  12.4 2.4 %collective-permute-start.4 = (bf16[96,512]{1,0:T(8,128)(2,1)S(1)}, bf16[96,512]{1,0:T(8,128)(2,1)S(1)}, u32[]{:S(2)}, u32[]{:S(2)}) collective-permute-start(bf16[96,512]{1,0:T(8,128)(2,1)S(1)} %get-tuple-element.57), channel_id=1, source_target_pairs={{0,192},{1,193},{2,194},{3,195},{4,196},{5,197},{6,198},{7,199},{8... | collective-permute-start | bytes 294920 | tf_op jit(solution)/shard_map/ppermute | solution.py:33
  14.8 4.0 %shard_map.56 = (bf16[256,8192]{1,0:T(8,128)(2,1)S(1)}, f32[256,128]{1,0:T(8,128)S(1)}) custom-call(bf16[512,8192]{1,0:T(8,128)(2,1)} %tokens.2), custom_call_target="tpu_custom_call" | custom-call | flops 16777216 | bytes 8388608 | tf_op jit(solution)/shard_map/pallas_call | solution.py:184
  19.7 1.6 %collective-permute-done.4.rest_3_ = bf16[96,512]{1,0:T(8,128)(2,1)S(1)} collective-permute-done((bf16[96,512]{1,0:T(8,128)(2,1)S(1)}, bf16[96,512]{1,0:T(8,128)(2,1)S(1)}, u32[]{:S(2)}, u32[]{:S(2)}) %collective-permute-start.4) | collective-permute-done | bytes 98336 | tf_op jit(solution)/shard_map/ppermute | solution.py:33
  21.7 1.4 %collective-permute-start.5 = (f32[64,512]{1,0:T(8,128)S(1)}, f32[64,512]{1,0:T(8,128)S(1)}, u32[]{:S(2)}, u32[]{:S(2)}) collective-permute-start(f32[64,512]{1,0:T(8,128)S(1)} %get-tuple-element.60), channel_id=1, source_target_pairs={{0,16},{1,17},{2,18},{3,19},{4,20},{5,21},{6,22},{7,23},{8,24},{9,... | collective-permute-start | bytes 393224 | tf_op jit(solution)/shard_map/ppermute | solution.py:33
  23.0 1.5 %collective-permute-start.6 = (f32[64,512]{1,0:T(8,128)S(1)}, f32[64,512]{1,0:T(8,128)S(1)}, u32[]{:S(2)}, u32[]{:S(2)}) collective-permute-start(f32[64,512]{1,0:T(8,128)S(1)} %get-tuple-element.61), channel_id=1, source_target_pairs={{0,48},{1,49},{2,50},{3,51},{4,52},{5,53},{6,54},{7,55},{8,56},{9,... | collective-permute-start | bytes 393224 | tf_op jit(solution)/shard_map/ppermute | solution.py:33
  24.6 1.6 %collective-permute-start.7 = (f32[64,512]{1,0:T(8,128)S(1)}, f32[64,512]{1,0:T(8,128)S(1)}, u32[]{:S(2)}, u32[]{:S(2)}) collective-permute-start(f32[64,512]{1,0:T(8,128)S(1)} %get-tuple-element.62), channel_id=1, source_target_pairs={{0,32},{1,33},{2,34},{3,35},{4,36},{5,37},{6,38},{7,39},{8,40},{9,... | collective-permute-start | bytes 393224 | tf_op jit(solution)/shard_map/ppermute | solution.py:33
  26.9 1.4 %collective-permute-start.2 = (bf16[32,512]{1,0:T(8,128)(2,1)S(1)}, bf16[32,512]{1,0:T(8,128)(2,1)S(1)}, u32[]{:S(2)}, u32[]{:S(2)}) collective-permute-start(bf16[32,512]{1,0:T(8,128)(2,1)S(1)} %get-tuple-element.53), channel_id=1, source_target_pairs={{0,1},{1,0},{2,3},{3,2},{4,5},{5,4},{6,7},{7,6},{8,9},{9,8},{10,11... | collective-permute-start | bytes 98312 | tf_op jit(solution)/shard_map/ppermute | solution.py:33
  28.3 4.0 %shard_map.57 = (bf16[256,8192]{1,0:T(8,128)(2,1)S(1)}, f32[256,128]{1,0:T(8,128)S(1)}) custom-call(bf16[512,8192]{1,0:T(8,128)(2,1)} %tokens.2), custom_call_target="tpu_custom_call" | custom-call | flops 16777216 | bytes 8388608 | tf_op jit(solution)/shard_map/pallas_call | solution.py:184
  32.3 4.0 %collective-permute-start.10 = (bf16[64,512]{1,0:T(8,128)(2,1)S(1)}, bf16[64,512]{1,0:T(8,128)(2,1)S(1)}, u32[]{:S(2)}, u32[]{:S(2)}) collective-permute-start(bf16[64,512]{1,0:T(8,128)(2,1)S(1)} %shard_map.59.refs_0_), channel_id=1, source_target_pairs={{0,128},{1,129},{2,130},{3,131},{4,132},{5,133},{6,134},{7,135},{8... | collective-permute-start | bytes 196616 | tf_op jit(solution)/shard_map/ppermute | solution.py:33
  36.9 1.8 %collective-permute-start.9 = (bf16[64,512]{1,0:T(8,128)(2,1)S(1)}, bf16[64,512]{1,0:T(8,128)(2,1)S(1)}, u32[]{:S(2)}, u32[]{:S(2)}) collective-permute-start(bf16[64,512]{1,0:T(8,128)(2,1)S(1)} %shard_map.59.refs_0_), channel_id=1, source_target_pairs={{0,64},{1,65},{2,66},{3,67},{4,68},{5,69},{6,70},{7,71},{8,72},{9,... | collective-permute-start | bytes 196616 | tf_op jit(solution)/shard_map/ppermute | solution.py:33
  38.7 4.0 %shard_map.60 = (bf16[256,8192]{1,0:T(8,128)(2,1)S(1)}, f32[256,128]{1,0:T(8,128)S(1)}) custom-call(bf16[512,8192]{1,0:T(8,128)(2,1)} %collective-permute-done.8.tokens), custom_call_target="tpu_custom_call" | custom-call | flops 16777216 | bytes 8388608 | tf_op jit(solution)/shard_map/pallas_call | solution.py:184
  42.7 1.7 %collective-permute-done.11.refs_3_ = bf16[64,512]{1,0:T(8,128)(2,1)S(1)} collective-permute-done((bf16[64,512]{1,0:T(8,128)(2,1)S(1)}, bf16[64,512]{1,0:T(8,128)(2,1)S(1)}, u32[]{:S(2)}, u32[]{:S(2)}) %collective-permute-start.11) | collective-permute-done | bytes 65568 | tf_op jit(solution)/shard_map/ppermute | solution.py:33
  44.4 1.3 %collective-permute-start.12 = (bf16[256,512]{1,0:T(8,128)(2,1)S(1)}, bf16[256,512]{1,0:T(8,128)(2,1)S(1)}, u32[]{:S(2)}, u32[]{:S(2)}) collective-permute-start(bf16[256,512]{1,0:T(8,128)(2,1)S(1)} %shard_map.61.refs_0_), channel_id=1, source_target_pairs={{0,16},{1,5},{2,18},{3,7},{4,20},{5,9},{6,22},{7,11},{8,24},{9,13}... | collective-permute-start | bytes 786440 | tf_op jit(solution)/shard_map/ppermute | solution.py:33
  45.7 2.4 %collective-permute-start.13 = (bf16[256,512]{1,0:T(8,128)(2,1)S(1)}, bf16[256,512]{1,0:T(8,128)(2,1)S(1)}, u32[]{:S(2)}, u32[]{:S(2)}) collective-permute-start(bf16[256,512]{1,0:T(8,128)(2,1)S(1)} %shard_map.61.refs_0_), channel_id=1, source_target_pairs={{0,32},{1,9},{2,34},{3,11},{4,36},{5,13},{6,38},{7,15},{8,40},{9,1... | collective-permute-start | bytes 786440 | tf_op jit(solution)/shard_map/ppermute | solution.py:33
  49.3 4.0 %shard_map.62 = (bf16[256,8192]{1,0:T(8,128)(2,1)S(1)}, f32[256,128]{1,0:T(8,128)S(1)}) custom-call(bf16[512,8192]{1,0:T(8,128)(2,1)} %collective-permute-done.8.tokens), custom_call_target="tpu_custom_call" | custom-call | flops 16777216 | bytes 8388608 | tf_op jit(solution)/shard_map/pallas_call | solution.py:184
  53.3 1.4 %collective-permute-done.13.refs_2_ = bf16[256,512]{1,0:T(8,128)(2,1)S(1)} collective-permute-done((bf16[256,512]{1,0:T(8,128)(2,1)S(1)}, bf16[256,512]{1,0:T(8,128)(2,1)S(1)}, u32[]{:S(2)}, u32[]{:S(2)}) %collective-permute-start.13) | collective-permute-done | bytes 262176 | tf_op jit(solution)/shard_map/ppermute | solution.py:33
  54.9 1.4 %collective-permute-start.15 = (bf16[1024,512]{1,0:T(8,128)(2,1)S(1)}, bf16[1024,512]{1,0:T(8,128)(2,1)S(1)}, u32[]{:S(2)}, u32[]{:S(2)}) collective-permute-start(bf16[1024,512]{1,0:T(8,128)(2,1)S(1)} %get-tuple-element.68.refs_4_), channel_id=1, source_target_pairs={{0,2},{1,195},{2,0},{3,65},{4,6},{5,199},{6,4},{7,69},{8,10},{9,20... | collective-permute-start | bytes 3145736 | tf_op jit(solution)/shard_map/ppermute | solution.py:33
  56.2 1.5 %collective-permute-start.16 = (bf16[512,512]{1,0:T(8,128)(2,1)S(1)}, bf16[512,512]{1,0:T(8,128)(2,1)S(1)}, u32[]{:S(2)}, u32[]{:S(2)}) collective-permute-start(bf16[512,512]{1,0:T(8,128)(2,1)S(1)} %get-tuple-element.69), channel_id=1, source_target_pairs={{0,4},{1,17},{2,6},{3,19},{4,8},{5,21},{6,10},{7,23},{8,12},{9,25}... | collective-permute-start | bytes 1572872 | tf_op jit(solution)/shard_map/ppermute | solution.py:33
  60.5 4.1 %collective-permute-done.17.refs_5_ = bf16[512,512]{1,0:T(8,128)(2,1)S(1)} collective-permute-done((bf16[512,512]{1,0:T(8,128)(2,1)S(1)}, bf16[512,512]{1,0:T(8,128)(2,1)S(1)}, u32[]{:S(2)}, u32[]{:S(2)}) %collective-permute-start.17) | collective-permute-done | bytes 524320 | tf_op jit(solution)/shard_map/ppermute | solution.py:33
  64.5 1.4 %collective-permute-start.20 = (bf16[512,512]{1,0:T(8,128)(2,1)S(1)}, bf16[512,512]{1,0:T(8,128)(2,1)S(1)}, u32[]{:S(2)}, u32[]{:S(2)}) collective-permute-start(bf16[512,512]{1,0:T(8,128)(2,1)S(1)} %collective-permute-done.17.refs_5_), channel_id=1, source_target_pairs={{0,2},{1,195},{2,0},{3,65},{4,6},{5,199},{6,4},{7,69},{8,10},{9,20... | collective-permute-start | bytes 1572872 | tf_op jit(solution)/shard_map/ppermute | solution.py:33
  65.9 1.7 %collective-permute-start.19 = (bf16[512,512]{1,0:T(8,128)(2,1)S(1)}, bf16[512,512]{1,0:T(8,128)(2,1)S(1)}, u32[]{:S(2)}, u32[]{:S(2)}) collective-permute-start(bf16[512,512]{1,0:T(8,128)(2,1)S(1)} %collective-permute-done.17.refs_5_), channel_id=1, source_target_pairs={{0,12},{1,49},{2,14},{3,51},{4,0},{5,53},{6,2},{7,55},{8,4},{9,57}... | collective-permute-start | bytes 1572872 | tf_op jit(solution)/shard_map/ppermute | solution.py:33
  67.6 2.5 %collective-permute-done.15.rows.refs_4_ = bf16[1024,512]{1,0:T(8,128)(2,1)S(1)} collective-permute-done((bf16[1024,512]{1,0:T(8,128)(2,1)S(1)}, bf16[1024,512]{1,0:T(8,128)(2,1)S(1)}, u32[]{:S(2)}, u32[]{:S(2)}) %collective-permute-start.15) | collective-permute-done | bytes 1048608 | tf_op jit(solution)/shard_map/ppermute | solution.py:33
  71.4 1.5 %collective-permute-start.27 = (bf16[512,512]{1,0:T(8,128)(2,1)S(1)}, bf16[512,512]{1,0:T(8,128)(2,1)S(1)}, u32[]{:S(2)}, u32[]{:S(2)}) collective-permute-start(bf16[512,512]{1,0:T(8,128)(2,1)S(1)} %shard_map.65), channel_id=1, source_target_pairs={{0,12},{1,49},{2,14},{3,51},{4,0},{5,53},{6,2},{7,55},{8,4},{9,57}... | collective-permute-start | bytes 1572872 | tf_op jit(solution)/shard_map/ppermute | solution.py:33
  72.9 2.8 %collective-permute-done.20.refs_5_ = bf16[512,512]{1,0:T(8,128)(2,1)S(1)} collective-permute-done((bf16[512,512]{1,0:T(8,128)(2,1)S(1)}, bf16[512,512]{1,0:T(8,128)(2,1)S(1)}, u32[]{:S(2)}, u32[]{:S(2)}) %collective-permute-start.20) | collective-permute-done | bytes 524320 | tf_op jit(solution)/shard_map/ppermute | solution.py:33
  75.8 1.4 %collective-permute-start.25 = (bf16[512,512]{1,0:T(8,128)(2,1)S(1)}, bf16[512,512]{1,0:T(8,128)(2,1)S(1)}, u32[]{:S(2)}, u32[]{:S(2)}) collective-permute-start(bf16[512,512]{1,0:T(8,128)(2,1)S(1)} %collective-permute-done.16.refs_5_), channel_id=1, source_target_pairs={{0,2},{1,195},{2,0},{3,65},{4,6},{5,199},{6,4},{7,69},{8,10},{9,20... | collective-permute-start | bytes 1572872 | tf_op jit(solution)/shard_map/ppermute | solution.py:33
  77.2 2.0 %collective-permute-start.24 = (bf16[512,512]{1,0:T(8,128)(2,1)S(1)}, bf16[512,512]{1,0:T(8,128)(2,1)S(1)}, u32[]{:S(2)}, u32[]{:S(2)}) collective-permute-start(bf16[512,512]{1,0:T(8,128)(2,1)S(1)} %collective-permute-done.20.refs_5_), channel_id=1, source_target_pairs={{0,12},{1,49},{2,14},{3,51},{4,0},{5,53},{6,2},{7,55},{8,4},{9,57}... | collective-permute-start | bytes 1572872 | tf_op jit(solution)/shard_map/ppermute | solution.py:33
  81.0 1.2 %shard_map.67.refs_6_ = f32[1024,512]{1,0:T(8,128)S(1)} custom-call(bf16[256,8192]{1,0:T(8,128)(2,1)S(1)} %get-tuple-element.50.refs_0_, bf16[256,8192]{1,0:T(8,128)(2,1)S(1)} %get-tuple-element.51.refs_1_, bf16[256,8192]{1,0:T(8,128)(2,1)S(1)} %get-tuple-element.64.refs_2_.refs_0_, bf16[256,8192]{1,0:T(8,128)(2,1)S(1)} %get-tuple-element.66.refs_3_.refs_1_, ...), custom_call_target="tpu_custom_call" | custom-call | flops 1024 | bytes 1024 | tf_op jit(solution)/shard_map/pallas_call | solution.py:73
  86.6 1.2 %shard_map.71.refs_4_ = f32[1024,512]{1,0:T(8,128)S(1)} custom-call(bf16[256,8192]{1,0:T(8,128)(2,1)S(1)} %get-tuple-element.50.refs_0_, bf16[256,8192]{1,0:T(8,128)(2,1)S(1)} %get-tuple-element.51.refs_1_, bf16[256,8192]{1,0:T(8,128)(2,1)S(1)} %get-tuple-element.64.refs_2_.refs_0_, bf16[256,8192]{1,0:T(8,128)(2,1)S(1)} %get-tuple-element.66.refs_3_.refs_1_, ...), custom_call_target="tpu_custom_call" | custom-call | flops 1024 | bytes 1024 | tf_op jit(solution)/shard_map/pallas_call | solution.py:73
  87.9 3.1 %collective-permute-done.23.refs_2_ = bf16[512,512]{1,0:T(8,128)(2,1)S(1)} collective-permute-done((bf16[512,512]{1,0:T(8,128)(2,1)S(1)}, bf16[512,512]{1,0:T(8,128)(2,1)S(1)}, u32[]{:S(2)}, u32[]{:S(2)}) %collective-permute-start.23) | collective-permute-done | bytes 524320 | tf_op jit(solution)/shard_map/ppermute | solution.py:33
  91.7 2.9 %collective-permute-start.28 = (bf16[512,512]{1,0:T(8,128)(2,1)S(1)}, bf16[512,512]{1,0:T(8,128)(2,1)S(1)}, u32[]{:S(2)}, u32[]{:S(2)}) collective-permute-start(bf16[512,512]{1,0:T(8,128)(2,1)S(1)} %shard_map.73), channel_id=1, source_target_pairs={{0,1},{1,0},{2,3},{3,2},{4,5},{5,4},{6,7},{7,6},{8,9},{9,8},{10,11... | collective-permute-start | bytes 1572872 | tf_op jit(solution)/shard_map/ppermute | solution.py:33
  (50 shorter events, 21.5 us)
Async XLA Ops:
  0.0 4.4 %collective-permute-start = (bf16[512,128]{1,0:T(8,128)(2,1)}, bf16[512,128]{1,0:T(8,128)(2,1)S(1)}, u32[]{:S(2)}, u32[]{:S(2)}) collective-permute-start(bf16[512,128]{1,0:T(8,128)(2,1)} %bitcast.2), channel_id=1, source_target_pairs={{0,1},{1,0},{2,3},{3,2},{4,5},{5,4},{6,7},{7,6},{8,9},{9,8},{10,11... | collective-permute-start | bytes 393224 | tf_op jit(solution)/shard_map/ppermute | solution.py:33
  4.4 34.3 %collective-permute-start.8 = (bf16[512,8192]{1,0:T(8,128)(2,1)}, bf16[512,8192]{1,0:T(8,128)(2,1)}, u32[]{:S(2)}, u32[]{:S(2)}) collective-permute-start(bf16[512,8192]{1,0:T(8,128)(2,1)} %tokens.2), channel_id=1, source_target_pairs={{0,1},{1,0},{2,3},{3,2},{4,5},{5,4},{6,7},{7,6},{8,9},{9,8},{10,11... | collective-permute-start | bytes 25165832 | tf_op jit(solution)/shard_map/ppermute | solution.py:33
  5.9 13.8 %collective-permute-start.1 = (bf16[96,512]{1,0:T(8,128)(2,1)S(1)}, bf16[96,512]{1,0:T(8,128)(2,1)S(1)}, u32[]{:S(2)}, u32[]{:S(2)}) collective-permute-start(bf16[96,512]{1,0:T(8,128)(2,1)S(1)} %get-tuple-element.52), channel_id=1, source_target_pairs={{0,128},{1,129},{2,130},{3,131},{4,132},{5,133},{6,134},{7,135},{8... | collective-permute-start | bytes 294920 | tf_op jit(solution)/shard_map/ppermute | solution.py:33
  11.2 8.5 %collective-permute-start.3 = (bf16[96,512]{1,0:T(8,128)(2,1)S(1)}, bf16[96,512]{1,0:T(8,128)(2,1)S(1)}, u32[]{:S(2)}, u32[]{:S(2)}) collective-permute-start(bf16[96,512]{1,0:T(8,128)(2,1)S(1)} %get-tuple-element.56), channel_id=1, source_target_pairs={{0,64},{1,65},{2,66},{3,67},{4,68},{5,69},{6,70},{7,71},{8,72},{9,... | collective-permute-start | bytes 294920 | tf_op jit(solution)/shard_map/ppermute | solution.py:33
  12.4 8.9 %collective-permute-start.4 = (bf16[96,512]{1,0:T(8,128)(2,1)S(1)}, bf16[96,512]{1,0:T(8,128)(2,1)S(1)}, u32[]{:S(2)}, u32[]{:S(2)}) collective-permute-start(bf16[96,512]{1,0:T(8,128)(2,1)S(1)} %get-tuple-element.57), channel_id=1, source_target_pairs={{0,192},{1,193},{2,194},{3,195},{4,196},{5,197},{6,198},{7,199},{8... | collective-permute-start | bytes 294920 | tf_op jit(solution)/shard_map/ppermute | solution.py:33
  21.7 10.6 %collective-permute-start.5 = (f32[64,512]{1,0:T(8,128)S(1)}, f32[64,512]{1,0:T(8,128)S(1)}, u32[]{:S(2)}, u32[]{:S(2)}) collective-permute-start(f32[64,512]{1,0:T(8,128)S(1)} %get-tuple-element.60), channel_id=1, source_target_pairs={{0,16},{1,17},{2,18},{3,19},{4,20},{5,21},{6,22},{7,23},{8,24},{9,... | collective-permute-start | bytes 393224 | tf_op jit(solution)/shard_map/ppermute | solution.py:33
  23.0 9.2 %collective-permute-start.6 = (f32[64,512]{1,0:T(8,128)S(1)}, f32[64,512]{1,0:T(8,128)S(1)}, u32[]{:S(2)}, u32[]{:S(2)}) collective-permute-start(f32[64,512]{1,0:T(8,128)S(1)} %get-tuple-element.61), channel_id=1, source_target_pairs={{0,48},{1,49},{2,50},{3,51},{4,52},{5,53},{6,54},{7,55},{8,56},{9,... | collective-permute-start | bytes 393224 | tf_op jit(solution)/shard_map/ppermute | solution.py:33
  24.6 7.7 %collective-permute-start.7 = (f32[64,512]{1,0:T(8,128)S(1)}, f32[64,512]{1,0:T(8,128)S(1)}, u32[]{:S(2)}, u32[]{:S(2)}) collective-permute-start(f32[64,512]{1,0:T(8,128)S(1)} %get-tuple-element.62), channel_id=1, source_target_pairs={{0,32},{1,33},{2,34},{3,35},{4,36},{5,37},{6,38},{7,39},{8,40},{9,... | collective-permute-start | bytes 393224 | tf_op jit(solution)/shard_map/ppermute | solution.py:33
  26.9 5.4 %collective-permute-start.2 = (bf16[32,512]{1,0:T(8,128)(2,1)S(1)}, bf16[32,512]{1,0:T(8,128)(2,1)S(1)}, u32[]{:S(2)}, u32[]{:S(2)}) collective-permute-start(bf16[32,512]{1,0:T(8,128)(2,1)S(1)} %get-tuple-element.53), channel_id=1, source_target_pairs={{0,1},{1,0},{2,3},{3,2},{4,5},{5,4},{6,7},{7,6},{8,9},{9,8},{10,11... | collective-permute-start | bytes 98312 | tf_op jit(solution)/shard_map/ppermute | solution.py:33
  32.3 10.3 %collective-permute-start.10 = (bf16[64,512]{1,0:T(8,128)(2,1)S(1)}, bf16[64,512]{1,0:T(8,128)(2,1)S(1)}, u32[]{:S(2)}, u32[]{:S(2)}) collective-permute-start(bf16[64,512]{1,0:T(8,128)(2,1)S(1)} %shard_map.59.refs_0_), channel_id=1, source_target_pairs={{0,128},{1,129},{2,130},{3,131},{4,132},{5,133},{6,134},{7,135},{8... | collective-permute-start | bytes 196616 | tf_op jit(solution)/shard_map/ppermute | solution.py:33
  36.4 8.0 %collective-permute-start.11 = (bf16[64,512]{1,0:T(8,128)(2,1)S(1)}, bf16[64,512]{1,0:T(8,128)(2,1)S(1)}, u32[]{:S(2)}, u32[]{:S(2)}) collective-permute-start(bf16[64,512]{1,0:T(8,128)(2,1)S(1)} %shard_map.59.refs_0_), channel_id=1, source_target_pairs={{0,192},{1,193},{2,194},{3,195},{4,196},{5,197},{6,198},{7,199},{8... | collective-permute-start | bytes 196616 | tf_op jit(solution)/shard_map/ppermute | solution.py:33
  36.9 7.5 %collective-permute-start.9 = (bf16[64,512]{1,0:T(8,128)(2,1)S(1)}, bf16[64,512]{1,0:T(8,128)(2,1)S(1)}, u32[]{:S(2)}, u32[]{:S(2)}) collective-permute-start(bf16[64,512]{1,0:T(8,128)(2,1)S(1)} %shard_map.59.refs_0_), channel_id=1, source_target_pairs={{0,64},{1,65},{2,66},{3,67},{4,68},{5,69},{6,70},{7,71},{8,72},{9,... | collective-permute-start | bytes 196616 | tf_op jit(solution)/shard_map/ppermute | solution.py:33
  44.4 8.9 %collective-permute-start.12 = (bf16[256,512]{1,0:T(8,128)(2,1)S(1)}, bf16[256,512]{1,0:T(8,128)(2,1)S(1)}, u32[]{:S(2)}, u32[]{:S(2)}) collective-permute-start(bf16[256,512]{1,0:T(8,128)(2,1)S(1)} %shard_map.61.refs_0_), channel_id=1, source_target_pairs={{0,16},{1,5},{2,18},{3,7},{4,20},{5,9},{6,22},{7,11},{8,24},{9,13}... | collective-permute-start | bytes 786440 | tf_op jit(solution)/shard_map/ppermute | solution.py:33
  45.7 9.0 %collective-permute-start.13 = (bf16[256,512]{1,0:T(8,128)(2,1)S(1)}, bf16[256,512]{1,0:T(8,128)(2,1)S(1)}, u32[]{:S(2)}, u32[]{:S(2)}) collective-permute-start(bf16[256,512]{1,0:T(8,128)(2,1)S(1)} %shard_map.61.refs_0_), channel_id=1, source_target_pairs={{0,32},{1,9},{2,34},{3,11},{4,36},{5,13},{6,38},{7,15},{8,40},{9,1... | collective-permute-start | bytes 786440 | tf_op jit(solution)/shard_map/ppermute | solution.py:33
  48.1 6.6 %collective-permute-start.14 = (bf16[256,512]{1,0:T(8,128)(2,1)S(1)}, bf16[256,512]{1,0:T(8,128)(2,1)S(1)}, u32[]{:S(2)}, u32[]{:S(2)}) collective-permute-start(bf16[256,512]{1,0:T(8,128)(2,1)S(1)} %shard_map.61.refs_0_), channel_id=1, source_target_pairs={{0,48},{1,13},{2,50},{3,15},{4,52},{5,1},{6,54},{7,3},{8,56},{9,5}... | collective-permute-start | bytes 786440 | tf_op jit(solution)/shard_map/ppermute | solution.py:33
  54.9 15.2 %collective-permute-start.15 = (bf16[1024,512]{1,0:T(8,128)(2,1)S(1)}, bf16[1024,512]{1,0:T(8,128)(2,1)S(1)}, u32[]{:S(2)}, u32[]{:S(2)}) collective-permute-start(bf16[1024,512]{1,0:T(8,128)(2,1)S(1)} %get-tuple-element.68.refs_4_), channel_id=1, source_target_pairs={{0,2},{1,195},{2,0},{3,65},{4,6},{5,199},{6,4},{7,69},{8,10},{9,20... | collective-permute-start | bytes 3145736 | tf_op jit(solution)/shard_map/ppermute | solution.py:33
  56.2 8.3 %collective-permute-start.17 = (bf16[512,512]{1,0:T(8,128)(2,1)S(1)}, bf16[512,512]{1,0:T(8,128)(2,1)S(1)}, u32[]{:S(2)}, u32[]{:S(2)}) collective-permute-start(bf16[512,512]{1,0:T(8,128)(2,1)S(1)} %get-tuple-element.69), channel_id=1, source_target_pairs={{0,12},{1,49},{2,14},{3,51},{4,0},{5,53},{6,2},{7,55},{8,4},{9,57}... | collective-permute-start | bytes 1572872 | tf_op jit(solution)/shard_map/ppermute | solution.py:33
  56.2 9.7 %collective-permute-start.16 = (bf16[512,512]{1,0:T(8,128)(2,1)S(1)}, bf16[512,512]{1,0:T(8,128)(2,1)S(1)}, u32[]{:S(2)}, u32[]{:S(2)}) collective-permute-start(bf16[512,512]{1,0:T(8,128)(2,1)S(1)} %get-tuple-element.69), channel_id=1, source_target_pairs={{0,4},{1,17},{2,6},{3,19},{4,8},{5,21},{6,10},{7,23},{8,12},{9,25}... | collective-permute-start | bytes 1572872 | tf_op jit(solution)/shard_map/ppermute | solution.py:33
  57.7 12.9 %collective-permute-start.22 = (bf16[512,512]{1,0:T(8,128)(2,1)S(1)}, bf16[512,512]{1,0:T(8,128)(2,1)S(1)}, u32[]{:S(2)}, u32[]{:S(2)}) collective-permute-start(bf16[512,512]{1,0:T(8,128)(2,1)S(1)} %get-tuple-element.74), channel_id=1, source_target_pairs={{0,12},{1,49},{2,14},{3,51},{4,0},{5,53},{6,2},{7,55},{8,4},{9,57}... | collective-permute-start | bytes 1572872 | tf_op jit(solution)/shard_map/ppermute | solution.py:33
  60.1 11.2 %collective-permute-start.21 = (bf16[512,512]{1,0:T(8,128)(2,1)S(1)}, bf16[512,512]{1,0:T(8,128)(2,1)S(1)}, u32[]{:S(2)}, u32[]{:S(2)}) collective-permute-start(bf16[512,512]{1,0:T(8,128)(2,1)S(1)} %get-tuple-element.74), channel_id=1, source_target_pairs={{0,4},{1,17},{2,6},{3,19},{4,8},{5,21},{6,10},{7,23},{8,12},{9,25}... | collective-permute-start | bytes 1572872 | tf_op jit(solution)/shard_map/ppermute | solution.py:33
  64.5 11.2 %collective-permute-start.20 = (bf16[512,512]{1,0:T(8,128)(2,1)S(1)}, bf16[512,512]{1,0:T(8,128)(2,1)S(1)}, u32[]{:S(2)}, u32[]{:S(2)}) collective-permute-start(bf16[512,512]{1,0:T(8,128)(2,1)S(1)} %collective-permute-done.17.refs_5_), channel_id=1, source_target_pairs={{0,2},{1,195},{2,0},{3,65},{4,6},{5,199},{6,4},{7,69},{8,10},{9,20... | collective-permute-start | bytes 1572872 | tf_op jit(solution)/shard_map/ppermute | solution.py:33
  65.9 9.8 %collective-permute-start.19 = (bf16[512,512]{1,0:T(8,128)(2,1)S(1)}, bf16[512,512]{1,0:T(8,128)(2,1)S(1)}, u32[]{:S(2)}, u32[]{:S(2)}) collective-permute-start(bf16[512,512]{1,0:T(8,128)(2,1)S(1)} %collective-permute-done.17.refs_5_), channel_id=1, source_target_pairs={{0,12},{1,49},{2,14},{3,51},{4,0},{5,53},{6,2},{7,55},{8,4},{9,57}... | collective-permute-start | bytes 1572872 | tf_op jit(solution)/shard_map/ppermute | solution.py:33
  70.1 9.6 %collective-permute-start.18 = (bf16[512,512]{1,0:T(8,128)(2,1)S(1)}, bf16[512,512]{1,0:T(8,128)(2,1)S(1)}, u32[]{:S(2)}, u32[]{:S(2)}) collective-permute-start(bf16[512,512]{1,0:T(8,128)(2,1)S(1)} %shard_map.65), channel_id=1, source_target_pairs={{0,4},{1,17},{2,6},{3,19},{4,8},{5,21},{6,10},{7,23},{8,12},{9,25}... | collective-permute-start | bytes 1572872 | tf_op jit(solution)/shard_map/ppermute | solution.py:33
  71.4 12.1 %collective-permute-start.27 = (bf16[512,512]{1,0:T(8,128)(2,1)S(1)}, bf16[512,512]{1,0:T(8,128)(2,1)S(1)}, u32[]{:S(2)}, u32[]{:S(2)}) collective-permute-start(bf16[512,512]{1,0:T(8,128)(2,1)S(1)} %shard_map.65), channel_id=1, source_target_pairs={{0,12},{1,49},{2,14},{3,51},{4,0},{5,53},{6,2},{7,55},{8,4},{9,57}... | collective-permute-start | bytes 1572872 | tf_op jit(solution)/shard_map/ppermute | solution.py:33
  72.9 12.5 %collective-permute-start.26 = (bf16[512,512]{1,0:T(8,128)(2,1)S(1)}, bf16[512,512]{1,0:T(8,128)(2,1)S(1)}, u32[]{:S(2)}, u32[]{:S(2)}) collective-permute-start(bf16[512,512]{1,0:T(8,128)(2,1)S(1)} %collective-permute-done.21.refs_4_), channel_id=1, source_target_pairs={{0,4},{1,17},{2,6},{3,19},{4,8},{5,21},{6,10},{7,23},{8,12},{9,25}... | collective-permute-start | bytes 1572872 | tf_op jit(solution)/shard_map/ppermute | solution.py:33
  75.8 10.8 %collective-permute-start.25 = (bf16[512,512]{1,0:T(8,128)(2,1)S(1)}, bf16[512,512]{1,0:T(8,128)(2,1)S(1)}, u32[]{:S(2)}, u32[]{:S(2)}) collective-permute-start(bf16[512,512]{1,0:T(8,128)(2,1)S(1)} %collective-permute-done.16.refs_5_), channel_id=1, source_target_pairs={{0,2},{1,195},{2,0},{3,65},{4,6},{5,199},{6,4},{7,69},{8,10},{9,20... | collective-permute-start | bytes 1572872 | tf_op jit(solution)/shard_map/ppermute | solution.py:33
  77.2 10.7 %collective-permute-start.24 = (bf16[512,512]{1,0:T(8,128)(2,1)S(1)}, bf16[512,512]{1,0:T(8,128)(2,1)S(1)}, u32[]{:S(2)}, u32[]{:S(2)}) collective-permute-start(bf16[512,512]{1,0:T(8,128)(2,1)S(1)} %collective-permute-done.20.refs_5_), channel_id=1, source_target_pairs={{0,12},{1,49},{2,14},{3,51},{4,0},{5,53},{6,2},{7,55},{8,4},{9,57}... | collective-permute-start | bytes 1572872 | tf_op jit(solution)/shard_map/ppermute | solution.py:33
  79.7 11.2 %collective-permute-start.23 = (bf16[512,512]{1,0:T(8,128)(2,1)S(1)}, bf16[512,512]{1,0:T(8,128)(2,1)S(1)}, u32[]{:S(2)}, u32[]{:S(2)}) collective-permute-start(bf16[512,512]{1,0:T(8,128)(2,1)S(1)} %collective-permute-done.18.refs_4_), channel_id=1, source_target_pairs={{0,4},{1,17},{2,6},{3,19},{4,8},{5,21},{6,10},{7,23},{8,12},{9,25}... | collective-permute-start | bytes 1572872 | tf_op jit(solution)/shard_map/ppermute | solution.py:33
  91.7 4.4 %collective-permute-start.28 = (bf16[512,512]{1,0:T(8,128)(2,1)S(1)}, bf16[512,512]{1,0:T(8,128)(2,1)S(1)}, u32[]{:S(2)}, u32[]{:S(2)}) collective-permute-start(bf16[512,512]{1,0:T(8,128)(2,1)S(1)} %shard_map.73), channel_id=1, source_target_pairs={{0,1},{1,0},{2,3},{3,2},{4,5},{5,4},{6,7},{7,6},{8,9},{9,8},{10,11... | collective-permute-start | bytes 1572872 | tf_op jit(solution)/shard_map/ppermute | solution.py:33

commit v5 on v4

--- a/solution.py
+++ b/solution.py
@@ -304,7 +304,9 @@
     right_low1 = after(right_low1, state)
     state = product(every, (right_up1, right_low1), state, (3072, 3584))
     far_low1 = after(far_low1, state)
-    ending, ats = (far_up1, far_low1), (5120, 5632)
+    state = product(every, (far_low1,), state, (5632,))
+    far_up1 = after(far_up1, state)
+    ending, ats = (far_up1,), (5120,)
     theirs = product(every[2:], ending, state, ats, scales[2:], 2)
     back = send(theirs, to_core)
     mine = product(every[:2], ending, state, ats, scales[:2], 1)

time: 97.6 us -> 97.3 us (level)
    pallas_call x16 -> x17, Pallas kernels: 12.9 us -> 13.1 us  [call(): pl.pallas_call(body, out_shape=outs, in_specs=[VMEM] * len(operands), out...]
where the time goes in v5:
time: 97.3 us; the launch traced here: 96.9 us
  starting transfers between devices  45.2 us (46%)
  Pallas kernels  28.9 us (30%)
  waiting for transfers between devices  20.8 us (21%)
  local copies, waits for them, and re-layouts  1.69 us (2%)
    ppermute x29, starting transfers between devices, send(): return lax.ppermute(array, AXES, pairs(move))  45.2 us
    ppermute x29, waiting for transfers between devices, send(): return lax.ppermute(array, AXES, pairs(move))  20.8 us
    pallas_call x4, Pallas kernels, stage(): pl.pallas_call(stage_body, grid=(steps,), out_shape=[pltpu.VMEM((SHARE, F...  15.8 us
    pallas_call x17, Pallas kernels, call(): pl.pallas_call(body, out_shape=outs, in_specs=[VMEM] * len(operands), out...  13.1 us
  transfers between devices with their start and end apart: 29, of which 13 were waited for; matrix products, arithmetic and copies ran while one was open for 2% of the time, Pallas kernels for 28%

profile of v5, /device:TPU:1, one launch (start us, length us, event | category | flops | bytes accessed | tf_op | source)
XLA Modules:
  0.0 96.9 jit_solution(3661443613640637603)
XLA Ops:
  0.0 3.2 %collective-permute-start = (bf16[512,128]{1,0:T(8,128)(2,1)}, bf16[512,128]{1,0:T(8,128)(2,1)S(1)}, u32[]{:S(2)}, u32[]{:S(2)}) collective-permute-start(bf16[512,128]{1,0:T(8,128)(2,1)} %bitcast.2), channel_id=1, source_target_pairs={{0,1},{1,0},{2,3},{3,2},{4,5},{5,4},{6,7},{7,6},{8,9},{9,8},{10,11... | collective-permute-start | bytes 393224 | tf_op jit(solution)/shard_map/ppermute | solution.py:33
  5.9 5.3 %collective-permute-start.1 = (bf16[96,512]{1,0:T(8,128)(2,1)S(1)}, bf16[96,512]{1,0:T(8,128)(2,1)S(1)}, u32[]{:S(2)}, u32[]{:S(2)}) collective-permute-start(bf16[96,512]{1,0:T(8,128)(2,1)S(1)} %get-tuple-element.53), channel_id=1, source_target_pairs={{0,128},{1,129},{2,130},{3,131},{4,132},{5,133},{6,134},{7,135},{8... | collective-permute-start | bytes 294920 | tf_op jit(solution)/shard_map/ppermute | solution.py:33
  12.4 2.4 %collective-permute-start.4 = (bf16[96,512]{1,0:T(8,128)(2,1)S(1)}, bf16[96,512]{1,0:T(8,128)(2,1)S(1)}, u32[]{:S(2)}, u32[]{:S(2)}) collective-permute-start(bf16[96,512]{1,0:T(8,128)(2,1)S(1)} %get-tuple-element.58), channel_id=1, source_target_pairs={{0,192},{1,193},{2,194},{3,195},{4,196},{5,197},{6,198},{7,199},{8... | collective-permute-start | bytes 294920 | tf_op jit(solution)/shard_map/ppermute | solution.py:33
  14.8 4.0 %shard_map.56 = (bf16[256,8192]{1,0:T(8,128)(2,1)S(1)}, f32[256,128]{1,0:T(8,128)S(1)}) custom-call(bf16[512,8192]{1,0:T(8,128)(2,1)} %tokens.2), custom_call_target="tpu_custom_call" | custom-call | flops 16777216 | bytes 8388608 | tf_op jit(solution)/shard_map/pallas_call | solution.py:184
  19.7 1.6 %collective-permute-done.4.rest_3_ = bf16[96,512]{1,0:T(8,128)(2,1)S(1)} collective-permute-done((bf16[96,512]{1,0:T(8,128)(2,1)S(1)}, bf16[96,512]{1,0:T(8,128)(2,1)S(1)}, u32[]{:S(2)}, u32[]{:S(2)}) %collective-permute-start.4) | collective-permute-done | bytes 98336 | tf_op jit(solution)/shard_map/ppermute | solution.py:33
  21.7 1.4 %collective-permute-start.5 = (f32[64,512]{1,0:T(8,128)S(1)}, f32[64,512]{1,0:T(8,128)S(1)}, u32[]{:S(2)}, u32[]{:S(2)}) collective-permute-start(f32[64,512]{1,0:T(8,128)S(1)} %get-tuple-element.61), channel_id=1, source_target_pairs={{0,16},{1,17},{2,18},{3,19},{4,20},{5,21},{6,22},{7,23},{8,24},{9,... | collective-permute-start | bytes 393224 | tf_op jit(solution)/shard_map/ppermute | solution.py:33
  23.0 1.5 %collective-permute-start.6 = (f32[64,512]{1,0:T(8,128)S(1)}, f32[64,512]{1,0:T(8,128)S(1)}, u32[]{:S(2)}, u32[]{:S(2)}) collective-permute-start(f32[64,512]{1,0:T(8,128)S(1)} %get-tuple-element.62), channel_id=1, source_target_pairs={{0,48},{1,49},{2,50},{3,51},{4,52},{5,53},{6,54},{7,55},{8,56},{9,... | collective-permute-start | bytes 393224 | tf_op jit(solution)/shard_map/ppermute | solution.py:33
  24.6 1.6 %collective-permute-start.7 = (f32[64,512]{1,0:T(8,128)S(1)}, f32[64,512]{1,0:T(8,128)S(1)}, u32[]{:S(2)}, u32[]{:S(2)}) collective-permute-start(f32[64,512]{1,0:T(8,128)S(1)} %get-tuple-element.63), channel_id=1, source_target_pairs={{0,32},{1,33},{2,34},{3,35},{4,36},{5,37},{6,38},{7,39},{8,40},{9,... | collective-permute-start | bytes 393224 | tf_op jit(solution)/shard_map/ppermute | solution.py:33
  26.9 1.4 %collective-permute-start.2 = (bf16[32,512]{1,0:T(8,128)(2,1)S(1)}, bf16[32,512]{1,0:T(8,128)(2,1)S(1)}, u32[]{:S(2)}, u32[]{:S(2)}) collective-permute-start(bf16[32,512]{1,0:T(8,128)(2,1)S(1)} %get-tuple-element.54), channel_id=1, source_target_pairs={{0,1},{1,0},{2,3},{3,2},{4,5},{5,4},{6,7},{7,6},{8,9},{9,8},{10,11... | collective-permute-start | bytes 98312 | tf_op jit(solution)/shard_map/ppermute | solution.py:33
  28.3 4.0 %shard_map.57 = (bf16[256,8192]{1,0:T(8,128)(2,1)S(1)}, f32[256,128]{1,0:T(8,128)S(1)}) custom-call(bf16[512,8192]{1,0:T(8,128)(2,1)} %tokens.2), custom_call_target="tpu_custom_call" | custom-call | flops 16777216 | bytes 8388608 | tf_op jit(solution)/shard_map/pallas_call | solution.py:184
  32.3 4.0 %collective-permute-start.10 = (bf16[64,512]{1,0:T(8,128)(2,1)S(1)}, bf16[64,512]{1,0:T(8,128)(2,1)S(1)}, u32[]{:S(2)}, u32[]{:S(2)}) collective-permute-start(bf16[64,512]{1,0:T(8,128)(2,1)S(1)} %shard_map.59.refs_0_), channel_id=1, source_target_pairs={{0,128},{1,129},{2,130},{3,131},{4,132},{5,133},{6,134},{7,135},{8... | collective-permute-start | bytes 196616 | tf_op jit(solution)/shard_map/ppermute | solution.py:33
  36.9 1.8 %collective-permute-start.9 = (bf16[64,512]{1,0:T(8,128)(2,1)S(1)}, bf16[64,512]{1,0:T(8,128)(2,1)S(1)}, u32[]{:S(2)}, u32[]{:S(2)}) collective-permute-start(bf16[64,512]{1,0:T(8,128)(2,1)S(1)} %shard_map.59.refs_0_), channel_id=1, source_target_pairs={{0,64},{1,65},{2,66},{3,67},{4,68},{5,69},{6,70},{7,71},{8,72},{9,... | collective-permute-start | bytes 196616 | tf_op jit(solution)/shard_map/ppermute | solution.py:33
  38.7 4.0 %shard_map.60 = (bf16[256,8192]{1,0:T(8,128)(2,1)S(1)}, f32[256,128]{1,0:T(8,128)S(1)}) custom-call(bf16[512,8192]{1,0:T(8,128)(2,1)} %collective-permute-done.8.tokens), custom_call_target="tpu_custom_call" | custom-call | flops 16777216 | bytes 8388608 | tf_op jit(solution)/shard_map/pallas_call | solution.py:184
  42.7 1.7 %collective-permute-done.11.refs_3_ = bf16[64,512]{1,0:T(8,128)(2,1)S(1)} collective-permute-done((bf16[64,512]{1,0:T(8,128)(2,1)S(1)}, bf16[64,512]{1,0:T(8,128)(2,1)S(1)}, u32[]{:S(2)}, u32[]{:S(2)}) %collective-permute-start.11) | collective-permute-done | bytes 65568 | tf_op jit(solution)/shard_map/ppermute | solution.py:33
  44.4 1.3 %collective-permute-start.12 = (bf16[256,512]{1,0:T(8,128)(2,1)S(1)}, bf16[256,512]{1,0:T(8,128)(2,1)S(1)}, u32[]{:S(2)}, u32[]{:S(2)}) collective-permute-start(bf16[256,512]{1,0:T(8,128)(2,1)S(1)} %shard_map.61.refs_0_), channel_id=1, source_target_pairs={{0,16},{1,5},{2,18},{3,7},{4,20},{5,9},{6,22},{7,11},{8,24},{9,13}... | collective-permute-start | bytes 786440 | tf_op jit(solution)/shard_map/ppermute | solution.py:33
  45.7 2.4 %collective-permute-start.13 = (bf16[256,512]{1,0:T(8,128)(2,1)S(1)}, bf16[256,512]{1,0:T(8,128)(2,1)S(1)}, u32[]{:S(2)}, u32[]{:S(2)}) collective-permute-start(bf16[256,512]{1,0:T(8,128)(2,1)S(1)} %shard_map.61.refs_0_), channel_id=1, source_target_pairs={{0,32},{1,9},{2,34},{3,11},{4,36},{5,13},{6,38},{7,15},{8,40},{9,1... | collective-permute-start | bytes 786440 | tf_op jit(solution)/shard_map/ppermute | solution.py:33
  49.3 4.0 %shard_map.62 = (bf16[256,8192]{1,0:T(8,128)(2,1)S(1)}, f32[256,128]{1,0:T(8,128)S(1)}) custom-call(bf16[512,8192]{1,0:T(8,128)(2,1)} %collective-permute-done.8.tokens), custom_call_target="tpu_custom_call" | custom-call | flops 16777216 | bytes 8388608 | tf_op jit(solution)/shard_map/pallas_call | solution.py:184
  53.3 1.4 %collective-permute-done.13.refs_2_ = bf16[256,512]{1,0:T(8,128)(2,1)S(1)} collective-permute-done((bf16[256,512]{1,0:T(8,128)(2,1)S(1)}, bf16[256,512]{1,0:T(8,128)(2,1)S(1)}, u32[]{:S(2)}, u32[]{:S(2)}) %collective-permute-start.13) | collective-permute-done | bytes 262176 | tf_op jit(solution)/shard_map/ppermute | solution.py:33
  54.9 1.4 %collective-permute-start.15 = (bf16[1024,512]{1,0:T(8,128)(2,1)S(1)}, bf16[1024,512]{1,0:T(8,128)(2,1)S(1)}, u32[]{:S(2)}, u32[]{:S(2)}) collective-permute-start(bf16[1024,512]{1,0:T(8,128)(2,1)S(1)} %get-tuple-element.69.refs_4_), channel_id=1, source_target_pairs={{0,2},{1,195},{2,0},{3,65},{4,6},{5,199},{6,4},{7,69},{8,10},{9,20... | collective-permute-start | bytes 3145736 | tf_op jit(solution)/shard_map/ppermute | solution.py:33
  56.2 1.5 %collective-permute-start.16 = (bf16[512,512]{1,0:T(8,128)(2,1)S(1)}, bf16[512,512]{1,0:T(8,128)(2,1)S(1)}, u32[]{:S(2)}, u32[]{:S(2)}) collective-permute-start(bf16[512,512]{1,0:T(8,128)(2,1)S(1)} %get-tuple-element.70), channel_id=1, source_target_pairs={{0,4},{1,17},{2,6},{3,19},{4,8},{5,21},{6,10},{7,23},{8,12},{9,25}... | collective-permute-start | bytes 1572872 | tf_op jit(solution)/shard_map/ppermute | solution.py:33
  60.5 4.1 %collective-permute-done.17.refs_5_ = bf16[512,512]{1,0:T(8,128)(2,1)S(1)} collective-permute-done((bf16[512,512]{1,0:T(8,128)(2,1)S(1)}, bf16[512,512]{1,0:T(8,128)(2,1)S(1)}, u32[]{:S(2)}, u32[]{:S(2)}) %collective-permute-start.17) | collective-permute-done | bytes 524320 | tf_op jit(solution)/shard_map/ppermute | solution.py:33
  64.5 1.4 %collective-permute-start.20 = (bf16[512,512]{1,0:T(8,128)(2,1)S(1)}, bf16[512,512]{1,0:T(8,128)(2,1)S(1)}, u32[]{:S(2)}, u32[]{:S(2)}) collective-permute-start(bf16[512,512]{1,0:T(8,128)(2,1)S(1)} %collective-permute-done.17.refs_5_), channel_id=1, source_target_pairs={{0,2},{1,195},{2,0},{3,65},{4,6},{5,199},{6,4},{7,69},{8,10},{9,20... | collective-permute-start | bytes 1572872 | tf_op jit(solution)/shard_map/ppermute | solution.py:33
  65.9 1.7 %collective-permute-start.19 = (bf16[512,512]{1,0:T(8,128)(2,1)S(1)}, bf16[512,512]{1,0:T(8,128)(2,1)S(1)}, u32[]{:S(2)}, u32[]{:S(2)}) collective-permute-start(bf16[512,512]{1,0:T(8,128)(2,1)S(1)} %collective-permute-done.17.refs_5_), channel_id=1, source_target_pairs={{0,12},{1,49},{2,14},{3,51},{4,0},{5,53},{6,2},{7,55},{8,4},{9,57}... | collective-permute-start | bytes 1572872 | tf_op jit(solution)/shard_map/ppermute | solution.py:33
  67.6 2.5 %collective-permute-done.15.rows.refs_4_ = bf16[1024,512]{1,0:T(8,128)(2,1)S(1)} collective-permute-done((bf16[1024,512]{1,0:T(8,128)(2,1)S(1)}, bf16[1024,512]{1,0:T(8,128)(2,1)S(1)}, u32[]{:S(2)}, u32[]{:S(2)}) %collective-permute-start.15) | collective-permute-done | bytes 1048608 | tf_op jit(solution)/shard_map/ppermute | solution.py:33
  71.4 1.5 %collective-permute-start.27 = (bf16[512,512]{1,0:T(8,128)(2,1)S(1)}, bf16[512,512]{1,0:T(8,128)(2,1)S(1)}, u32[]{:S(2)}, u32[]{:S(2)}) collective-permute-start(bf16[512,512]{1,0:T(8,128)(2,1)S(1)} %shard_map.65), channel_id=1, source_target_pairs={{0,12},{1,49},{2,14},{3,51},{4,0},{5,53},{6,2},{7,55},{8,4},{9,57}... | collective-permute-start | bytes 1572872 | tf_op jit(solution)/shard_map/ppermute | solution.py:33
  72.9 2.8 %collective-permute-done.20.refs_5_ = bf16[512,512]{1,0:T(8,128)(2,1)S(1)} collective-permute-done((bf16[512,512]{1,0:T(8,128)(2,1)S(1)}, bf16[512,512]{1,0:T(8,128)(2,1)S(1)}, u32[]{:S(2)}, u32[]{:S(2)}) %collective-permute-start.20) | collective-permute-done | bytes 524320 | tf_op jit(solution)/shard_map/ppermute | solution.py:33
  75.8 1.4 %collective-permute-start.25 = (bf16[512,512]{1,0:T(8,128)(2,1)S(1)}, bf16[512,512]{1,0:T(8,128)(2,1)S(1)}, u32[]{:S(2)}, u32[]{:S(2)}) collective-permute-start(bf16[512,512]{1,0:T(8,128)(2,1)S(1)} %collective-permute-done.16.refs_5_), channel_id=1, source_target_pairs={{0,2},{1,195},{2,0},{3,65},{4,6},{5,199},{6,4},{7,69},{8,10},{9,20... | collective-permute-start | bytes 1572872 | tf_op jit(solution)/shard_map/ppermute | solution.py:33
  77.2 2.0 %collective-permute-start.24 = (bf16[512,512]{1,0:T(8,128)(2,1)S(1)}, bf16[512,512]{1,0:T(8,128)(2,1)S(1)}, u32[]{:S(2)}, u32[]{:S(2)}) collective-permute-start(bf16[512,512]{1,0:T(8,128)(2,1)S(1)} %collective-permute-done.20.refs_5_), channel_id=1, source_target_pairs={{0,12},{1,49},{2,14},{3,51},{4,0},{5,53},{6,2},{7,55},{8,4},{9,57}... | collective-permute-start | bytes 1572872 | tf_op jit(solution)/shard_map/ppermute | solution.py:33
  81.0 1.2 %shard_map.67.refs_6_ = f32[1024,512]{1,0:T(8,128)S(1)} custom-call(bf16[256,8192]{1,0:T(8,128)(2,1)S(1)} %get-tuple-element.51.refs_0_, bf16[256,8192]{1,0:T(8,128)(2,1)S(1)} %get-tuple-element.52.refs_1_, bf16[256,8192]{1,0:T(8,128)(2,1)S(1)} %get-tuple-element.65.refs_2_.refs_0_, bf16[256,8192]{1,0:T(8,128)(2,1)S(1)} %get-tuple-element.67.refs_3_.refs_1_, ...), custom_call_target="tpu_custom_call" | custom-call | flops 1024 | bytes 1024 | tf_op jit(solution)/shard_map/pallas_call | solution.py:73
  86.6 1.2 %shard_map.71.refs_5_ = f32[1024,512]{1,0:T(8,128)S(1)} custom-call(bf16[256,8192]{1,0:T(8,128)(2,1)S(1)} %get-tuple-element.51.refs_0_, bf16[256,8192]{1,0:T(8,128)(2,1)S(1)} %get-tuple-element.52.refs_1_, bf16[256,8192]{1,0:T(8,128)(2,1)S(1)} %get-tuple-element.65.refs_2_.refs_0_, bf16[256,8192]{1,0:T(8,128)(2,1)S(1)} %get-tuple-element.67.refs_3_.refs_1_, ...), custom_call_target="tpu_custom_call" | custom-call | flops 1024 | bytes 1024 | tf_op jit(solution)/shard_map/pallas_call | solution.py:73
  88.6 2.4 %collective-permute-done.23.refs_2_ = bf16[512,512]{1,0:T(8,128)(2,1)S(1)} collective-permute-done((bf16[512,512]{1,0:T(8,128)(2,1)S(1)}, bf16[512,512]{1,0:T(8,128)(2,1)S(1)}, u32[]{:S(2)}, u32[]{:S(2)}) %collective-permute-start.23) | collective-permute-done | bytes 524320 | tf_op jit(solution)/shard_map/ppermute | solution.py:33
  91.4 2.9 %collective-permute-start.28 = (bf16[512,512]{1,0:T(8,128)(2,1)S(1)}, bf16[512,512]{1,0:T(8,128)(2,1)S(1)}, u32[]{:S(2)}, u32[]{:S(2)}) collective-permute-start(bf16[512,512]{1,0:T(8,128)(2,1)S(1)} %shard_map.74), channel_id=1, source_target_pairs={{0,1},{1,0},{2,3},{3,2},{4,5},{5,4},{6,7},{7,6},{8,9},{9,8},{10,11... | collective-permute-start | bytes 1572872 | tf_op jit(solution)/shard_map/ppermute | solution.py:33
  (51 shorter events, 22.0 us)
Async XLA Ops:
  0.0 4.4 %collective-permute-start = (bf16[512,128]{1,0:T(8,128)(2,1)}, bf16[512,128]{1,0:T(8,128)(2,1)S(1)}, u32[]{:S(2)}, u32[]{:S(2)}) collective-permute-start(bf16[512,128]{1,0:T(8,128)(2,1)} %bitcast.2), channel_id=1, source_target_pairs={{0,1},{1,0},{2,3},{3,2},{4,5},{5,4},{6,7},{7,6},{8,9},{9,8},{10,11... | collective-permute-start | bytes 393224 | tf_op jit(solution)/shard_map/ppermute | solution.py:33
  4.4 34.3 %collective-permute-start.8 = (bf16[512,8192]{1,0:T(8,128)(2,1)}, bf16[512,8192]{1,0:T(8,128)(2,1)}, u32[]{:S(2)}, u32[]{:S(2)}) collective-permute-start(bf16[512,8192]{1,0:T(8,128)(2,1)} %tokens.2), channel_id=1, source_target_pairs={{0,1},{1,0},{2,3},{3,2},{4,5},{5,4},{6,7},{7,6},{8,9},{9,8},{10,11... | collective-permute-start | bytes 25165832 | tf_op jit(solution)/shard_map/ppermute | solution.py:33
  5.9 13.8 %collective-permute-start.1 = (bf16[96,512]{1,0:T(8,128)(2,1)S(1)}, bf16[96,512]{1,0:T(8,128)(2,1)S(1)}, u32[]{:S(2)}, u32[]{:S(2)}) collective-permute-start(bf16[96,512]{1,0:T(8,128)(2,1)S(1)} %get-tuple-element.53), channel_id=1, source_target_pairs={{0,128},{1,129},{2,130},{3,131},{4,132},{5,133},{6,134},{7,135},{8... | collective-permute-start | bytes 294920 | tf_op jit(solution)/shard_map/ppermute | solution.py:33
  11.2 8.5 %collective-permute-start.3 = (bf16[96,512]{1,0:T(8,128)(2,1)S(1)}, bf16[96,512]{1,0:T(8,128)(2,1)S(1)}, u32[]{:S(2)}, u32[]{:S(2)}) collective-permute-start(bf16[96,512]{1,0:T(8,128)(2,1)S(1)} %get-tuple-element.57), channel_id=1, source_target_pairs={{0,64},{1,65},{2,66},{3,67},{4,68},{5,69},{6,70},{7,71},{8,72},{9,... | collective-permute-start | bytes 294920 | tf_op jit(solution)/shard_map/ppermute | solution.py:33
  12.4 8.9 %collective-permute-start.4 = (bf16[96,512]{1,0:T(8,128)(2,1)S(1)}, bf16[96,512]{1,0:T(8,128)(2,1)S(1)}, u32[]{:S(2)}, u32[]{:S(2)}) collective-permute-start(bf16[96,512]{1,0:T(8,128)(2,1)S(1)} %get-tuple-element.58), channel_id=1, source_target_pairs={{0,192},{1,193},{2,194},{3,195},{4,196},{5,197},{6,198},{7,199},{8... | collective-permute-start | bytes 294920 | tf_op jit(solution)/shard_map/ppermute | solution.py:33
  21.7 10.6 %collective-permute-start.5 = (f32[64,512]{1,0:T(8,128)S(1)}, f32[64,512]{1,0:T(8,128)S(1)}, u32[]{:S(2)}, u32[]{:S(2)}) collective-permute-start(f32[64,512]{1,0:T(8,128)S(1)} %get-tuple-element.61), channel_id=1, source_target_pairs={{0,16},{1,17},{2,18},{3,19},{4,20},{5,21},{6,22},{7,23},{8,24},{9,... | collective-permute-start | bytes 393224 | tf_op jit(solution)/shard_map/ppermute | solution.py:33
  23.0 9.2 %collective-permute-start.6 = (f32[64,512]{1,0:T(8,128)S(1)}, f32[64,512]{1,0:T(8,128)S(1)}, u32[]{:S(2)}, u32[]{:S(2)}) collective-permute-start(f32[64,512]{1,0:T(8,128)S(1)} %get-tuple-element.62), channel_id=1, source_target_pairs={{0,48},{1,49},{2,50},{3,51},{4,52},{5,53},{6,54},{7,55},{8,56},{9,... | collective-permute-start | bytes 393224 | tf_op jit(solution)/shard_map/ppermute | solution.py:33
  24.6 7.7 %collective-permute-start.7 = (f32[64,512]{1,0:T(8,128)S(1)}, f32[64,512]{1,0:T(8,128)S(1)}, u32[]{:S(2)}, u32[]{:S(2)}) collective-permute-start(f32[64,512]{1,0:T(8,128)S(1)} %get-tuple-element.63), channel_id=1, source_target_pairs={{0,32},{1,33},{2,34},{3,35},{4,36},{5,37},{6,38},{7,39},{8,40},{9,... | collective-permute-start | bytes 393224 | tf_op jit(solution)/shard_map/ppermute | solution.py:33
  26.9 5.4 %collective-permute-start.2 = (bf16[32,512]{1,0:T(8,128)(2,1)S(1)}, bf16[32,512]{1,0:T(8,128)(2,1)S(1)}, u32[]{:S(2)}, u32[]{:S(2)}) collective-permute-start(bf16[32,512]{1,0:T(8,128)(2,1)S(1)} %get-tuple-element.54), channel_id=1, source_target_pairs={{0,1},{1,0},{2,3},{3,2},{4,5},{5,4},{6,7},{7,6},{8,9},{9,8},{10,11... | collective-permute-start | bytes 98312 | tf_op jit(solution)/shard_map/ppermute | solution.py:33
  32.3 10.3 %collective-permute-start.10 = (bf16[64,512]{1,0:T(8,128)(2,1)S(1)}, bf16[64,512]{1,0:T(8,128)(2,1)S(1)}, u32[]{:S(2)}, u32[]{:S(2)}) collective-permute-start(bf16[64,512]{1,0:T(8,128)(2,1)S(1)} %shard_map.59.refs_0_), channel_id=1, source_target_pairs={{0,128},{1,129},{2,130},{3,131},{4,132},{5,133},{6,134},{7,135},{8... | collective-permute-start | bytes 196616 | tf_op jit(solution)/shard_map/ppermute | solution.py:33
  36.4 8.0 %collective-permute-start.11 = (bf16[64,512]{1,0:T(8,128)(2,1)S(1)}, bf16[64,512]{1,0:T(8,128)(2,1)S(1)}, u32[]{:S(2)}, u32[]{:S(2)}) collective-permute-start(bf16[64,512]{1,0:T(8,128)(2,1)S(1)} %shard_map.59.refs_0_), channel_id=1, source_target_pairs={{0,192},{1,193},{2,194},{3,195},{4,196},{5,197},{6,198},{7,199},{8... | collective-permute-start | bytes 196616 | tf_op jit(solution)/shard_map/ppermute | solution.py:33
  36.9 7.5 %collective-permute-start.9 = (bf16[64,512]{1,0:T(8,128)(2,1)S(1)}, bf16[64,512]{1,0:T(8,128)(2,1)S(1)}, u32[]{:S(2)}, u32[]{:S(2)}) collective-permute-start(bf16[64,512]{1,0:T(8,128)(2,1)S(1)} %shard_map.59.refs_0_), channel_id=1, source_target_pairs={{0,64},{1,65},{2,66},{3,67},{4,68},{5,69},{6,70},{7,71},{8,72},{9,... | collective-permute-start | bytes 196616 | tf_op jit(solution)/shard_map/ppermute | solution.py:33
  44.4 8.9 %collective-permute-start.12 = (bf16[256,512]{1,0:T(8,128)(2,1)S(1)}, bf16[256,512]{1,0:T(8,128)(2,1)S(1)}, u32[]{:S(2)}, u32[]{:S(2)}) collective-permute-start(bf16[256,512]{1,0:T(8,128)(2,1)S(1)} %shard_map.61.refs_0_), channel_id=1, source_target_pairs={{0,16},{1,5},{2,18},{3,7},{4,20},{5,9},{6,22},{7,11},{8,24},{9,13}... | collective-permute-start | bytes 786440 | tf_op jit(solution)/shard_map/ppermute | solution.py:33
  45.7 9.0 %collective-permute-start.13 = (bf16[256,512]{1,0:T(8,128)(2,1)S(1)}, bf16[256,512]{1,0:T(8,128)(2,1)S(1)}, u32[]{:S(2)}, u32[]{:S(2)}) collective-permute-start(bf16[256,512]{1,0:T(8,128)(2,1)S(1)} %shard_map.61.refs_0_), channel_id=1, source_target_pairs={{0,32},{1,9},{2,34},{3,11},{4,36},{5,13},{6,38},{7,15},{8,40},{9,1... | collective-permute-start | bytes 786440 | tf_op jit(solution)/shard_map/ppermute | solution.py:33
  48.1 6.6 %collective-permute-start.14 = (bf16[256,512]{1,0:T(8,128)(2,1)S(1)}, bf16[256,512]{1,0:T(8,128)(2,1)S(1)}, u32[]{:S(2)}, u32[]{:S(2)}) collective-permute-start(bf16[256,512]{1,0:T(8,128)(2,1)S(1)} %shard_map.61.refs_0_), channel_id=1, source_target_pairs={{0,48},{1,13},{2,50},{3,15},{4,52},{5,1},{6,54},{7,3},{8,56},{9,5}... | collective-permute-start | bytes 786440 | tf_op jit(solution)/shard_map/ppermute | solution.py:33
  54.9 15.2 %collective-permute-start.15 = (bf16[1024,512]{1,0:T(8,128)(2,1)S(1)}, bf16[1024,512]{1,0:T(8,128)(2,1)S(1)}, u32[]{:S(2)}, u32[]{:S(2)}) collective-permute-start(bf16[1024,512]{1,0:T(8,128)(2,1)S(1)} %get-tuple-element.69.refs_4_), channel_id=1, source_target_pairs={{0,2},{1,195},{2,0},{3,65},{4,6},{5,199},{6,4},{7,69},{8,10},{9,20... | collective-permute-start | bytes 3145736 | tf_op jit(solution)/shard_map/ppermute | solution.py:33
  56.2 8.3 %collective-permute-start.17 = (bf16[512,512]{1,0:T(8,128)(2,1)S(1)}, bf16[512,512]{1,0:T(8,128)(2,1)S(1)}, u32[]{:S(2)}, u32[]{:S(2)}) collective-permute-start(bf16[512,512]{1,0:T(8,128)(2,1)S(1)} %get-tuple-element.70), channel_id=1, source_target_pairs={{0,12},{1,49},{2,14},{3,51},{4,0},{5,53},{6,2},{7,55},{8,4},{9,57}... | collective-permute-start | bytes 1572872 | tf_op jit(solution)/shard_map/ppermute | solution.py:33
  56.2 9.7 %collective-permute-start.16 = (bf16[512,512]{1,0:T(8,128)(2,1)S(1)}, bf16[512,512]{1,0:T(8,128)(2,1)S(1)}, u32[]{:S(2)}, u32[]{:S(2)}) collective-permute-start(bf16[512,512]{1,0:T(8,128)(2,1)S(1)} %get-tuple-element.70), channel_id=1, source_target_pairs={{0,4},{1,17},{2,6},{3,19},{4,8},{5,21},{6,10},{7,23},{8,12},{9,25}... | collective-permute-start | bytes 1572872 | tf_op jit(solution)/shard_map/ppermute | solution.py:33
  57.7 12.9 %collective-permute-start.22 = (bf16[512,512]{1,0:T(8,128)(2,1)S(1)}, bf16[512,512]{1,0:T(8,128)(2,1)S(1)}, u32[]{:S(2)}, u32[]{:S(2)}) collective-permute-start(bf16[512,512]{1,0:T(8,128)(2,1)S(1)} %get-tuple-element.75), channel_id=1, source_target_pairs={{0,12},{1,49},{2,14},{3,51},{4,0},{5,53},{6,2},{7,55},{8,4},{9,57}... | collective-permute-start | bytes 1572872 | tf_op jit(solution)/shard_map/ppermute | solution.py:33
  60.1 11.2 %collective-permute-start.21 = (bf16[512,512]{1,0:T(8,128)(2,1)S(1)}, bf16[512,512]{1,0:T(8,128)(2,1)S(1)}, u32[]{:S(2)}, u32[]{:S(2)}) collective-permute-start(bf16[512,512]{1,0:T(8,128)(2,1)S(1)} %get-tuple-element.75), channel_id=1, source_target_pairs={{0,4},{1,17},{2,6},{3,19},{4,8},{5,21},{6,10},{7,23},{8,12},{9,25}... | collective-permute-start | bytes 1572872 | tf_op jit(solution)/shard_map/ppermute | solution.py:33
  64.5 11.2 %collective-permute-start.20 = (bf16[512,512]{1,0:T(8,128)(2,1)S(1)}, bf16[512,512]{1,0:T(8,128)(2,1)S(1)}, u32[]{:S(2)}, u32[]{:S(2)}) collective-permute-start(bf16[512,512]{1,0:T(8,128)(2,1)S(1)} %collective-permute-done.17.refs_5_), channel_id=1, source_target_pairs={{0,2},{1,195},{2,0},{3,65},{4,6},{5,199},{6,4},{7,69},{8,10},{9,20... | collective-permute-start | bytes 1572872 | tf_op jit(solution)/shard_map/ppermute | solution.py:33
  65.9 9.8 %collective-permute-start.19 = (bf16[512,512]{1,0:T(8,128)(2,1)S(1)}, bf16[512,512]{1,0:T(8,128)(2,1)S(1)}, u32[]{:S(2)}, u32[]{:S(2)}) collective-permute-start(bf16[512,512]{1,0:T(8,128)(2,1)S(1)} %collective-permute-done.17.refs_5_), channel_id=1, source_target_pairs={{0,12},{1,49},{2,14},{3,51},{4,0},{5,53},{6,2},{7,55},{8,4},{9,57}... | collective-permute-start | bytes 1572872 | tf_op jit(solution)/shard_map/ppermute | solution.py:33
  70.1 9.6 %collective-permute-start.18 = (bf16[512,512]{1,0:T(8,128)(2,1)S(1)}, bf16[512,512]{1,0:T(8,128)(2,1)S(1)}, u32[]{:S(2)}, u32[]{:S(2)}) collective-permute-start(bf16[512,512]{1,0:T(8,128)(2,1)S(1)} %shard_map.65), channel_id=1, source_target_pairs={{0,4},{1,17},{2,6},{3,19},{4,8},{5,21},{6,10},{7,23},{8,12},{9,25}... | collective-permute-start | bytes 1572872 | tf_op jit(solution)/shard_map/ppermute | solution.py:33
  71.4 12.1 %collective-permute-start.27 = (bf16[512,512]{1,0:T(8,128)(2,1)S(1)}, bf16[512,512]{1,0:T(8,128)(2,1)S(1)}, u32[]{:S(2)}, u32[]{:S(2)}) collective-permute-start(bf16[512,512]{1,0:T(8,128)(2,1)S(1)} %shard_map.65), channel_id=1, source_target_pairs={{0,12},{1,49},{2,14},{3,51},{4,0},{5,53},{6,2},{7,55},{8,4},{9,57}... | collective-permute-start | bytes 1572872 | tf_op jit(solution)/shard_map/ppermute | solution.py:33
  72.9 12.5 %collective-permute-start.26 = (bf16[512,512]{1,0:T(8,128)(2,1)S(1)}, bf16[512,512]{1,0:T(8,128)(2,1)S(1)}, u32[]{:S(2)}, u32[]{:S(2)}) collective-permute-start(bf16[512,512]{1,0:T(8,128)(2,1)S(1)} %collective-permute-done.21.refs_4_), channel_id=1, source_target_pairs={{0,4},{1,17},{2,6},{3,19},{4,8},{5,21},{6,10},{7,23},{8,12},{9,25}... | collective-permute-start | bytes 1572872 | tf_op jit(solution)/shard_map/ppermute | solution.py:33
  75.8 10.8 %collective-permute-start.25 = (bf16[512,512]{1,0:T(8,128)(2,1)S(1)}, bf16[512,512]{1,0:T(8,128)(2,1)S(1)}, u32[]{:S(2)}, u32[]{:S(2)}) collective-permute-start(bf16[512,512]{1,0:T(8,128)(2,1)S(1)} %collective-permute-done.16.refs_5_), channel_id=1, source_target_pairs={{0,2},{1,195},{2,0},{3,65},{4,6},{5,199},{6,4},{7,69},{8,10},{9,20... | collective-permute-start | bytes 1572872 | tf_op jit(solution)/shard_map/ppermute | solution.py:33
  77.2 10.7 %collective-permute-start.24 = (bf16[512,512]{1,0:T(8,128)(2,1)S(1)}, bf16[512,512]{1,0:T(8,128)(2,1)S(1)}, u32[]{:S(2)}, u32[]{:S(2)}) collective-permute-start(bf16[512,512]{1,0:T(8,128)(2,1)S(1)} %collective-permute-done.20.refs_5_), channel_id=1, source_target_pairs={{0,12},{1,49},{2,14},{3,51},{4,0},{5,53},{6,2},{7,55},{8,4},{9,57}... | collective-permute-start | bytes 1572872 | tf_op jit(solution)/shard_map/ppermute | solution.py:33
  79.7 11.2 %collective-permute-start.23 = (bf16[512,512]{1,0:T(8,128)(2,1)S(1)}, bf16[512,512]{1,0:T(8,128)(2,1)S(1)}, u32[]{:S(2)}, u32[]{:S(2)}) collective-permute-start(bf16[512,512]{1,0:T(8,128)(2,1)S(1)} %collective-permute-done.18.refs_4_), channel_id=1, source_target_pairs={{0,4},{1,17},{2,6},{3,19},{4,8},{5,21},{6,10},{7,23},{8,12},{9,25}... | collective-permute-start | bytes 1572872 | tf_op jit(solution)/shard_map/ppermute | solution.py:33
  91.4 4.4 %collective-permute-start.28 = (bf16[512,512]{1,0:T(8,128)(2,1)S(1)}, bf16[512,512]{1,0:T(8,128)(2,1)S(1)}, u32[]{:S(2)}, u32[]{:S(2)}) collective-permute-start(bf16[512,512]{1,0:T(8,128)(2,1)S(1)} %shard_map.74), channel_id=1, source_target_pairs={{0,1},{1,0},{2,3},{3,2},{4,5},{5,4},{6,7},{7,6},{8,9},{9,8},{10,11... | collective-permute-start | bytes 1572872 | tf_op jit(solution)/shard_map/ppermute | solution.py:33
